TPU v7x, 32 devices: a whole 2x2x4 slice. The times are simulated.
32 devices in a mesh: scenario: 2 (over y), site: 4 (over z), structur: 2 (over x), sub: 2 (over core).
Axes of the slice: x: 2, y: 2, z: 4, core: 2. Of those that a mesh axis runs over, the one named last changes fastest.
Arguments:
- tiles: bfloat16 [8, 8, 8, 256, 256], P(('site', 'structur'), None, 'sub'), may hold values from -0.046875 to 0.046875
- history: bfloat16 [16, 9, 256, 128], P(('scenario', 'site', 'structur')), parts along dimension 0, may hold values from -6 to 6
- self_inverse: bfloat16 [8, 256, 256], P(('site', 'structur')), may hold values from -0.375 to 0.375
- pair_src: int32 [8, 8], P(('site', 'structur')), may hold values from 0 to 7, as said below
- pair_delay: int32 [8, 8], P(('site', 'structur')), may hold values from 1 to 2
- strike_seg: int32 [256], P('scenario'), parts along dimension 0, may hold values from 0 to 2047
- waveform: float32 [4, 128], P('scenario'), parts along dimension 0, may hold values from -24 to 24
Outputs:
- currents: bfloat16 [16, 2, 256, 128], P(('scenario', 'site', 'structur')), parts along dimension 0
There are 2 independent parts, one for each index of `scenario`. A program takes and returns all parts, laid end to end along the dimension named above; an argument that names none is the same for every part. Nothing has to cross between parts.
Inputs may be any that keep to these rules, and one draw needn't show every extreme that they name: The source block's site, pair_src // 2, differs from the observer block's site, b // 2, by at most one.
All inputs are finite; a program needn't handle non-finite values.
Results may differ from a plain program's by a relative error of at most 0.0051.
Values may be sent and summed in bfloat16 or wider, within the bound.
No kernel may reach another device: no remote copies, remote signals or barrier semaphores. Data moves between devices by JAX's collectives and lax.ppermute only.
A program may use at most 128 MiB of HBM per device.

v0:
```python
import jax
import jax.numpy as jnp
from jax import lax
from jax.sharding import PartitionSpec as P


def with_halo(block, sides, width):
    for axis, dim in sides:
        count = lax.axis_size(axis)
        forward = [(i, i + 1) for i in range(count - 1)]
        backward = [(target, source) for source, target in forward]
        low = lax.ppermute(
            lax.slice_in_dim(block, block.shape[dim] - width, None, axis=dim), axis, forward
        )
        high = lax.ppermute(lax.slice_in_dim(block, 0, width, axis=dim), axis, backward)
        block = jnp.concatenate([low, block, high], axis=dim)
    return block


def place_sources(pair_src, blk):
    groups = lax.axis_size("structur")
    here = lax.axis_index("site")
    target = pair_src // (blk * groups)
    member = pair_src // blk % groups
    within = pair_src % blk
    return (target - here + 1) * groups * blk + member * blk + within


def spread_history(history):
    grouped = lax.all_gather(history, "structur", axis=0, tiled=True)
    return with_halo(grouped, (("site", 0),), grouped.shape[0])


def spread_newest(newest):
    grouped = lax.all_gather(newest, "structur", axis=0, tiled=True)
    return with_halo(grouped, (("site", 0),), grouped.shape[0])


def tap_field(tiles, vectors):
    partial_field = jnp.einsum(
        "bpkij,bpkjs->bis", tiles, vectors, preferred_element_type=jnp.float32
    )
    return lax.psum(partial_field, "sub")


def per_device(tiles, history, self_inverse, pair_src, pair_delay, strike_seg, waveform):
    blk = history.shape[0]
    seg_count = history.shape[2]
    tap_local = tiles.shape[2]
    first_tap = lax.axis_index("sub") * tap_local
    taps = first_tap + jnp.arange(tap_local, dtype=jnp.int32)
    device = lax.axis_index("site") * lax.axis_size("structur") + lax.axis_index("structur")
    global_blocks = device * blk + jnp.arange(blk, dtype=jnp.int32)
    segments = global_blocks[:, None] * seg_count + jnp.arange(seg_count, dtype=jnp.int32)[None, :]
    hits = segments[:, :, None] == strike_seg[None, None, :]
    slots = place_sources(pair_src, blk)
    back = pair_delay[:, :, None] + taps[None, None, :] - 1
    nearby = spread_history(history)

    def advance(vectors, step):
        field = tap_field(tiles, vectors)
        incident = jnp.where(hits, waveform[step][None, None, :], jnp.float32(0.0))
        rhs = (incident - field).astype(jnp.bfloat16)
        return jnp.einsum(
            "bij,bjs->bis", self_inverse, rhs, preferred_element_type=jnp.float32
        ).astype(jnp.bfloat16)

    first = advance(nearby[slots[:, :, None], back], 0)
    fresh = spread_newest(first)
    later = back - 1
    older = nearby[slots[:, :, None], jnp.maximum(later, 0)]
    newest_rows = fresh[slots][:, :, None]
    second = advance(jnp.where((later < 0)[:, :, :, None, None], newest_rows, older), 1)
    return jnp.stack([first, second], axis=1)


def solution(mesh):
    in_specs = (
        P(("site", "structur"), None, "sub", None, None),
        P(("scenario", "site", "structur"), None, None, None),
        P(("site", "structur"), None, None),
        P(("site", "structur"), None),
        P(("site", "structur"), None),
        P("scenario"),
        P("scenario", None),
    )
    out_specs = P(("scenario", "site", "structur"), None, None, None)
    return jax.shard_map(
        per_device, mesh=mesh, in_specs=in_specs, out_specs=out_specs, check_vma=False
    )
```

profile of v0, /device:TPU:0, one launch (start us, length us, event | category | flops | bytes accessed | tf_op | source)
XLA Modules:
  0.0 145.0 jit_solution(447354561170501825)
XLA Ops:
  6.5 0.7 all-gather.3.cloned.1.call-update
  7.3 27.1 %all-gather.3.cloned.1.call-done = bf16[2,9,256,128]{3,2,1,0:T(8,128)(2,1)} async-done(((bf16[1,9,256,128]{3,2,1,0:T(8,128)(2,1)}), bf16[2,9,256,128]{3,2,1,0:T(8,128)(2,1)}) %all-gather.3.cloned.1.call-update) | async-done | bytes 1179664 | tf_op jit(solution)/shard_map/all_gather | solution.py:30
  34.4 3.5 %collective-permute-start = (bf16[2,9,256,128]{3,2,1,0:T(8,128)(2,1)}, bf16[2,9,256,128]{3,2,1,0:T(8,128)(2,1)S(1)}, u32[]{:S(2)}, u32[]{:S(2)}) collective-permute-start(bf16[2,9,256,128]{3,2,1,0:T(8,128)(2,1)} %all-gather.3.cloned.1.call-done), channel_id=1, source_target_pairs={{0,4},{4,8},{8,12},{1,5},{5,9},{9,13},{2,6},{6,10},{10,14},{3,7},{... | collective-permute-start | bytes 3538952 | tf_op jit(solution)/shard_map/ppermute | solution.py:12
  37.9 0.7 fusion.47
  38.6 1.3 collective-permute-start.1
  39.9 0.7 compare_select_fusion.2
  40.6 0.1 copy.27
  40.7 0.1 reshape.404
  40.8 22.5 %collective-permute-done = bf16[2,9,256,128]{3,2,1,0:T(8,128)(2,1)S(1)} collective-permute-done((bf16[2,9,256,128]{3,2,1,0:T(8,128)(2,1)}, bf16[2,9,256,128]{3,2,1,0:T(8,128)(2,1)S(1)}, u32[]{:S(2)}, u32[]{:S(2)}) %collective-permute-start) | collective-permute-done | bytes 1179680 | tf_op jit(solution)/shard_map/ppermute | solution.py:12
  63.3 1.1 constant_dynamic-update-slice_fusion.2
  64.5 2.4 %constant_dynamic-update-slice_fusion.1 = bf16[6,9,256,128]{3,2,1,0:T(8,128)(2,1)} fusion(bf16[6,9,256,128]{3,2,1,0:T(8,128)(2,1)} %constant_dynamic-update-slice_fusion.2, bf16[2,9,256,128]{3,2,1,0:T(8,128)(2,1)} %all-gather.3.cloned.1.call-done), kind=kLoop, calls=%fused_computation.37 | loop fusion | bytes 2359296
  66.9 1.2 collective-permute-done.1
  68.1 1.1 constant_dynamic-update-slice_fusion
  69.2 3.0 %gather_fusion = bf16[32,256,128]{2,1,0:T(8,128)(2,1)S(1)} fusion(bf16[6,9,256,128]{3,2,1,0:T(8,128)(2,1)} %constant_dynamic-update-slice_fusion, s32[32]{0:T(128)S(1)} %reshape.404), kind=kCustom, calls=%fused_computation | custom fusion | bytes 4194560 | tf_op jit(solution)/shard_map/gather | solution.py:68
  72.2 4.4 %fusion.12 = f32[1,256,128]{1,2,0:T(8,128)} fusion(bf16[8,4,256,128]{3,2,1,0:T(8,128)(2,1)S(1)} %bitcast.62, bf16[1,8,4,256,256]{4,3,2,1,0:T(8,128)(2,1)} %param.7), kind=kOutput, calls=%fused_computation.11 | convolution fusion | flops 536870912 | bytes 6422528 | tf_op jit(solution)/shard_map/bpkij,bpkjs->bis/dot_general | solution.py:40
  76.7 17.6 %all-reduce.3.cloned.1.call-done = f32[1,256,128]{1,2,0:T(8,128)} async-done(((f32[1,256,128]{1,2,0:T(8,128)}), f32[1,256,128]{1,2,0:T(8,128)}) %all-reduce.3.cloned.1.call-update) | async-done | bytes 131088 | tf_op jit(solution)/shard_map/psum | solution.py:43
  94.3 1.1 convolution_convert_fusion.1
  95.5 4.9 %all-gather = bf16[512,128]{0,1:T(8,128)(2,1)S(1)} all-gather(bf16[256,128]{0,1:T(8,128)(2,1)S(1)} %bitcast.63), channel_id=2, replica_groups=mesh['scenario'=2,'site'=4,'structur'=2,'sub'=2] {'structur'}, dimensions={0}, use_global_device_ids=true | all-gather | bytes 196608 | tf_op jit(solution)/shard_map/all_gather | solution.py:35
  100.4 0.1 copy.42
  100.5 1.3 collective-permute-start.3
  101.8 4.6 %collective-permute-start.2 = (bf16[2,256,128]{2,1,0:T(8,128)(2,1)S(1)}, bf16[2,256,128]{2,1,0:T(8,128)(2,1)S(1)}, u32[]{:S(2)}, u32[]{:S(2)}) collective-permute-start(bf16[2,256,128]{2,1,0:T(8,128)(2,1)S(1)} %bitcast.66), channel_id=1, source_target_pairs={{0,4},{4,8},{8,12},{1,5},{5,9},{9,13},{2,6},{6,10},{10,14},{3,7},{... | collective-permute-start | bytes 393224 | tf_op jit(solution)/shard_map/ppermute | solution.py:12
  106.4 0.1 add_compare_fusion
  106.5 0.1 copy.34
  106.6 0.1 reshape.420
  106.7 3.0 %gather_fusion.2 = bf16[32,256,128]{2,1,0:T(8,128)(2,1)S(1)} fusion(bf16[6,9,256,128]{3,2,1,0:T(8,128)(2,1)} %constant_dynamic-update-slice_fusion, s32[32]{0:T(128)S(1)} %reshape.420), kind=kCustom, calls=%fused_computation.2 | custom fusion | bytes 4194560 | tf_op jit(solution)/shard_map/gather | solution.py:71
  109.6 2.6 %copy.35 = bf16[8,4,256,128]{2,3,0,1:T(8,128)(2,1)} copy(bf16[8,4,256,128]{3,2,1,0:T(8,128)(2,1)S(1)} %bitcast.61) | data formatting | bytes 4194304 | tf_op jit(solution)/shard_map/gather | solution.py:71
  112.3 0.6 gather_fusion.1
  113.0 0.2 copy.33
  113.2 5.0 %fusion.7 = f32[1,256,128]{1,2,0:T(8,128)} fusion(bf16[8,4,256,128]{2,3,0,1:T(8,128)(2,1)} %copy.35, pred[8,4]{0,1:T(4,128)(4,1)S(1)} %add_compare_fusion, bf16[8,256,128]{1,2,0:T(8,128)(2,1)S(1)} %copy.33, bf16[1,8,4,256,256]{4,3,2,1,0:T(8,128)(2,1)} %param.7), kind=kOutput, calls=%fused_computation.10 | convolution fusion | flops 537919488 | bytes 6946848 | tf_op jit(solution)/shard_map/bpkij,bpkjs->bis/dot_general | solution.py:40
  118.2 18.4 %all-reduce.5.cloned.1.call-done = f32[1,256,128]{1,2,0:T(8,128)} async-done(((f32[1,256,128]{1,2,0:T(8,128)}), f32[1,256,128]{1,2,0:T(8,128)}) %all-reduce.5.cloned.1.call-update) | async-done | bytes 131088 | tf_op jit(solution)/shard_map/psum | solution.py:43
  136.6 1.1 fusion.17
  137.7 0.8 copy.37
  (25 shorter events, 0.2 us)
Async XLA Ops:
  6.5 87.8 %copy-start = (bf16[1,256,256]{2,1,0:T(8,128)(2,1)S(1)}, bf16[1,256,256]{2,1,0:T(8,128)(2,1)}, u32[]{:S(2)}) copy-start(bf16[1,256,256]{2,1,0:T(8,128)(2,1)} %param.9) | copy-start | bytes 393220
  6.5 27.9 %all-gather.3.cloned.1.call-start = ((), (), s32[]{:S(2)}) async-start(), calls=%async_computation | async-start | bytes 1769472 | tf_op jit(solution)/shard_map/all_gather | solution.py:30
  7.3 87.1 %all-reduce.3.cloned.1.call-start = ((), (), s32[]{:S(2)}) async-start(), calls=%async_computation.1 | async-start | bytes 262144 | tf_op jit(solution)/shard_map/psum | solution.py:43
  34.4 28.9 %collective-permute-start = (bf16[2,9,256,128]{3,2,1,0:T(8,128)(2,1)}, bf16[2,9,256,128]{3,2,1,0:T(8,128)(2,1)S(1)}, u32[]{:S(2)}, u32[]{:S(2)}) collective-permute-start(bf16[2,9,256,128]{3,2,1,0:T(8,128)(2,1)} %all-gather.3.cloned.1.call-done), channel_id=1, source_target_pairs={{0,4},{4,8},{8,12},{1,5},{5,9},{9,13},{2,6},{6,10},{10,14},{3,7},{... | collective-permute-start | bytes 3538952 | tf_op jit(solution)/shard_map/ppermute | solution.py:12
  38.6 29.5 %collective-permute-start.1 = (bf16[2,9,256,128]{3,2,1,0:T(8,128)(2,1)}, bf16[2,9,256,128]{3,2,1,0:T(8,128)(2,1)S(1)}, u32[]{:S(2)}, u32[]{:S(2)}) collective-permute-start(bf16[2,9,256,128]{3,2,1,0:T(8,128)(2,1)} %all-gather.3.cloned.1.call-done), channel_id=1, source_target_pairs={{4,0},{8,4},{12,8},{5,1},{9,5},{13,9},{6,2},{10,6},{14,10},{7,3},{... | collective-permute-start | bytes 3538952 | tf_op jit(solution)/shard_map/ppermute | solution.py:15
  72.2 4.5 %copy-start.2 = (f32[2,128]{1,0:T(2,128)S(1)}, f32[2,128]{1,0:T(2,128)}, u32[]{:S(2)}) copy-start(f32[2,128]{1,0:T(2,128)} %param.13) | copy-start | bytes 3076
  72.2 22.2 %copy-start.1 = (s32[128]{0:T(128)S(1)}, s32[128]{0:T(128)}, u32[]{:S(2)}) copy-start(s32[128]{0:T(128)} %param.12) | copy-start | bytes 1540
  72.2 34.2 %copy-start.3 = (s32[1,8]{1,0:T(1,128)S(1)}, s32[1,8]{1,0:T(1,128)}, u32[]{:S(2)}) copy-start(s32[1,8]{1,0:T(1,128)} %param.11) | copy-start | bytes 100
  76.6 59.9 %all-reduce.5.cloned.1.call-start = ((), (), s32[]{:S(2)}) async-start(), calls=%async_computation.2 | async-start | bytes 262144 | tf_op jit(solution)/shard_map/psum | solution.py:43
  100.5 11.7 %collective-permute-start.3 = (bf16[2,256,128]{2,1,0:T(8,128)(2,1)S(1)}, bf16[2,256,128]{2,1,0:T(8,128)(2,1)S(1)}, u32[]{:S(2)}, u32[]{:S(2)}) collective-permute-start(bf16[2,256,128]{2,1,0:T(8,128)(2,1)S(1)} %bitcast.65), channel_id=1, source_target_pairs={{4,0},{8,4},{12,8},{5,1},{9,5},{13,9},{6,2},{10,6},{14,10},{7,3},{... | collective-permute-start | bytes 393224 | tf_op jit(solution)/shard_map/ppermute | solution.py:15
  101.8 10.4 %collective-permute-start.2 = (bf16[2,256,128]{2,1,0:T(8,128)(2,1)S(1)}, bf16[2,256,128]{2,1,0:T(8,128)(2,1)S(1)}, u32[]{:S(2)}, u32[]{:S(2)}) collective-permute-start(bf16[2,256,128]{2,1,0:T(8,128)(2,1)S(1)} %bitcast.66), channel_id=1, source_target_pairs={{0,4},{4,8},{8,12},{1,5},{5,9},{9,13},{2,6},{6,10},{10,14},{3,7},{... | collective-permute-start | bytes 393224 | tf_op jit(solution)/shard_map/ppermute | solution.py:12
Sparse Core Ops, SparseCore 0:
  8.9 25.4 all-gather.2
  76.7 17.5 all-reduce.2
  118.3 18.1 all-reduce.4
where the time goes:
time: 145 us
  waiting for transfers between devices  87.6 us (60%)
  local copies, waits for them, and re-layouts  15.3 us (11%)
  between operations  13.3 us (9%)
  matrix products  11.6 us (8%)
  starting transfers between devices  10.7 us (7%)
  blocking collectives  4.94 us (3%)
  other arithmetic  1.58 us (1%)
    psum x2, waiting for transfers between devices, tap_field(): return lax.psum(partial_field, 'sub')  36 us
    all_gather x1, waiting for transfers between devices, spread_history(): grouped = lax.all_gather(history, 'structur', axis=0, tiled=True)  27.1 us
    ppermute x2, waiting for transfers between devices, with_halo(): lax.ppermute(lax.slice_in_dim(block, block.shape[dim] - width, None, axis...  22.5 us
    dot_general x2, matrix products, tap_field(): jnp.einsum('bpkij,bpkjs->bis', tiles, vectors, preferred_element_type=jnp...  9.37 us
    ppermute x2, starting transfers between devices, with_halo(): lax.ppermute(lax.slice_in_dim(block, block.shape[dim] - width, None, axis...  8.01 us
    gather x2, local copies, waits for them, and re-layouts, per_device(): older = nearby[slots[:, :, None], jnp.maximum(later, 0)]  5.58 us
    all_gather x1, blocking collectives, spread_newest(): grouped = lax.all_gather(newest, 'structur', axis=0, tiled=True)  4.94 us
    unnamed x10, local copies, waits for them, and re-layouts  3.55 us
  transfers between devices with their start and end apart: 7, of which 5 were waited for; matrix products, arithmetic and copies ran while one was open for 8% of the time, Pallas kernels for 0%

commit v1 on v0

v1 whole, which is shorter than its diff:
```python
import functools

import jax
import jax.numpy as jnp
from jax import lax
from jax.experimental import pallas as pl
from jax.experimental.pallas import tpu as pltpu
from jax.sharding import PartitionSpec as P

GRID_AXES = ("site", "structur", "sub")


def partner_site(site, kind, sites):
    other = site ^ 1 if kind == "even" else (site + 1 if site % 2 else site - 1)
    return other if 0 <= other < sites else None


def link_pairs(kind, turn, sites, groups):
    pairs = []
    for site in range(sites):
        to_site = site if kind == "own" else partner_site(site, kind, sites)
        if to_site is None:
            continue
        for member in range(groups):
            pairs.append(
                (site * groups + member, to_site * groups + (member - turn) % groups)
            )
    return pairs


def swap_cores(x):
    return lax.ppermute(x, "sub", [(0, 1), (1, 0)])


def field_kernel(first, count, has_acc, *refs):
    meta, tiles, extra = refs[:3]
    sources = refs[3 : 3 + count]
    refs = refs[3 + count :]
    acc_in = None
    if has_acc:
        acc_in, refs = refs[0], refs[1:]
    out, tile_buf, extra_buf, plane_buf, tile_sem, extra_sem, plane_sem = refs
    pairs, taps = tiles.shape[0], tiles.shape[1]
    planes = sources[0].shape[0]
    width = sources[0].shape[2]

    def wanted(p):
        slot = meta[0, p]
        return jnp.logical_and(slot >= first, slot < first + count)

    def tile_copy(p):
        return pltpu.make_async_copy(tiles.at[p], tile_buf.at[p], tile_sem.at[p])

    def extra_copy(p):
        return pltpu.make_async_copy(extra.at[p], extra_buf.at[p], extra_sem.at[p])

    def plane_copy(n):
        return pltpu.make_async_copy(
            sources[n], plane_buf.at[n, pl.ds(1, planes)], plane_sem.at[n]
        )

    for n in range(count):
        plane_copy(n).start()
    for p in range(pairs):

        @pl.when(wanted(p))
        def _():
            tile_copy(p).start()

        @pl.when(jnp.logical_and(wanted(p), meta[2, p] == 1))
        def _():
            extra_copy(p).start()

    for n in range(count):
        plane_buf[n, 0] = jnp.zeros(plane_buf.shape[2:], plane_buf.dtype)
    if has_acc:
        out[...] = acc_in[...]
    else:
        out[...] = jnp.zeros_like(out)
    for n in range(count):
        plane_copy(n).wait()

    for p in range(pairs):

        @pl.when(wanted(p))
        def _():
            slot = meta[0, p] - first
            late = meta[1, p]
            tile_copy(p).wait()
            total = None
            for k in range(taps):
                both = jnp.concatenate(
                    [plane_buf[slot, late + k + 1], plane_buf[slot, late + k]], axis=1
                )
                term = jnp.dot(
                    tile_buf[p, k], both, preferred_element_type=jnp.float32
                )
                total = term if total is None else total + term
            out[0] += total[:, :width]
            out[1] += total[:, width:]

        @pl.when(jnp.logical_and(wanted(p), meta[2, p] == 1))
        def _():
            extra_copy(p).wait()
            out[1] += jnp.dot(
                extra_buf[p],
                plane_buf[meta[0, p] - first, taps],
                preferred_element_type=jnp.float32,
            )


def field_part(meta, tiles, extra, sources, first, acc=None):
    count = len(sources)
    pairs, taps, rows, cols = tiles.shape
    planes, _, width = sources[0].shape
    anywhere = pl.BlockSpec(memory_space=pl.ANY)
    vmem = pl.BlockSpec(memory_space=pltpu.VMEM)
    operands = [meta, tiles, extra, *sources]
    specs = [pl.BlockSpec(memory_space=pltpu.SMEM)] + [anywhere] * (2 + count)
    if acc is not None:
        operands.append(acc)
        specs.append(vmem)
    plane_bytes = rows * width * 2
    need = (
        pairs * (taps + 1) * rows * cols * 2
        + count * (planes + 1) * plane_bytes
        + 16 * plane_bytes
    )
    return pl.pallas_call(
        functools.partial(field_kernel, first, count, acc is not None),
        out_shape=jax.ShapeDtypeStruct((2, rows, width), jnp.float32),
        in_specs=specs,
        out_specs=vmem,
        scratch_shapes=[
            pltpu.VMEM((pairs, taps, rows, cols), tiles.dtype),
            pltpu.VMEM((pairs, rows, cols), tiles.dtype),
            pltpu.VMEM((count, planes + 1, rows, width), sources[0].dtype),
            pltpu.SemaphoreType.DMA((pairs,)),
            pltpu.SemaphoreType.DMA((pairs,)),
            pltpu.SemaphoreType.DMA((count,)),
        ],
        compiler_params=pltpu.CompilerParams(vmem_limit_bytes=need + (2 << 20)),
        name="field_part",
    )(*operands)


def solve_rows(base, mine, other, inverse, strike, wave):
    rows, width = mine.shape
    segments = base + lax.broadcasted_iota(jnp.int32, (rows, width), 0)
    incident = jnp.where(segments == strike, wave, jnp.float32(0.0))
    rhs = (incident - (mine + other)).astype(jnp.bfloat16)
    return jnp.dot(inverse, rhs, preferred_element_type=jnp.float32).astype(
        jnp.bfloat16
    )


def first_kernel(meta, mine, other, inverse, strike, wave, out):
    out[...] = solve_rows(
        meta[3, 0], mine[...], other[...], inverse[...], strike[...], wave[0:1, :]
    )


def second_kernel(meta, first, mine, other, inverse, strike, wave, out):
    out[0] = first[...]
    out[1] = solve_rows(
        meta[3, 0], mine[...], other[...], inverse[...], strike[...], wave[1:2, :]
    )


def fresh_kernel(count, meta, tiles, extra, *refs):
    sources = refs[:count]
    acc, out, tile_buf, tile_sem = refs[count:]
    pairs = tiles.shape[0]

    def use(p, n):
        return meta[4, p] == n

    for p in range(pairs):
        local = jnp.logical_and(meta[4, p] >= 0, meta[3, 1] == 0)
        swapped = jnp.logical_and(meta[4, p] >= 0, meta[3, 1] == 1)

        @pl.when(local)
        def _():
            pltpu.make_async_copy(
                tiles.at[p, 0], tile_buf.at[p], tile_sem.at[p]
            ).start()

        @pl.when(swapped)
        def _():
            pltpu.make_async_copy(extra.at[p], tile_buf.at[p], tile_sem.at[p]).start()

    out[...] = acc[...]
    for p in range(pairs):

        @pl.when(meta[4, p] >= 0)
        def _():
            pltpu.make_async_copy(extra.at[p], tile_buf.at[p], tile_sem.at[p]).wait()

        for n in range(count):

            @pl.when(use(p, n))
            def _():
                out[...] += jnp.dot(
                    tile_buf[p], sources[n][...], preferred_element_type=jnp.float32
                )


def per_device(tiles, history, self_inverse, pair_src, pair_delay, strike_seg, waveform):
    sites, groups = lax.axis_size("site"), lax.axis_size("structur")
    site, member, core = (lax.axis_index(a) for a in GRID_AXES)
    tiles, history, inverse = tiles[0], history[0], self_inverse[0]
    src, delay = pair_src[0], pair_delay[0]
    pairs, taps, rows, cols = tiles.shape
    width = history.shape[2]

    planes = lax.dynamic_slice_in_dim(history, core * taps, taps + 1, axis=0)
    extra = swap_cores(tiles[:, 0])

    def fetch(x, kind, turn):
        return lax.ppermute(
            x, ("site", "structur"), link_pairs(kind, turn, sites, groups)
        )

    own = [planes] + [fetch(planes, "own", t) for t in range(1, groups)]
    even = [fetch(planes, "even", 0)]
    odd = [fetch(planes, "odd", 0)]
    even += [fetch(x, "even", 0) for x in own[1:]]
    odd += [fetch(x, "odd", 0) for x in own[1:]]
    near = own + even[:1] + odd[:1]
    far = even[1:] + odd[1:]

    turn = (src % groups - member) % groups
    dist = src // groups - site
    is_even = jnp.where(site % 2 == 0, dist == 1, dist == -1)
    slot = jnp.where(
        dist == 0,
        turn,
        jnp.where(
            turn == 0,
            jnp.where(is_even, groups, groups + 1),
            jnp.where(is_even, groups + 1 + turn, 2 * groups + turn),
        ),
    )

    messages = [("odd", t) for t in range(groups)]
    messages += [("even", t) for t in range(groups)]
    messages += [("own", t) for t in range(1, groups)]
    if len(messages) % 2 == 0:
        messages.append(None)
    rounds = (len(messages) + 1) // 2
    number = jnp.where(
        dist == 0,
        2 * groups - 1 + turn,
        jnp.where(is_even, groups + turn, turn),
    )
    mine_round = jnp.where(number % 2 == core, number // 2, -1)
    own_here = jnp.where(core == 1, rounds, -1)
    mine_round = jnp.where(
        jnp.logical_and(dist == 0, turn == 0), own_here, mine_round
    )
    mine_round = jnp.where(delay == 1, mine_round, -1)

    base = (site * groups + member) * rows
    lane = jnp.arange(pairs, dtype=jnp.int32)
    meta = jnp.stack(
        [
            slot,
            delay - 1,
            jnp.logical_and(delay == 1, core == 0).astype(jnp.int32),
            jnp.where(lane == 0, base, core),
            mine_round,
        ]
    ).astype(jnp.int32)

    acc = field_part(meta, tiles, extra, near, 0)
    acc = field_part(meta, tiles, extra, far, groups + 2, acc)
    mine0, mine1 = acc[0], acc[1]

    strike = strike_seg[None, :]
    smem = pl.BlockSpec(memory_space=pltpu.SMEM)
    vmem = pl.BlockSpec(memory_space=pltpu.VMEM)
    anywhere = pl.BlockSpec(memory_space=pl.ANY)
    current0 = pl.pallas_call(
        first_kernel,
        out_shape=jax.ShapeDtypeStruct((rows, width), jnp.bfloat16),
        in_specs=[smem] + [vmem] * 5,
        out_specs=vmem,
        name="first_currents",
    )(meta, mine0, swap_cores(mine0), inverse, strike, waveform)

    fresh = []
    for r in range(rounds):
        perm = []
        for c in range(2):
            m = 2 * r + c
            if m < len(messages) and messages[m] is not None:
                kind, t = messages[m]
                perm += [
                    (2 * a + c, 2 * b + c)
                    for a, b in link_pairs(kind, t, sites, groups)
                ]
        fresh.append(lax.ppermute(current0, GRID_AXES, perm))
    fresh.append(current0)

    mine1 = pl.pallas_call(
        functools.partial(fresh_kernel, len(fresh)),
        out_shape=jax.ShapeDtypeStruct((rows, width), jnp.float32),
        in_specs=[smem, anywhere, anywhere] + [vmem] * (len(fresh) + 1),
        out_specs=vmem,
        scratch_shapes=[
            pltpu.VMEM((pairs, rows, cols), tiles.dtype),
            pltpu.SemaphoreType.DMA((pairs,)),
        ],
        name="fresh_part",
    )(meta, tiles, extra, *fresh, mine1)

    currents = pl.pallas_call(
        second_kernel,
        out_shape=jax.ShapeDtypeStruct((2, rows, width), jnp.bfloat16),
        in_specs=[smem] + [vmem] * 6,
        out_specs=vmem,
        name="second_currents",
    )(meta, current0, mine1, swap_cores(mine1), inverse, strike, waveform)
    return currents[None]


def solution(mesh):
    in_specs = (
        P(("site", "structur"), None, "sub", None, None),
        P(("scenario", "site", "structur"), None, None, None),
        P(("site", "structur"), None, None),
        P(("site", "structur"), None),
        P(("site", "structur"), None),
        P("scenario"),
        P("scenario", None),
    )
    out_specs = P(("scenario", "site", "structur"), None, None, None)
    return jax.shard_map(
        per_device, mesh=mesh, in_specs=in_specs, out_specs=out_specs, check_vma=False
    )
```

time: 145 us -> 55.2 us (0.38)
  waiting for transfers between devices: 87.6 us -> 11.7 us
  Pallas kernels: 0 us -> 14.8 us
  between operations: 13.3 us -> 0.24 us
  matrix products: 11.6 us -> 0 us
  starting transfers between devices: 10.7 us -> 19.4 us
  local copies, waits for them, and re-layouts: 15.3 us -> 8.86 us
  blocking collectives: 4.94 us -> 0 us
  other arithmetic: 1.58 us -> 0.04 us
    psum x2 -> x0, waiting for transfers between devices: 36 us -> none  [tap_field(): return lax.psum(partial_field, 'sub')]
    all_gather x1 -> x0, waiting for transfers between devices: 27.1 us -> none  [spread_history(): grouped = lax.all_gather(history, 'structur', axis=0, tiled=True)]
    pallas_call x0 -> x5, Pallas kernels: none -> 14.8 us  [the longest x2 7.62 us: field_part(): pl.pallas_call(functools.partial(field_kernel, first, count, acc is not N...]
    ppermute x4 -> x11, waiting for transfers between devices: 23.8 us -> 11.7 us  [the longest x5 6.06 us: fetch(): lax.ppermute(x, ('site', 'structur'), link_pairs(kind, turn, sites, groups))]
    dot_general x4 -> x0, matrix products: 11.6 us -> none  [the longest x2 9.37 us: tap_field(): jnp.einsum('bpkij,bpkjs->bis', tiles, vectors, preferred_element_type=jnp...]
    gather x5 -> x0, local copies, waits for them, and re-layouts: 9.41 us -> none  [the longest x2 5.58 us: per_device(): older = nearby[slots[:, :, None], jnp.maximum(later, 0)]]
    ppermute x4 -> x11, starting transfers between devices: 10.6 us -> 19.4 us  [the longest x3 10.8 us: per_device(): fresh.append(lax.ppermute(current0, GRID_AXES, perm))]
    all_gather x1 -> x0, blocking collectives: 4.94 us -> none  [spread_newest(): grouped = lax.all_gather(newest, 'structur', axis=0, tiled=True)]
  transfers between devices with their start and end apart: 7 -> 11, of which waited for: 5 -> 4; matrix products, arithmetic and copies ran while one was open for 8% -> 0% of each run, Pallas kernels for 0% -> 9%
where the time goes in v1:
time: 55.2 us; the launch traced here: 55.1 us
  starting transfers between devices  19.4 us (35%)
  Pallas kernels  14.8 us (27%)
  waiting for transfers between devices  11.7 us (21%)
  local copies, waits for them, and re-layouts  8.86 us (16%)
    ppermute x3, starting transfers between devices, per_device(): fresh.append(lax.ppermute(current0, GRID_AXES, perm))  10.8 us
    ppermute x5, starting transfers between devices, fetch(): lax.ppermute(x, ('site', 'structur'), link_pairs(kind, turn, sites, groups))  8.03 us
    pallas_call x2, Pallas kernels, field_part(): pl.pallas_call(functools.partial(field_kernel, first, count, acc is not N...  7.62 us
    unnamed x27, local copies, waits for them, and re-layouts  7.04 us
    ppermute x5, waiting for transfers between devices, fetch(): lax.ppermute(x, ('site', 'structur'), link_pairs(kind, turn, sites, groups))  6.06 us
    pallas_call x1, Pallas kernels, per_device(): pl.pallas_call(functools.partial(fresh_kernel, len(fresh)), out_shape=jax...  3.41 us
    ppermute x3, waiting for transfers between devices, swap_cores(): return lax.ppermute(x, 'sub', [(0, 1), (1, 0)])  2.89 us
    ppermute x3, waiting for transfers between devices, per_device(): fresh.append(lax.ppermute(current0, GRID_AXES, perm))  2.75 us
  transfers between devices with their start and end apart: 11, of which 4 were waited for; matrix products, arithmetic and copies ran while one was open for 0% of the time, Pallas kernels for 9%

profile of v1, /device:TPU:0, one launch (start us, length us, event | category | flops | bytes accessed | tf_op | source)
XLA Modules:
  0.0 55.1 jit_solution(10531001290004479258)
XLA Ops:
  0.0 2.5 %copy.14 = bf16[1,8,4,256,256]{4,3,1,2,0:T(8,128)(2,1)S(1)} copy(bf16[1,8,4,256,256]{4,3,2,1,0:T(8,128)(2,1)} %param.7) | data formatting | bytes 8388608 | tf_op args[0]
  2.5 1.1 %slice_bitcast_fusion = bf16[8,256,256]{2,1,0:T(8,128)(2,1)} fusion(bf16[8,4,256,256]{3,2,0,1:T(8,128)(2,1)S(1)} %bitcast.18), kind=kLoop, calls=%fused_computation.1 | loop fusion | bytes 2097152 | tf_op jit(solution)/shard_map/squeeze | solution.py:217
  3.6 0.5 collective-permute-start
  4.1 2.6 %collective-permute-start.1 = (bf16[5,256,128]{2,1,0:T(8,128)(2,1)S(1)}, bf16[5,256,128]{2,1,0:T(8,128)(2,1)S(1)}, u32[]{:S(2)}, u32[]{:S(2)}) collective-permute-start(bf16[5,256,128]{2,1,0:T(8,128)(2,1)S(1)} %dynamic-slice_bitcast_fusion.refs_3_), channel_id=1, source_target_pairs={{0,2},{2,0},{4,6},{6,4},{8,10},{10,8},{12,14},{14,12},{1,3},{3,1},... | collective-permute-start | bytes 983048 | tf_op jit(solution)/shard_map/ppermute | solution.py:220
  6.7 1.6 %collective-permute-start.4 = (bf16[5,256,128]{2,1,0:T(8,128)(2,1)S(1)}, bf16[5,256,128]{2,1,0:T(8,128)(2,1)S(1)}, u32[]{:S(2)}, u32[]{:S(2)}) collective-permute-start(bf16[5,256,128]{2,1,0:T(8,128)(2,1)S(1)} %dynamic-slice_bitcast_fusion.refs_3_), channel_id=1, source_target_pairs={{0,4},{2,6},{4,0},{6,2},{8,12},{10,14},{12,8},{14,10},{1,5},{3,7},... | collective-permute-start | bytes 983048 | tf_op jit(solution)/shard_map/ppermute | solution.py:220
  8.2 0.7 %collective-permute-start.5 = (bf16[5,256,128]{2,1,0:T(8,128)(2,1)S(1)}, bf16[5,256,128]{2,1,0:T(8,128)(2,1)S(1)}, u32[]{:S(2)}, u32[]{:S(2)}) collective-permute-start(bf16[5,256,128]{2,1,0:T(8,128)(2,1)S(1)} %dynamic-slice_bitcast_fusion.refs_3_), channel_id=1, source_target_pairs={{4,8},{6,10},{8,4},{10,6},{5,9},{7,11},{9,5},{11,7},{20,24},{22,26... | collective-permute-start | bytes 983048 | tf_op jit(solution)/shard_map/ppermute | solution.py:220
  9.0 6.0 %collective-permute-done.1.refs_4_ = bf16[5,256,128]{2,1,0:T(8,128)(2,1)S(1)} collective-permute-done((bf16[5,256,128]{2,1,0:T(8,128)(2,1)S(1)}, bf16[5,256,128]{2,1,0:T(8,128)(2,1)S(1)}, u32[]{:S(2)}, u32[]{:S(2)}) %collective-permute-start.1) | collective-permute-done | bytes 327712 | tf_op jit(solution)/shard_map/ppermute | solution.py:220
  15.0 1.8 %collective-permute-start.2 = (bf16[5,256,128]{2,1,0:T(8,128)(2,1)S(1)}, bf16[5,256,128]{2,1,0:T(8,128)(2,1)S(1)}, u32[]{:S(2)}, u32[]{:S(2)}) collective-permute-start(bf16[5,256,128]{2,1,0:T(8,128)(2,1)S(1)} %collective-permute-done.1.refs_4_), channel_id=1, source_target_pairs={{0,4},{2,6},{4,0},{6,2},{8,12},{10,14},{12,8},{14,10},{1,5},{3,7},... | collective-permute-start | bytes 983048 | tf_op jit(solution)/shard_map/ppermute | solution.py:220
  16.9 1.4 %collective-permute-start.3 = (bf16[5,256,128]{2,1,0:T(8,128)(2,1)S(1)}, bf16[5,256,128]{2,1,0:T(8,128)(2,1)}, u32[]{:S(2)}, u32[]{:S(2)}) collective-permute-start(bf16[5,256,128]{2,1,0:T(8,128)(2,1)S(1)} %collective-permute-done.1.refs_4_), channel_id=1, source_target_pairs={{4,8},{6,10},{8,4},{10,6},{5,9},{7,11},{9,5},{11,7},{20,24},{22,26... | collective-permute-start | bytes 983048 | tf_op jit(solution)/shard_map/ppermute | solution.py:220
  18.3 0.0 collective-permute-done.5.refs_6_
  18.3 0.0 collective-permute-done.refs_2_.extra
  18.4 0.0 copy-start.1
  18.4 2.6 %copy-done.1 = bf16[1,8,4,256,256]{4,3,2,1,0:T(8,128)(2,1)S(1)} copy-done((bf16[1,8,4,256,256]{4,3,2,1,0:T(8,128)(2,1)S(1)}, bf16[1,8,4,256,256]{4,3,2,1,0:T(8,128)(2,1)}, u32[]{:S(2)}) %copy-start.1) | copy-done | bytes 4194328
  20.9 4.9 %field_part.2.refs_5_ = f32[2,256,128]{2,1,0:T(8,128)S(1)} custom-call(s32[5,8]{1,0:T(8,128)S(1)} %stack.2.refs_0_.meta, bf16[8,4,256,256]{3,2,1,0:T(8,128)(2,1)S(1)} %bitcast.16, bf16[8,256,256]{2,1,0:T(8,128)(2,1)S(1)} %collective-permute-done.refs_2_.extra, bf16[5,256,128]{2,1,0:T(8,128)(2,1)S(1)} %dynamic-slice_bitcast_fusion.refs_3_, ...), custom_call_target="tpu_custom_call" | custom-call | tf_op jit(solution)/shard_map/field_part/pallas_call | solution.py:129
  25.9 0.0 collective-permute-done.2.refs_3_
  25.9 0.0 collective-permute-done.3.refs_4_
  25.9 2.7 %field_part.3 = f32[2,256,128]{2,1,0:T(8,128)S(1)} custom-call(s32[5,8]{1,0:T(8,128)S(1)} %stack.2.refs_0_.meta, bf16[8,4,256,256]{3,2,1,0:T(8,128)(2,1)S(1)} %bitcast.17, bf16[8,256,256]{2,1,0:T(8,128)(2,1)S(1)} %collective-permute-done.refs_2_.extra, bf16[5,256,128]{2,1,0:T(8,128)(2,1)S(1)} %collective-permute-done.2.refs_3_, ...), custom_call_target="tpu_custom_call" | custom-call | tf_op jit(solution)/shard_map/field_part/pallas_call | solution.py:129
  28.6 0.7 %slice_bitcast_fusion.1 = (f32[256,128]{1,0:T(8,128)}, f32[256,128]{1,0:T(8,128)S(1)}) fusion(f32[2,256,128]{2,1,0:T(8,128)S(1)} %field_part.3), kind=kLoop, calls=%fused_computation.3 | loop fusion | bytes 524288 | tf_op jit(solution)/shard_map/squeeze | solution.py:277
  29.3 0.0 collective-permute-start.6
  29.3 1.3 %collective-permute-done.6.other = f32[256,128]{1,0:T(8,128)S(1)} collective-permute-done((f32[256,128]{1,0:T(8,128)S(1)}, f32[256,128]{1,0:T(8,128)S(1)}, u32[]{:S(2)}, u32[]{:S(2)}) %collective-permute-start.6) | collective-permute-done | bytes 131104 | tf_op jit(solution)/shard_map/ppermute | solution.py:32
  30.7 0.6 %copy-done.6 = f32[256,128]{1,0:T(8,128)} copy-done((f32[256,128]{1,0:T(8,128)}, f32[256,128]{1,0:T(8,128)S(1)}, u32[]{:S(2)}) %copy-start.6) | copy-done | bytes 131096
  31.3 1.9 %first_currents.1.refs_3_.first = bf16[256,128]{1,0:T(8,128)(2,1)} custom-call(s32[5,8]{1,0:T(8,128)} %copy-done.4, f32[256,128]{1,0:T(8,128)} %copy-done.5, f32[256,128]{1,0:T(8,128)} %copy-done.6, bf16[256,256]{1,0:T(8,128)(2,1)} %bitcast.19, s32[1,128]{1,0:T(1,128)} %bitcast.21, f32[2,128]{1,0:T(2,128)} %wave.3), custom_call_target="tpu_custom_call" | custom-call | tf_op jit(solution)/shard_map/first_currents/pallas_call | solution.py:283
  33.2 0.7 %collective-permute-start.7 = (bf16[256,128]{1,0:T(8,128)(2,1)}, bf16[256,128]{1,0:T(8,128)(2,1)S(1)}, u32[]{:S(2)}, u32[]{:S(2)}) collective-permute-start(bf16[256,128]{1,0:T(8,128)(2,1)} %first_currents.1.refs_3_.first), channel_id=1, source_target_pairs={{4,8},{6,10},{8,4},{10,6},{5,11},{7,9},{9,7},{11,5},{20,24},{22,26... | collective-permute-start | bytes 196616 | tf_op jit(solution)/shard_map/ppermute | solution.py:302
  33.8 6.6 %collective-permute-start.8 = (bf16[256,128]{1,0:T(8,128)(2,1)}, bf16[256,128]{1,0:T(8,128)(2,1)S(1)}, u32[]{:S(2)}, u32[]{:S(2)}) collective-permute-start(bf16[256,128]{1,0:T(8,128)(2,1)} %first_currents.1.refs_3_.first), channel_id=1, source_target_pairs={{0,4},{2,6},{4,0},{6,2},{8,12},{10,14},{12,8},{14,10},{1,7},{3,5},... | collective-permute-start | bytes 196616 | tf_op jit(solution)/shard_map/ppermute | solution.py:302
  40.5 3.6 %collective-permute-start.9 = (bf16[256,128]{1,0:T(8,128)(2,1)}, bf16[256,128]{1,0:T(8,128)(2,1)S(1)}, u32[]{:S(2)}, u32[]{:S(2)}) collective-permute-start(bf16[256,128]{1,0:T(8,128)(2,1)} %first_currents.1.refs_3_.first), channel_id=1, source_target_pairs={{0,2},{2,0},{4,6},{6,4},{8,10},{10,8},{12,14},{14,12},{16,18},{18,... | collective-permute-start | bytes 196616 | tf_op jit(solution)/shard_map/ppermute | solution.py:302
  44.1 2.7 %collective-permute-done.9.refs_2_ = bf16[256,128]{1,0:T(8,128)(2,1)S(1)} collective-permute-done((bf16[256,128]{1,0:T(8,128)(2,1)}, bf16[256,128]{1,0:T(8,128)(2,1)S(1)}, u32[]{:S(2)}, u32[]{:S(2)}) %collective-permute-start.9) | collective-permute-done | bytes 65568 | tf_op jit(solution)/shard_map/ppermute | solution.py:302
  46.8 0.6 %copy-done.10 = bf16[256,128]{1,0:T(8,128)(2,1)} copy-done((bf16[256,128]{1,0:T(8,128)(2,1)}, bf16[256,128]{1,0:T(8,128)(2,1)S(1)}, u32[]{:S(2)}) %copy-start.10) | copy-done | bytes 65560
  47.5 3.4 %fresh_part.1.mine = f32[256,128]{1,0:T(8,128)} custom-call(s32[5,8]{1,0:T(8,128)} %copy-done.4, bf16[8,4,256,256]{3,2,1,0:T(8,128)(2,1)} %bitcast.15, bf16[8,256,256]{2,1,0:T(8,128)(2,1)} %copy-done.3, bf16[256,128]{1,0:T(8,128)(2,1)} %copy-done.8, bf16[256,128]{1,0:T(8,128)(2,1)} %copy-done.9, bf16[256,128]{1,0:T(8,128)(2,1)} %copy-done.10, ...), custom_call_target="tpu_custom_call" | custom-call | tf_op jit(solution)/shard_map/fresh_part/pallas_call | solution.py:305
  50.9 0.1 collective-permute-start.10
  51.0 1.5 %collective-permute-done.10.other = f32[256,128]{1,0:T(8,128)S(1)} collective-permute-done((f32[256,128]{1,0:T(8,128)}, f32[256,128]{1,0:T(8,128)S(1)}, u32[]{:S(2)}, u32[]{:S(2)}) %collective-permute-start.10) | collective-permute-done | bytes 131104 | tf_op jit(solution)/shard_map/ppermute | solution.py:32
  52.5 0.7 %copy-done.7 = f32[256,128]{1,0:T(8,128)} copy-done((f32[256,128]{1,0:T(8,128)}, f32[256,128]{1,0:T(8,128)S(1)}, u32[]{:S(2)}) %copy-start.7) | copy-done | bytes 131096
  53.2 1.9 %second_currents.1 = bf16[2,256,128]{2,1,0:T(8,128)(2,1)} custom-call(s32[5,8]{1,0:T(8,128)} %copy-done.4, bf16[256,128]{1,0:T(8,128)(2,1)} %first_currents.1.refs_3_.first, f32[256,128]{1,0:T(8,128)} %fresh_part.1.mine, f32[256,128]{1,0:T(8,128)} %copy-done.7, bf16[256,256]{1,0:T(8,128)(2,1)} %bitcast.20, s32[1,128]{1,0:T(1,128)} %bitcast.22, f32[2,128]{1,0:T(2,128)} %wave.3), custom_call_target="tpu_custom_call" | custom-call | tf_op jit(solution)/shard_map/second_currents/pallas_call | solution.py:317
  (29 shorter events, 0.1 us)
Async XLA Ops:
  0.0 4.1 %copy-start = (bf16[1,9,256,128]{3,2,1,0:T(8,128)(2,1)S(1)}, bf16[1,9,256,128]{3,2,1,0:T(8,128)(2,1)}, u32[]{:S(2)}) copy-start(bf16[1,9,256,128]{3,2,1,0:T(8,128)(2,1)} %param.8) | copy-start | bytes 1769476
  0.0 8.9 %copy-start.12 = (s32[1,8]{1,0:T(1,128)S(1)}, s32[1,8]{1,0:T(1,128)}, u32[]{:S(2)}) copy-start(s32[1,8]{1,0:T(1,128)} %param.11) | copy-start | bytes 100
  0.0 8.9 %copy-start.11 = (s32[1,8]{1,0:T(1,128)S(1)}, s32[1,8]{1,0:T(1,128)}, u32[]{:S(2)}) copy-start(s32[1,8]{1,0:T(1,128)} %param.10) | copy-start | bytes 100
  3.6 14.7 %collective-permute-start = (bf16[8,256,256]{2,1,0:T(8,128)(2,1)}, bf16[8,256,256]{2,1,0:T(8,128)(2,1)S(1)}, u32[]{:S(2)}, u32[]{:S(2)}) collective-permute-start(bf16[8,256,256]{2,1,0:T(8,128)(2,1)} %slice_bitcast_fusion), channel_id=1, source_target_pairs={{0,1},{1,0},{2,3},{3,2},{4,5},{5,4},{6,7},{7,6},{8,9},{9,8},{10,11... | collective-permute-start | bytes 3145736 | tf_op jit(solution)/shard_map/ppermute | solution.py:32
  4.1 10.9 %collective-permute-start.1 = (bf16[5,256,128]{2,1,0:T(8,128)(2,1)S(1)}, bf16[5,256,128]{2,1,0:T(8,128)(2,1)S(1)}, u32[]{:S(2)}, u32[]{:S(2)}) collective-permute-start(bf16[5,256,128]{2,1,0:T(8,128)(2,1)S(1)} %dynamic-slice_bitcast_fusion.refs_3_), channel_id=1, source_target_pairs={{0,2},{2,0},{4,6},{6,4},{8,10},{10,8},{12,14},{14,12},{1,3},{3,1},... | collective-permute-start | bytes 983048 | tf_op jit(solution)/shard_map/ppermute | solution.py:220
  6.7 11.7 %collective-permute-start.4 = (bf16[5,256,128]{2,1,0:T(8,128)(2,1)S(1)}, bf16[5,256,128]{2,1,0:T(8,128)(2,1)S(1)}, u32[]{:S(2)}, u32[]{:S(2)}) collective-permute-start(bf16[5,256,128]{2,1,0:T(8,128)(2,1)S(1)} %dynamic-slice_bitcast_fusion.refs_3_), channel_id=1, source_target_pairs={{0,4},{2,6},{4,0},{6,2},{8,12},{10,14},{12,8},{14,10},{1,5},{3,7},... | collective-permute-start | bytes 983048 | tf_op jit(solution)/shard_map/ppermute | solution.py:220
  8.2 10.1 %collective-permute-start.5 = (bf16[5,256,128]{2,1,0:T(8,128)(2,1)S(1)}, bf16[5,256,128]{2,1,0:T(8,128)(2,1)S(1)}, u32[]{:S(2)}, u32[]{:S(2)}) collective-permute-start(bf16[5,256,128]{2,1,0:T(8,128)(2,1)S(1)} %dynamic-slice_bitcast_fusion.refs_3_), channel_id=1, source_target_pairs={{4,8},{6,10},{8,4},{10,6},{5,9},{7,11},{9,5},{11,7},{20,24},{22,26... | collective-permute-start | bytes 983048 | tf_op jit(solution)/shard_map/ppermute | solution.py:220
  15.0 10.8 %collective-permute-start.2 = (bf16[5,256,128]{2,1,0:T(8,128)(2,1)S(1)}, bf16[5,256,128]{2,1,0:T(8,128)(2,1)S(1)}, u32[]{:S(2)}, u32[]{:S(2)}) collective-permute-start(bf16[5,256,128]{2,1,0:T(8,128)(2,1)S(1)} %collective-permute-done.1.refs_4_), channel_id=1, source_target_pairs={{0,4},{2,6},{4,0},{6,2},{8,12},{10,14},{12,8},{14,10},{1,5},{3,7},... | collective-permute-start | bytes 983048 | tf_op jit(solution)/shard_map/ppermute | solution.py:220
  16.9 9.0 %collective-permute-start.3 = (bf16[5,256,128]{2,1,0:T(8,128)(2,1)S(1)}, bf16[5,256,128]{2,1,0:T(8,128)(2,1)}, u32[]{:S(2)}, u32[]{:S(2)}) collective-permute-start(bf16[5,256,128]{2,1,0:T(8,128)(2,1)S(1)} %collective-permute-done.1.refs_4_), channel_id=1, source_target_pairs={{4,8},{6,10},{8,4},{10,6},{5,9},{7,11},{9,5},{11,7},{20,24},{22,26... | collective-permute-start | bytes 983048 | tf_op jit(solution)/shard_map/ppermute | solution.py:220
  18.3 10.3 %copy-start.4 = (s32[5,8]{1,0:T(8,128)}, s32[5,8]{1,0:T(8,128)S(1)}, u32[]{:S(2)}) copy-start(s32[5,8]{1,0:T(8,128)S(1)} %stack.2.refs_0_.meta) | copy-start | bytes 484
  18.4 10.3 %copy-start.3 = (bf16[8,256,256]{2,1,0:T(8,128)(2,1)}, bf16[8,256,256]{2,1,0:T(8,128)(2,1)S(1)}, u32[]{:S(2)}) copy-start(bf16[8,256,256]{2,1,0:T(8,128)(2,1)S(1)} %collective-permute-done.refs_2_.extra) | copy-start | bytes 3145732
  18.4 2.6 %copy-start.1 = (bf16[1,8,4,256,256]{4,3,2,1,0:T(8,128)(2,1)S(1)}, bf16[1,8,4,256,256]{4,3,2,1,0:T(8,128)(2,1)}, u32[]{:S(2)}) copy-start(bf16[1,8,4,256,256]{4,3,2,1,0:T(8,128)(2,1)} %param.7) | copy-start | bytes 12582916
  20.9 4.9 %copy-start.2 = (bf16[1,8,4,256,256]{4,3,2,1,0:T(8,128)(2,1)S(1)}, bf16[1,8,4,256,256]{4,3,2,1,0:T(8,128)(2,1)}, u32[]{:S(2)}) copy-start(bf16[1,8,4,256,256]{4,3,2,1,0:T(8,128)(2,1)} %param.7) | copy-start | bytes 12582916
  29.3 1.4 %copy-start.5 = (f32[256,128]{1,0:T(8,128)}, f32[256,128]{1,0:T(8,128)S(1)}, u32[]{:S(2)}) copy-start(f32[256,128]{1,0:T(8,128)S(1)} %get-tuple-element.9.mine) | copy-start | bytes 393220
  29.3 1.3 %collective-permute-start.6 = (f32[256,128]{1,0:T(8,128)S(1)}, f32[256,128]{1,0:T(8,128)S(1)}, u32[]{:S(2)}, u32[]{:S(2)}) collective-permute-start(f32[256,128]{1,0:T(8,128)S(1)} %get-tuple-element.9.mine), channel_id=1, source_target_pairs={{0,1},{1,0},{2,3},{3,2},{4,5},{5,4},{6,7},{7,6},{8,9},{9,8},{10,11... | collective-permute-start | bytes 393224 | tf_op jit(solution)/shard_map/ppermute | solution.py:32
  30.7 0.7 %copy-start.6 = (f32[256,128]{1,0:T(8,128)}, f32[256,128]{1,0:T(8,128)S(1)}, u32[]{:S(2)}) copy-start(f32[256,128]{1,0:T(8,128)S(1)} %collective-permute-done.6.other) | copy-start | bytes 393220
  33.2 10.9 %collective-permute-start.7 = (bf16[256,128]{1,0:T(8,128)(2,1)}, bf16[256,128]{1,0:T(8,128)(2,1)S(1)}, u32[]{:S(2)}, u32[]{:S(2)}) collective-permute-start(bf16[256,128]{1,0:T(8,128)(2,1)} %first_currents.1.refs_3_.first), channel_id=1, source_target_pairs={{4,8},{6,10},{8,4},{10,6},{5,11},{7,9},{9,7},{11,5},{20,24},{22,26... | collective-permute-start | bytes 196616 | tf_op jit(solution)/shard_map/ppermute | solution.py:302
  33.8 10.2 %collective-permute-start.8 = (bf16[256,128]{1,0:T(8,128)(2,1)}, bf16[256,128]{1,0:T(8,128)(2,1)S(1)}, u32[]{:S(2)}, u32[]{:S(2)}) collective-permute-start(bf16[256,128]{1,0:T(8,128)(2,1)} %first_currents.1.refs_3_.first), channel_id=1, source_target_pairs={{0,4},{2,6},{4,0},{6,2},{8,12},{10,14},{12,8},{14,10},{1,7},{3,5},... | collective-permute-start | bytes 196616 | tf_op jit(solution)/shard_map/ppermute | solution.py:302
  40.5 6.4 %collective-permute-start.9 = (bf16[256,128]{1,0:T(8,128)(2,1)}, bf16[256,128]{1,0:T(8,128)(2,1)S(1)}, u32[]{:S(2)}, u32[]{:S(2)}) collective-permute-start(bf16[256,128]{1,0:T(8,128)(2,1)} %first_currents.1.refs_3_.first), channel_id=1, source_target_pairs={{0,2},{2,0},{4,6},{6,4},{8,10},{10,8},{12,14},{14,12},{16,18},{18,... | collective-permute-start | bytes 196616 | tf_op jit(solution)/shard_map/ppermute | solution.py:302
  44.1 2.8 %copy-start.8 = (bf16[256,128]{1,0:T(8,128)(2,1)}, bf16[256,128]{1,0:T(8,128)(2,1)S(1)}, u32[]{:S(2)}) copy-start(bf16[256,128]{1,0:T(8,128)(2,1)S(1)} %collective-permute-done.7.refs_0_) | copy-start | bytes 196612
  44.1 2.8 %copy-start.9 = (bf16[256,128]{1,0:T(8,128)(2,1)}, bf16[256,128]{1,0:T(8,128)(2,1)S(1)}, u32[]{:S(2)}) copy-start(bf16[256,128]{1,0:T(8,128)(2,1)S(1)} %collective-permute-done.8.refs_1_) | copy-start | bytes 196612
  46.8 0.6 %copy-start.10 = (bf16[256,128]{1,0:T(8,128)(2,1)}, bf16[256,128]{1,0:T(8,128)(2,1)S(1)}, u32[]{:S(2)}) copy-start(bf16[256,128]{1,0:T(8,128)(2,1)S(1)} %collective-permute-done.9.refs_2_) | copy-start | bytes 196612
  50.9 1.6 %collective-permute-start.10 = (f32[256,128]{1,0:T(8,128)}, f32[256,128]{1,0:T(8,128)S(1)}, u32[]{:S(2)}, u32[]{:S(2)}) collective-permute-start(f32[256,128]{1,0:T(8,128)} %fresh_part.1.mine), channel_id=1, source_target_pairs={{0,1},{1,0},{2,3},{3,2},{4,5},{5,4},{6,7},{7,6},{8,9},{9,8},{10,11... | collective-permute-start | bytes 393224 | tf_op jit(solution)/shard_map/ppermute | solution.py:32
  52.5 0.7 %copy-start.7 = (f32[256,128]{1,0:T(8,128)}, f32[256,128]{1,0:T(8,128)S(1)}, u32[]{:S(2)}) copy-start(f32[256,128]{1,0:T(8,128)S(1)} %collective-permute-done.10.other) | copy-start | bytes 393220

commit v2 on v0

v2 whole, which is shorter than its diff:
```python
import functools

import jax
import jax.numpy as jnp
from jax import lax
from jax.experimental import pallas as pl
from jax.experimental.pallas import tpu as pltpu
from jax.sharding import PartitionSpec as P

GRID_AXES = ("site", "structur", "sub")
SMEM = pl.BlockSpec(memory_space=pltpu.SMEM)
VMEM = pl.BlockSpec(memory_space=pltpu.VMEM)
ANY = pl.BlockSpec(memory_space=pl.ANY)
SMALL = pltpu.CompilerParams(vmem_limit_bytes=4 << 20)

SLOT, LATE, NEWS, ORDER, PLACE = range(5)
CHUNK = 4


def held(x):
    return pltpu.with_memory_space_constraint(x, pltpu.VMEM)


def far(x):
    return pltpu.with_memory_space_constraint(x, pltpu.HBM)


def table(x):
    return pltpu.with_memory_space_constraint(x, pltpu.SMEM)


def partner_site(site, kind, sites):
    other = site ^ 1 if kind == "even" else (site + 1 if site % 2 else site - 1)
    return other if 0 <= other < sites else None


def link_pairs(kind, turn, sites, groups):
    pairs = []
    for site in range(sites):
        to_site = site if kind == "own" else partner_site(site, kind, sites)
        if to_site is None:
            continue
        for member in range(groups):
            pairs.append(
                (site * groups + member, to_site * groups + (member - turn) % groups)
            )
    return pairs


def swap_cores(x):
    return lax.ppermute(x, "sub", [(0, 1), (1, 0)])


def start_kernel(slots, sites, groups, *refs):
    src, delay, history, tiles, planes, taps, meta, src_buf, delay_buf, sem = refs
    site, member, core = (lax.axis_index(a) for a in GRID_AXES)
    count, rows = planes.shape[:2]
    copies = [
        pltpu.make_async_copy(
            history.at[pl.ds(core * (count - 1), count)], planes, sem.at[0]
        ),
        pltpu.make_async_copy(src, src_buf, sem.at[1]),
        pltpu.make_async_copy(delay, delay_buf, sem.at[2]),
        pltpu.make_async_copy(tiles.at[:, 0], taps, sem.at[3]),
    ]
    for copy in copies:
        copy.start()
    copies[1].wait()
    copies[2].wait()
    even_step = jnp.where(site % 2 == 0, 1, -1)
    ahead = jnp.int32(0)
    behind = jnp.int32(src.shape[1])
    for p in range(src.shape[1]):
        value, wait = src_buf[0, p], delay_buf[0, p]
        turn = (value % groups - member + groups) % groups
        dist = value // groups - site
        kind = jnp.where(dist == 0, 2, jnp.where(dist == even_step, 1, 0))
        key = kind * groups + turn
        slot = jnp.int32(-1)
        for n in range(3 * groups):
            mine = jnp.where(core == 0, slots[0][n], slots[1][n])
            slot = jnp.where(key == n, mine, slot)
        mine = jnp.where(kind == 2, 0, jnp.where(kind == 1 - core, 1, -1))
        news = jnp.logical_and(wait == 1, mine >= 0)
        meta[SLOT, p] = slot
        meta[LATE, p] = wait - 1
        meta[NEWS, p] = jnp.where(news, 2 * turn + mine, -1)
        relayed = slot >= groups + 2
        behind = behind - jnp.where(relayed, 0, 1)
        meta[ORDER, jnp.where(relayed, ahead, behind)] = p
        ahead = ahead + jnp.where(relayed, 1, 0)
        meta[PLACE, p] = core
    meta[PLACE, 0] = (site * groups + member) * rows
    meta[PLACE, 2] = ahead
    copies[0].wait()
    copies[3].wait()


def near_kernel(count, meta, tiles, extra, *refs):
    sources, (total, newest) = refs[:count], refs[count:]
    width = sources[0].shape[2]
    taps = tiles.shape[1]
    core = meta[PLACE, 1]
    total[...] = jnp.zeros_like(total)

    def one(p, source):
        late = meta[LATE, p]
        empty = jnp.zeros(source.shape[1:], source.dtype)
        right = jnp.where(late == 1, source[0], empty)
        planes = []
        for k in range(taps):
            planes.append(jnp.concatenate([source[late + k], right], axis=1))
            right = source[late + k]
        total[...] += jnp.dot(
            jnp.concatenate([tiles[p, k] for k in range(taps)], axis=1),
            jnp.concatenate(planes, axis=0),
            preferred_element_type=jnp.float32,
        )

        @pl.when(jnp.logical_and(core == 0, late == 0))
        def _():
            total[:, width:] += jnp.dot(
                extra[p], source[taps - 1], preferred_element_type=jnp.float32
            )

    @pl.loop(0, tiles.shape[0])
    def _(p):
        @pl.when(core == 0)
        def _():
            newest[p] = tiles[p, 0]

        @pl.when(core == 1)
        def _():
            newest[p] = extra[p]

        for slot, source in enumerate(sources):
            pl.when(meta[SLOT, p] == slot)(functools.partial(one, p, source))


def near_part(meta, tiles, extra, sources):
    rows, width = sources[0].shape[1:]
    return pl.pallas_call(
        functools.partial(near_kernel, len(sources)),
        out_shape=[
            pltpu.VMEM((rows, 2 * width), jnp.float32),
            pltpu.VMEM(extra.shape, extra.dtype),
        ],
        in_specs=[SMEM] + [VMEM] * (2 + len(sources)),
        out_specs=[VMEM, VMEM],
        compiler_params=SMALL,
        name="near_part",
    )(table(meta), held(tiles), held(extra), *[held(x) for x in sources])


def relayed_kernel(first, count, meta, tiles, extra, acc, *refs):
    sources, (out0, out1, total, store) = refs[:count], refs[count:]
    planes, _, width = sources[0].shape
    pairs, taps = tiles.shape[:2]
    none = count * planes
    for n, source in enumerate(sources):
        store[n * planes : (n + 1) * planes] = source[...]
    store[none] = jnp.zeros(store.shape[1:], store.dtype)
    total[...] = acc[...]

    def chunk(start):
        numbers, left, right, swapped = [], [], [], []
        for i in range(start, start + CHUNK):
            p = meta[ORDER, i]
            used = i < meta[PLACE, 2]
            late = meta[LATE, p]
            base = (meta[SLOT, p] - first) * planes
            numbers.append(p)
            places = [jnp.where(used, base + late + k, none) for k in range(taps)]
            before = jnp.where(jnp.logical_and(used, late == 1), base, none)
            left += places
            right += [before] + places[:-1]
            swapped.append(
                jnp.where(jnp.logical_and(used, late == 0), base + taps - 1, none)
            )
        total[...] += jnp.dot(
            jnp.concatenate([tiles[p, k] for p in numbers for k in range(taps)], axis=1),
            jnp.concatenate(
                [
                    jnp.concatenate([store[a], store[b]], axis=1)
                    for a, b in zip(left, right)
                ],
                axis=0,
            ),
            preferred_element_type=jnp.float32,
        )

        @pl.when(meta[PLACE, 1] == 0)
        def _():
            total[:, width:] += jnp.dot(
                jnp.concatenate([extra[p] for p in numbers], axis=1),
                jnp.concatenate([store[a] for a in swapped], axis=0),
                preferred_element_type=jnp.float32,
            )

    for start in range(0, pairs, CHUNK):
        pl.when(meta[PLACE, 2] > start)(functools.partial(chunk, start))
    out0[...] = total[:, :width]
    out1[...] = total[:, width:]


def relayed_part(meta, tiles, extra, acc, sources, first):
    planes, rows, width = sources[0].shape
    store = (len(sources) * planes + 1, rows, width)
    half = pltpu.VMEM((rows, width), jnp.float32)
    room = 2 * store[0] * rows * width + 4 * acc.size
    return pl.pallas_call(
        functools.partial(relayed_kernel, first, len(sources)),
        out_shape=[half, half],
        in_specs=[SMEM] + [VMEM] * (3 + len(sources)),
        out_specs=[VMEM, VMEM],
        scratch_shapes=[
            pltpu.VMEM(acc.shape, acc.dtype),
            pltpu.VMEM(store, sources[0].dtype),
        ],
        compiler_params=pltpu.CompilerParams(vmem_limit_bytes=room + (4 << 20)),
        name="relayed_part",
    )(table(meta), held(tiles), held(extra), held(acc), *[held(x) for x in sources])


def solve_rows(base, mine, other, inverse, strike, wave):
    rows, width = mine.shape
    segments = base + lax.broadcasted_iota(jnp.int32, (rows, width), 0)
    incident = jnp.where(segments == strike, wave, jnp.float32(0.0))
    rhs = (incident - (mine + other)).astype(jnp.bfloat16)
    return jnp.dot(inverse, rhs, preferred_element_type=jnp.float32).astype(
        jnp.bfloat16
    )


def first_kernel(meta, mine, other, inverse, strike, wave, out):
    out[...] = solve_rows(
        meta[PLACE, 0], mine[...], other[...], inverse[...], strike[...], wave[0:1, :]
    )


def second_kernel(meta, first, mine, other, inverse, strike, wave, out):
    out[0] = first[...]
    out[1] = solve_rows(
        meta[PLACE, 0], mine[...], other[...], inverse[...], strike[...], wave[1:2, :]
    )


def pack_kernel(meta, own, other, out):
    half = own.shape[0] // 2

    @pl.when(meta[PLACE, 1] == 0)
    def _():
        out[:half] = own[:half]

    @pl.when(meta[PLACE, 1] == 1)
    def _():
        out[:half] = own[half:]

    out[half:] = other[...]


def pack(meta, own, other):
    rows, width = own.shape
    return pl.pallas_call(
        pack_kernel,
        out_shape=pltpu.VMEM((rows // 2 + rows, width), own.dtype),
        in_specs=[SMEM] + [VMEM] * 2,
        out_specs=VMEM,
        compiler_params=SMALL,
        name="pack",
    )(table(meta), held(own), held(other))


def fresh_kernel(turn, meta, tiles, source, acc, out):
    out[...] = acc[...]
    half = tiles.shape[2] // 2
    core = meta[PLACE, 1]

    def add(left, right):
        out[...] += jnp.dot(left, right, preferred_element_type=jnp.float32)

    @pl.loop(0, tiles.shape[0])
    def _(p):
        news = meta[NEWS, p]

        @pl.when(jnp.logical_and(news == 2 * turn, core == 0))
        def _():
            add(tiles[p, :, :half], source[:half])

        @pl.when(jnp.logical_and(news == 2 * turn, core == 1))
        def _():
            add(tiles[p, :, half:], source[:half])

        @pl.when(news == 2 * turn + 1)
        def _():
            add(tiles[p], source[half:])


def fresh_part(meta, tiles, source, turn, acc):
    return pl.pallas_call(
        functools.partial(fresh_kernel, turn),
        out_shape=pltpu.VMEM(acc.shape, acc.dtype),
        in_specs=[SMEM] + [VMEM] * 3,
        out_specs=VMEM,
        compiler_params=SMALL,
        name="fresh_part",
    )(table(meta), held(tiles), held(source), held(acc))


def per_device(tiles, history, self_inverse, pair_src, pair_delay, strike_seg, waveform):
    sites, groups = lax.axis_size("site"), lax.axis_size("structur")
    tiles, history, inverse = tiles[0], history[0], self_inverse[0]
    pairs, taps, rows, cols = tiles.shape
    width = history.shape[2]

    kinds = ("odd", "even", "own")
    key = {(k, t): n * groups + t for n, k in enumerate(kinds) for t in range(groups)}

    def send(x, *messages):
        pairs = [
            (2 * a + c, 2 * b + c)
            for c, m in enumerate(messages)
            for a, b in link_pairs(*m, sites, groups)
        ]
        return lax.ppermute(x, GRID_AXES, pairs)

    slots = [[-1] * (3 * groups) for _ in range(2)]
    for c in range(2):
        for t in range(groups):
            slots[c][key["own", t]] = t
            for n, kind in enumerate(("even", "odd")):
                slots[c][key[kind, t]] = groups + 2 * t + (n ^ c)

    planes, taps0, meta = pl.pallas_call(
        functools.partial(start_kernel, slots, sites, groups),
        out_shape=[
            pltpu.VMEM((taps + 1, rows, width), history.dtype),
            pltpu.VMEM((pairs, rows, cols), tiles.dtype),
            pltpu.SMEM((5, pairs), jnp.int32),
        ],
        in_specs=[ANY] * 4,
        out_specs=[VMEM, VMEM, SMEM],
        scratch_shapes=[
            pltpu.SMEM((1, pairs), jnp.int32),
            pltpu.SMEM((1, pairs), jnp.int32),
            pltpu.SemaphoreType.DMA((4,)),
        ],
        compiler_params=SMALL,
        name="start",
    )(far(pair_src), far(pair_delay), far(history), far(tiles))

    own = [planes] + [send(planes, *[("own", t)] * 2) for t in range(1, groups)]
    partners = []
    for x in own:
        partners.append(send(x, ("even", 0), ("odd", 0)))
        partners.append(send(x, ("odd", 0), ("even", 0)))
    extra = swap_cores(taps0)

    acc, newest = near_part(meta, tiles, extra, own + partners[:2])
    mine0, mine1 = relayed_part(meta, tiles, extra, acc, partners[2:], groups + 2)

    strike, inverse, wave = held(strike_seg[None, :]), held(inverse), held(waveform)
    current0 = pl.pallas_call(
        first_kernel,
        out_shape=pltpu.VMEM((rows, width), jnp.bfloat16),
        in_specs=[SMEM] + [VMEM] * 5,
        out_specs=VMEM,
        compiler_params=SMALL,
        name="first_currents",
    )(table(meta), held(mine0), held(swap_cores(mine0)), inverse, strike, wave)

    packed = pack(meta, current0, send(current0, ("even", 0), ("odd", 0)))
    passed = [send(packed, *[("own", t)] * 2) for t in range(1, groups)]
    for turn, block in enumerate([packed] + passed):
        mine1 = fresh_part(meta, newest, block, turn, mine1)

    currents = pl.pallas_call(
        second_kernel,
        out_shape=jax.ShapeDtypeStruct((2, rows, width), jnp.bfloat16),
        in_specs=[SMEM] + [VMEM] * 6,
        out_specs=VMEM,
        compiler_params=SMALL,
        name="second_currents",
    )(
        table(meta),
        held(current0),
        held(mine1),
        held(swap_cores(mine1)),
        inverse,
        strike,
        wave,
    )
    return currents[None]


def solution(mesh):
    in_specs = (
        P(("site", "structur"), None, "sub", None, None),
        P(("scenario", "site", "structur"), None, None, None),
        P(("site", "structur"), None, None),
        P(("site", "structur"), None),
        P(("site", "structur"), None),
        P("scenario"),
        P("scenario", None),
    )
    out_specs = P(("scenario", "site", "structur"), None, None, None)
    return jax.shard_map(
        per_device, mesh=mesh, in_specs=in_specs, out_specs=out_specs, check_vma=False
    )
```

time: 145 us -> 41.3 us (0.28)
  waiting for transfers between devices: 87.6 us -> 14.2 us
  local copies, waits for them, and re-layouts: 15.3 us -> 0.02 us
  between operations: 13.3 us -> 0.16 us
  matrix products: 11.6 us -> 0 us
  starting transfers between devices: 10.7 us -> 19.2 us
  Pallas kernels: 0 us -> 7.43 us
  blocking collectives: 4.94 us -> 0 us
  other arithmetic: 1.58 us -> 0 us
    psum x2 -> x0, waiting for transfers between devices: 36 us -> none  [tap_field(): return lax.psum(partial_field, 'sub')]
    all_gather x1 -> x0, waiting for transfers between devices: 27.1 us -> none  [spread_history(): grouped = lax.all_gather(history, 'structur', axis=0, tiled=True)]
    dot_general x4 -> x0, matrix products: 11.6 us -> none  [the longest x2 9.37 us: tap_field(): jnp.einsum('bpkij,bpkjs->bis', tiles, vectors, preferred_element_type=jnp...]
    ppermute x4 -> x10, waiting for transfers between devices: 23.8 us -> 14.2 us  [the longest x7 11.9 us: send(): return lax.ppermute(x, GRID_AXES, pairs)]
    gather x5 -> x0, local copies, waits for them, and re-layouts: 9.41 us -> none  [the longest x2 5.58 us: per_device(): older = nearby[slots[:, :, None], jnp.maximum(later, 0)]]
    ppermute x4 -> x10, starting transfers between devices: 10.6 us -> 19.2 us  [the longest x7 16.9 us: send(): return lax.ppermute(x, GRID_AXES, pairs)]
    pallas_call x0 -> x8, Pallas kernels: none -> 7.43 us  [the longest x1 2.61 us: near_part(): pl.pallas_call(functools.partial(near_kernel, len(sources)), out_shape=[p...]
    all_gather x1 -> x0, blocking collectives: 4.94 us -> none  [spread_newest(): grouped = lax.all_gather(newest, 'structur', axis=0, tiled=True)]
  transfers between devices with their start and end apart: 7 -> 10, of which waited for: 5 -> 6; matrix products, arithmetic and copies ran while one was open for 8% -> 0% of each run, Pallas kernels for 0% -> 8%
where the time goes in v2:
time: 41.3 us; the launch traced here: 41 us
  starting transfers between devices  19.2 us (46%)
  waiting for transfers between devices  14.2 us (34%)
  Pallas kernels  7.43 us (18%)
    ppermute x7, starting transfers between devices, send(): return lax.ppermute(x, GRID_AXES, pairs)  16.9 us
    ppermute x7, waiting for transfers between devices, send(): return lax.ppermute(x, GRID_AXES, pairs)  11.9 us
    pallas_call x1, Pallas kernels, near_part(): pl.pallas_call(functools.partial(near_kernel, len(sources)), out_shape=[p...  2.61 us
    ppermute x3, waiting for transfers between devices, swap_cores(): return lax.ppermute(x, 'sub', [(0, 1), (1, 0)])  2.32 us
    ppermute x3, starting transfers between devices, swap_cores(): return lax.ppermute(x, 'sub', [(0, 1), (1, 0)])  2.27 us
    pallas_call x1, Pallas kernels, per_device(): pl.pallas_call(functools.partial(start_kernel, slots, sites, groups), out...  1.51 us
    pallas_call x2, Pallas kernels, fresh_part(): pl.pallas_call(functools.partial(fresh_kernel, turn), out_shape=pltpu.VME...  1.19 us
    pallas_call x1, Pallas kernels, relayed_part(): pl.pallas_call(functools.partial(relayed_kernel, first, len(sources)), ou...  1.08 us
  transfers between devices with their start and end apart: 10, of which 6 were waited for; matrix products, arithmetic and copies ran while one was open for 0% of the time, Pallas kernels for 8%

profile of v2, /device:TPU:0, one launch (start us, length us, event | category | flops | bytes accessed | tf_op | source)
XLA Modules:
  0.0 41.0 jit_solution(15336655318703781625)
XLA Ops:
  0.0 1.5 %start.1 = (bf16[5,256,128]{2,1,0:T(8,128)(2,1)S(1)}, bf16[8,256,256]{2,1,0:T(8,128)(2,1)S(1)}, s32[5,8]{1,0:T(8,128)S(4)}) custom-call(s32[1,8]{1,0:T(1,128)} %refs_0_.1, s32[1,8]{1,0:T(1,128)} %refs_1_.1, bf16[9,256,128]{2,1,0:T(8,128)(2,1)} %bitcast.12, bf16[8,4,256,256]{3,2,1,0:T(8,128)(2,1)} %bitcast.5), custom_call_target="tpu_custom_call" | custom-call | tf_op jit(solution)/shard_map/start/pallas_call | solution.py:334
  1.5 0.5 %collective-permute-start = (bf16[8,256,256]{2,1,0:T(8,128)(2,1)S(1)}, bf16[8,256,256]{2,1,0:T(8,128)(2,1)S(1)}, u32[]{:S(2)}, u32[]{:S(2)}) collective-permute-start(bf16[8,256,256]{2,1,0:T(8,128)(2,1)S(1)} %get-tuple-element.13), channel_id=1, source_target_pairs={{0,1},{1,0},{2,3},{3,2},{4,5},{5,4},{6,7},{7,6},{8,9},{9,8},{10,11... | collective-permute-start | bytes 3145736 | tf_op jit(solution)/shard_map/ppermute | solution.py:51
  2.0 2.6 %collective-permute-start.1 = (bf16[5,256,128]{2,1,0:T(8,128)(2,1)S(1)}, bf16[5,256,128]{2,1,0:T(8,128)(2,1)S(1)}, u32[]{:S(2)}, u32[]{:S(2)}) collective-permute-start(bf16[5,256,128]{2,1,0:T(8,128)(2,1)S(1)} %get-tuple-element.14.refs_0_), channel_id=1, source_target_pairs={{0,2},{2,0},{4,6},{6,4},{8,10},{10,8},{12,14},{14,12},{1,3},{3,1},... | collective-permute-start | bytes 983048 | tf_op jit(solution)/shard_map/ppermute | solution.py:325
  4.6 3.5 %collective-permute-start.2 = (bf16[5,256,128]{2,1,0:T(8,128)(2,1)S(1)}, bf16[5,256,128]{2,1,0:T(8,128)(2,1)S(1)}, u32[]{:S(2)}, u32[]{:S(2)}) collective-permute-start(bf16[5,256,128]{2,1,0:T(8,128)(2,1)S(1)} %get-tuple-element.14.refs_0_), channel_id=1, source_target_pairs={{0,4},{2,6},{4,0},{6,2},{8,12},{10,14},{12,8},{14,10},{5,9},{7,11}... | collective-permute-start | bytes 983048 | tf_op jit(solution)/shard_map/ppermute | solution.py:325
  8.1 0.7 %collective-permute-start.3 = (bf16[5,256,128]{2,1,0:T(8,128)(2,1)S(1)}, bf16[5,256,128]{2,1,0:T(8,128)(2,1)S(1)}, u32[]{:S(2)}, u32[]{:S(2)}) collective-permute-start(bf16[5,256,128]{2,1,0:T(8,128)(2,1)S(1)} %get-tuple-element.14.refs_0_), channel_id=1, source_target_pairs={{4,8},{6,10},{8,4},{10,6},{1,5},{3,7},{5,1},{7,3},{9,13},{11,15},{... | collective-permute-start | bytes 983048 | tf_op jit(solution)/shard_map/ppermute | solution.py:325
  8.8 4.1 %collective-permute-done.1.refs_1_ = bf16[5,256,128]{2,1,0:T(8,128)(2,1)S(1)} collective-permute-done((bf16[5,256,128]{2,1,0:T(8,128)(2,1)S(1)}, bf16[5,256,128]{2,1,0:T(8,128)(2,1)S(1)}, u32[]{:S(2)}, u32[]{:S(2)}) %collective-permute-start.1) | collective-permute-done | bytes 327712 | tf_op jit(solution)/shard_map/ppermute | solution.py:325
  12.9 3.7 %collective-permute-start.4 = (bf16[5,256,128]{2,1,0:T(8,128)(2,1)S(1)}, bf16[5,256,128]{2,1,0:T(8,128)(2,1)S(1)}, u32[]{:S(2)}, u32[]{:S(2)}) collective-permute-start(bf16[5,256,128]{2,1,0:T(8,128)(2,1)S(1)} %collective-permute-done.1.refs_1_), channel_id=1, source_target_pairs={{0,4},{2,6},{4,0},{6,2},{8,12},{10,14},{12,8},{14,10},{5,9},{7,11}... | collective-permute-start | bytes 983048 | tf_op jit(solution)/shard_map/ppermute | solution.py:325
  16.7 0.7 %collective-permute-start.5 = (bf16[5,256,128]{2,1,0:T(8,128)(2,1)S(1)}, bf16[5,256,128]{2,1,0:T(8,128)(2,1)S(1)}, u32[]{:S(2)}, u32[]{:S(2)}) collective-permute-start(bf16[5,256,128]{2,1,0:T(8,128)(2,1)S(1)} %collective-permute-done.1.refs_1_), channel_id=1, source_target_pairs={{4,8},{6,10},{8,4},{10,6},{1,5},{3,7},{5,1},{7,3},{9,13},{11,15},{... | collective-permute-start | bytes 983048 | tf_op jit(solution)/shard_map/ppermute | solution.py:325
  17.3 0.0 collective-permute-done.2.refs_2_
  17.4 0.0 collective-permute-done.3.refs_3_
  17.4 0.0 collective-permute-done.extra
  17.4 0.0 copy-done
  17.4 2.6 %near_part.1 = (f32[256,256]{1,0:T(8,128)S(1)}, bf16[8,256,256]{2,1,0:T(8,128)(2,1)S(1)}) custom-call(s32[5,8]{1,0:T(8,128)S(4)} %get-tuple-element.12.meta, bf16[8,4,256,256]{3,2,1,0:T(8,128)(2,1)S(1)} %bitcast.6, bf16[8,256,256]{2,1,0:T(8,128)(2,1)S(1)} %collective-permute-done.extra, bf16[5,256,128]{2,1,0:T(8,128)(2,1)S(1)} %get-tuple-element.14.refs_0_, ...), custom_call_target="tpu_custom_call" | custom-call | tf_op jit(solution)/shard_map/near_part/pallas_call | solution.py:142
  20.0 0.0 copy-start.1
  20.0 0.0 copy-start.2
  20.0 0.0 copy-start.3
  20.0 3.3 %collective-permute-done.4.refs_0_ = bf16[5,256,128]{2,1,0:T(8,128)(2,1)S(1)} collective-permute-done((bf16[5,256,128]{2,1,0:T(8,128)(2,1)S(1)}, bf16[5,256,128]{2,1,0:T(8,128)(2,1)S(1)}, u32[]{:S(2)}, u32[]{:S(2)}) %collective-permute-start.4) | collective-permute-done | bytes 327712 | tf_op jit(solution)/shard_map/ppermute | solution.py:325
  23.3 0.0 collective-permute-done.5.refs_1_
  23.3 1.1 %relayed_part.1 = (f32[256,128]{1,0:T(8,128)S(1)}, f32[256,128]{1,0:T(8,128)S(1)}) custom-call(s32[5,8]{1,0:T(8,128)S(4)} %get-tuple-element.12.meta, bf16[8,4,256,256]{3,2,1,0:T(8,128)(2,1)S(1)} %bitcast.7, bf16[8,256,256]{2,1,0:T(8,128)(2,1)S(1)} %collective-permute-done.extra, f32[256,256]{1,0:T(8,128)S(1)} %get-tuple-element.15.acc, ...), custom_call_target="tpu_custom_call" | custom-call | tf_op jit(solution)/shard_map/relayed_part/pallas_call | solution.py:211
  24.4 1.7 %collective-permute-start.6 = (f32[256,128]{1,0:T(8,128)S(1)}, f32[256,128]{1,0:T(8,128)S(1)}, u32[]{:S(2)}, u32[]{:S(2)}) collective-permute-start(f32[256,128]{1,0:T(8,128)S(1)} %get-tuple-element.16.mine), channel_id=1, source_target_pairs={{0,1},{1,0},{2,3},{3,2},{4,5},{5,4},{6,7},{7,6},{8,9},{9,8},{10,11... | collective-permute-start | bytes 393224 | tf_op jit(solution)/shard_map/ppermute | solution.py:51
  26.1 1.0 %collective-permute-done.6.other = f32[256,128]{1,0:T(8,128)S(1)} collective-permute-done((f32[256,128]{1,0:T(8,128)S(1)}, f32[256,128]{1,0:T(8,128)S(1)}, u32[]{:S(2)}, u32[]{:S(2)}) %collective-permute-start.6) | collective-permute-done | bytes 131104 | tf_op jit(solution)/shard_map/ppermute | solution.py:51
  27.1 0.0 copy-done.3
  27.1 0.2 first_currents.1.own.first
  27.3 4.1 %collective-permute-start.7 = (bf16[256,128]{1,0:T(8,128)(2,1)S(1)}, bf16[256,128]{1,0:T(8,128)(2,1)S(1)}, u32[]{:S(2)}, u32[]{:S(2)}) collective-permute-start(bf16[256,128]{1,0:T(8,128)(2,1)S(1)} %first_currents.1.own.first), channel_id=1, source_target_pairs={{0,4},{2,6},{4,0},{6,2},{8,12},{10,14},{12,8},{14,10},{5,9},{7,11}... | collective-permute-start | bytes 196616 | tf_op jit(solution)/shard_map/ppermute | solution.py:325
  31.4 2.2 %collective-permute-done.7.other = bf16[256,128]{1,0:T(8,128)(2,1)S(1)} collective-permute-done((bf16[256,128]{1,0:T(8,128)(2,1)S(1)}, bf16[256,128]{1,0:T(8,128)(2,1)S(1)}, u32[]{:S(2)}, u32[]{:S(2)}) %collective-permute-start.7) | collective-permute-done | bytes 65568 | tf_op jit(solution)/shard_map/ppermute | solution.py:325
  33.6 1.6 %collective-permute-start.8 = (bf16[384,128]{1,0:T(8,128)(2,1)S(1)}, bf16[384,128]{1,0:T(8,128)(2,1)S(1)}, u32[]{:S(2)}, u32[]{:S(2)}) collective-permute-start(bf16[384,128]{1,0:T(8,128)(2,1)S(1)} %pack.1.source), channel_id=1, source_target_pairs={{0,2},{2,0},{4,6},{6,4},{8,10},{10,8},{12,14},{14,12},{1,3},{3,1},... | collective-permute-start | bytes 294920 | tf_op jit(solution)/shard_map/ppermute | solution.py:325
  35.3 0.8 %fresh_part.2.acc = f32[256,128]{1,0:T(8,128)S(1)} custom-call(s32[5,8]{1,0:T(8,128)S(4)} %get-tuple-element.12.meta, bf16[8,256,256]{2,1,0:T(8,128)(2,1)S(1)} %get-tuple-element.17.tiles, bf16[384,128]{1,0:T(8,128)(2,1)S(1)} %pack.1.source, f32[256,128]{1,0:T(8,128)S(1)} %get-tuple-element.18.acc), custom_call_target="tpu_custom_call" | custom-call | tf_op jit(solution)/shard_map/fresh_part/pallas_call | solution.py:300
  36.1 2.2 %collective-permute-done.8.source = bf16[384,128]{1,0:T(8,128)(2,1)S(1)} collective-permute-done((bf16[384,128]{1,0:T(8,128)(2,1)S(1)}, bf16[384,128]{1,0:T(8,128)(2,1)S(1)}, u32[]{:S(2)}, u32[]{:S(2)}) %collective-permute-start.8) | collective-permute-done | bytes 98336 | tf_op jit(solution)/shard_map/ppermute | solution.py:325
  38.3 0.4 fresh_part.3.mine
  38.7 0.1 collective-permute-start.9
  38.8 1.3 %collective-permute-done.9.other = f32[256,128]{1,0:T(8,128)S(1)} collective-permute-done((f32[256,128]{1,0:T(8,128)S(1)}, f32[256,128]{1,0:T(8,128)S(1)}, u32[]{:S(2)}, u32[]{:S(2)}) %collective-permute-start.9) | collective-permute-done | bytes 131104 | tf_op jit(solution)/shard_map/ppermute | solution.py:51
  40.1 0.9 %second_currents.1 = bf16[2,256,128]{2,1,0:T(8,128)(2,1)} custom-call(s32[5,8]{1,0:T(8,128)S(4)} %get-tuple-element.12.meta, bf16[256,128]{1,0:T(8,128)(2,1)S(1)} %first_currents.1.own.first, f32[256,128]{1,0:T(8,128)S(1)} %fresh_part.3.mine, f32[256,128]{1,0:T(8,128)S(1)} %collective-permute-done.9.other, bf16[256,256]{1,0:T(8,128)(2,1)S(1)} %bitcast.9, ...), custom_call_target="tpu_custom_call" | custom-call | tf_op jit(solution)/shard_map/second_currents/pallas_call | solution.py:377
  (4 shorter events, 0.0 us)
Async XLA Ops:
  0.0 17.4 %copy-start = (bf16[1,8,4,256,256]{4,3,2,1,0:T(8,128)(2,1)S(1)}, bf16[1,8,4,256,256]{4,3,2,1,0:T(8,128)(2,1)}, u32[]{:S(2)}) copy-start(bf16[1,8,4,256,256]{4,3,2,1,0:T(8,128)(2,1)} %param.7) | copy-start | bytes 12582916
  1.5 15.8 %collective-permute-start = (bf16[8,256,256]{2,1,0:T(8,128)(2,1)S(1)}, bf16[8,256,256]{2,1,0:T(8,128)(2,1)S(1)}, u32[]{:S(2)}, u32[]{:S(2)}) collective-permute-start(bf16[8,256,256]{2,1,0:T(8,128)(2,1)S(1)} %get-tuple-element.13), channel_id=1, source_target_pairs={{0,1},{1,0},{2,3},{3,2},{4,5},{5,4},{6,7},{7,6},{8,9},{9,8},{10,11... | collective-permute-start | bytes 3145736 | tf_op jit(solution)/shard_map/ppermute | solution.py:51
  2.0 10.9 %collective-permute-start.1 = (bf16[5,256,128]{2,1,0:T(8,128)(2,1)S(1)}, bf16[5,256,128]{2,1,0:T(8,128)(2,1)S(1)}, u32[]{:S(2)}, u32[]{:S(2)}) collective-permute-start(bf16[5,256,128]{2,1,0:T(8,128)(2,1)S(1)} %get-tuple-element.14.refs_0_), channel_id=1, source_target_pairs={{0,2},{2,0},{4,6},{6,4},{8,10},{10,8},{12,14},{14,12},{1,3},{3,1},... | collective-permute-start | bytes 983048 | tf_op jit(solution)/shard_map/ppermute | solution.py:325
  4.6 12.7 %collective-permute-start.2 = (bf16[5,256,128]{2,1,0:T(8,128)(2,1)S(1)}, bf16[5,256,128]{2,1,0:T(8,128)(2,1)S(1)}, u32[]{:S(2)}, u32[]{:S(2)}) collective-permute-start(bf16[5,256,128]{2,1,0:T(8,128)(2,1)S(1)} %get-tuple-element.14.refs_0_), channel_id=1, source_target_pairs={{0,4},{2,6},{4,0},{6,2},{8,12},{10,14},{12,8},{14,10},{5,9},{7,11}... | collective-permute-start | bytes 983048 | tf_op jit(solution)/shard_map/ppermute | solution.py:325
  8.1 9.3 %collective-permute-start.3 = (bf16[5,256,128]{2,1,0:T(8,128)(2,1)S(1)}, bf16[5,256,128]{2,1,0:T(8,128)(2,1)S(1)}, u32[]{:S(2)}, u32[]{:S(2)}) collective-permute-start(bf16[5,256,128]{2,1,0:T(8,128)(2,1)S(1)} %get-tuple-element.14.refs_0_), channel_id=1, source_target_pairs={{4,8},{6,10},{8,4},{10,6},{1,5},{3,7},{5,1},{7,3},{9,13},{11,15},{... | collective-permute-start | bytes 983048 | tf_op jit(solution)/shard_map/ppermute | solution.py:325
  12.9 10.4 %collective-permute-start.4 = (bf16[5,256,128]{2,1,0:T(8,128)(2,1)S(1)}, bf16[5,256,128]{2,1,0:T(8,128)(2,1)S(1)}, u32[]{:S(2)}, u32[]{:S(2)}) collective-permute-start(bf16[5,256,128]{2,1,0:T(8,128)(2,1)S(1)} %collective-permute-done.1.refs_1_), channel_id=1, source_target_pairs={{0,4},{2,6},{4,0},{6,2},{8,12},{10,14},{12,8},{14,10},{5,9},{7,11}... | collective-permute-start | bytes 983048 | tf_op jit(solution)/shard_map/ppermute | solution.py:325
  16.7 6.6 %collective-permute-start.5 = (bf16[5,256,128]{2,1,0:T(8,128)(2,1)S(1)}, bf16[5,256,128]{2,1,0:T(8,128)(2,1)S(1)}, u32[]{:S(2)}, u32[]{:S(2)}) collective-permute-start(bf16[5,256,128]{2,1,0:T(8,128)(2,1)S(1)} %collective-permute-done.1.refs_1_), channel_id=1, source_target_pairs={{4,8},{6,10},{8,4},{10,6},{1,5},{3,7},{5,1},{7,3},{9,13},{11,15},{... | collective-permute-start | bytes 983048 | tf_op jit(solution)/shard_map/ppermute | solution.py:325
  20.0 7.1 %copy-start.1 = (bf16[1,256,256]{2,1,0:T(8,128)(2,1)S(1)}, bf16[1,256,256]{2,1,0:T(8,128)(2,1)}, u32[]{:S(2)}) copy-start(bf16[1,256,256]{2,1,0:T(8,128)(2,1)} %param.9) | copy-start | bytes 393220
  20.0 7.0 %copy-start.2 = (f32[2,128]{1,0:T(2,128)S(1)}, f32[2,128]{1,0:T(2,128)}, u32[]{:S(2)}) copy-start(f32[2,128]{1,0:T(2,128)} %wave.3) | copy-start | bytes 3076
  20.0 7.0 %copy-start.3 = (s32[128]{0:T(128)S(1)}, s32[128]{0:T(128)}, u32[]{:S(2)}) copy-start(s32[128]{0:T(128)} %param.12) | copy-start | bytes 1540
  24.4 2.7 %collective-permute-start.6 = (f32[256,128]{1,0:T(8,128)S(1)}, f32[256,128]{1,0:T(8,128)S(1)}, u32[]{:S(2)}, u32[]{:S(2)}) collective-permute-start(f32[256,128]{1,0:T(8,128)S(1)} %get-tuple-element.16.mine), channel_id=1, source_target_pairs={{0,1},{1,0},{2,3},{3,2},{4,5},{5,4},{6,7},{7,6},{8,9},{9,8},{10,11... | collective-permute-start | bytes 393224 | tf_op jit(solution)/shard_map/ppermute | solution.py:51
  27.3 6.4 %collective-permute-start.7 = (bf16[256,128]{1,0:T(8,128)(2,1)S(1)}, bf16[256,128]{1,0:T(8,128)(2,1)S(1)}, u32[]{:S(2)}, u32[]{:S(2)}) collective-permute-start(bf16[256,128]{1,0:T(8,128)(2,1)S(1)} %first_currents.1.own.first), channel_id=1, source_target_pairs={{0,4},{2,6},{4,0},{6,2},{8,12},{10,14},{12,8},{14,10},{5,9},{7,11}... | collective-permute-start | bytes 196616 | tf_op jit(solution)/shard_map/ppermute | solution.py:325
  33.6 4.7 %collective-permute-start.8 = (bf16[384,128]{1,0:T(8,128)(2,1)S(1)}, bf16[384,128]{1,0:T(8,128)(2,1)S(1)}, u32[]{:S(2)}, u32[]{:S(2)}) collective-permute-start(bf16[384,128]{1,0:T(8,128)(2,1)S(1)} %pack.1.source), channel_id=1, source_target_pairs={{0,2},{2,0},{4,6},{6,4},{8,10},{10,8},{12,14},{14,12},{1,3},{3,1},... | collective-permute-start | bytes 294920 | tf_op jit(solution)/shard_map/ppermute | solution.py:325
  38.7 1.4 %collective-permute-start.9 = (f32[256,128]{1,0:T(8,128)S(1)}, f32[256,128]{1,0:T(8,128)S(1)}, u32[]{:S(2)}, u32[]{:S(2)}) collective-permute-start(f32[256,128]{1,0:T(8,128)S(1)} %fresh_part.3.mine), channel_id=1, source_target_pairs={{0,1},{1,0},{2,3},{3,2},{4,5},{5,4},{6,7},{7,6},{8,9},{9,8},{10,11... | collective-permute-start | bytes 393224 | tf_op jit(solution)/shard_map/ppermute | solution.py:51

commit v3 on v2

--- a/solution.py
+++ b/solution.py
@@ -8,6 +8,7 @@
 from jax.sharding import PartitionSpec as P
 
 GRID_AXES = ("site", "structur", "sub")
+ALL_AXES = ("scenario",) + GRID_AXES
 SMEM = pl.BlockSpec(memory_space=pltpu.SMEM)
 VMEM = pl.BlockSpec(memory_space=pltpu.VMEM)
 ANY = pl.BlockSpec(memory_space=pl.ANY)
@@ -317,12 +318,19 @@
     key = {(k, t): n * groups + t for n, k in enumerate(kinds) for t in range(groups)}
 
     def send(x, *messages):
-        pairs = [
-            (2 * a + c, 2 * b + c)
-            for c, m in enumerate(messages)
-            for a, b in link_pairs(*m, sites, groups)
-        ]
-        return lax.ppermute(x, GRID_AXES, pairs)
+        scenarios, grid = lax.axis_size("scenario"), sites * groups * 2
+        pairs = []
+        for scenario in range(scenarios):
+            twin = scenario ^ 1
+            for c, m in enumerate(messages):
+                moves = dict(link_pairs(*m, sites, groups))
+                for a in range(sites * groups):
+                    source = scenario * grid + 2 * a + c
+                    if a in moves:
+                        pairs.append((source, scenario * grid + 2 * moves[a] + c))
+                    elif twin < scenarios:
+                        pairs.append((source, twin * grid + 2 * a + c))
+        return lax.ppermute(x, ALL_AXES, pairs)
 
     slots = [[-1] * (3 * groups) for _ in range(2)]
     for c in range(2):

time: 41.3 us -> 38 us (0.920)
  starting transfers between devices: 19.2 us -> 13.3 us
  waiting for transfers between devices: 14.2 us -> 17.1 us
    ppermute x7, starting transfers between devices: 16.9 us -> 12.7 us  [send(): return lax.ppermute(x, ALL_AXES, pairs)]
    ppermute x7, waiting for transfers between devices: 11.9 us -> 14.4 us  [send(): return lax.ppermute(x, ALL_AXES, pairs)]
    ppermute x3, starting transfers between devices: 2.27 us -> 0.66 us  [swap_cores(): return lax.ppermute(x, 'sub', [(0, 1), (1, 0)])]
where the time goes in v3:
time: 38 us; the launch traced here: 37.9 us
  waiting for transfers between devices  17.1 us (45%)
  starting transfers between devices  13.3 us (35%)
  Pallas kernels  7.33 us (19%)
    ppermute x7, waiting for transfers between devices, send(): return lax.ppermute(x, ALL_AXES, pairs)  14.4 us
    ppermute x7, starting transfers between devices, send(): return lax.ppermute(x, ALL_AXES, pairs)  12.7 us
    ppermute x3, waiting for transfers between devices, swap_cores(): return lax.ppermute(x, 'sub', [(0, 1), (1, 0)])  2.67 us
    pallas_call x1, Pallas kernels, near_part(): pl.pallas_call(functools.partial(near_kernel, len(sources)), out_shape=[p...  2.46 us
    pallas_call x1, Pallas kernels, per_device(): pl.pallas_call(functools.partial(start_kernel, slots, sites, groups), out...  1.51 us
    pallas_call x2, Pallas kernels, fresh_part(): pl.pallas_call(functools.partial(fresh_kernel, turn), out_shape=pltpu.VME...  1.24 us
    pallas_call x1, Pallas kernels, relayed_part(): pl.pallas_call(functools.partial(relayed_kernel, first, len(sources)), ou...  1.08 us
    pallas_call x1, Pallas kernels, per_device(): pl.pallas_call(second_kernel, out_shape=jax.ShapeDtypeStruct((2, rows, wi...  0.85 us
  transfers between devices with their start and end apart: 10, of which 6 were waited for; matrix products, arithmetic and copies ran while one was open for 0% of the time, Pallas kernels for 8%

profile of v3, /device:TPU:0, one launch (start us, length us, event | category | flops | bytes accessed | tf_op | source)
XLA Modules:
  0.0 37.9 jit_solution(7178265254648569981)
XLA Ops:
  0.0 1.5 %start.1 = (bf16[5,256,128]{2,1,0:T(8,128)(2,1)S(1)}, bf16[8,256,256]{2,1,0:T(8,128)(2,1)S(1)}, s32[5,8]{1,0:T(8,128)S(4)}) custom-call(s32[1,8]{1,0:T(1,128)} %refs_0_.1, s32[1,8]{1,0:T(1,128)} %refs_1_.1, bf16[9,256,128]{2,1,0:T(8,128)(2,1)} %bitcast.12, bf16[8,4,256,256]{3,2,1,0:T(8,128)(2,1)} %bitcast.5), custom_call_target="tpu_custom_call" | custom-call | tf_op jit(solution)/shard_map/start/pallas_call | solution.py:342
  1.5 0.5 %collective-permute-start = (bf16[8,256,256]{2,1,0:T(8,128)(2,1)S(1)}, bf16[8,256,256]{2,1,0:T(8,128)(2,1)S(1)}, u32[]{:S(2)}, u32[]{:S(2)}) collective-permute-start(bf16[8,256,256]{2,1,0:T(8,128)(2,1)S(1)} %get-tuple-element.13), channel_id=1, source_target_pairs={{0,1},{1,0},{2,3},{3,2},{4,5},{5,4},{6,7},{7,6},{8,9},{9,8},{10,11... | collective-permute-start | bytes 3145736 | tf_op jit(solution)/shard_map/ppermute | solution.py:52
  2.0 2.6 %collective-permute-start.1 = (bf16[5,256,128]{2,1,0:T(8,128)(2,1)S(1)}, bf16[5,256,128]{2,1,0:T(8,128)(2,1)S(1)}, u32[]{:S(2)}, u32[]{:S(2)}) collective-permute-start(bf16[5,256,128]{2,1,0:T(8,128)(2,1)S(1)} %get-tuple-element.14.refs_0_), channel_id=1, source_target_pairs={{0,2},{2,0},{4,6},{6,4},{8,10},{10,8},{12,14},{14,12},{1,3},{3,1},... | collective-permute-start | bytes 983048 | tf_op jit(solution)/shard_map/ppermute | solution.py:333
  4.6 1.6 %collective-permute-start.2 = (bf16[5,256,128]{2,1,0:T(8,128)(2,1)S(1)}, bf16[5,256,128]{2,1,0:T(8,128)(2,1)S(1)}, u32[]{:S(2)}, u32[]{:S(2)}) collective-permute-start(bf16[5,256,128]{2,1,0:T(8,128)(2,1)S(1)} %get-tuple-element.14.refs_0_), channel_id=1, source_target_pairs={{0,4},{2,6},{4,0},{6,2},{8,12},{10,14},{12,8},{14,10},{1,17},{3,19... | collective-permute-start | bytes 983048 | tf_op jit(solution)/shard_map/ppermute | solution.py:333
  6.2 1.5 %collective-permute-start.3 = (bf16[5,256,128]{2,1,0:T(8,128)(2,1)S(1)}, bf16[5,256,128]{2,1,0:T(8,128)(2,1)S(1)}, u32[]{:S(2)}, u32[]{:S(2)}) collective-permute-start(bf16[5,256,128]{2,1,0:T(8,128)(2,1)S(1)} %get-tuple-element.14.refs_0_), channel_id=1, source_target_pairs={{0,16},{2,18},{4,8},{6,10},{8,4},{10,6},{12,28},{14,30},{1,5},{3,7... | collective-permute-start | bytes 983048 | tf_op jit(solution)/shard_map/ppermute | solution.py:333
  7.7 5.2 %collective-permute-done.1.refs_1_ = bf16[5,256,128]{2,1,0:T(8,128)(2,1)S(1)} collective-permute-done((bf16[5,256,128]{2,1,0:T(8,128)(2,1)S(1)}, bf16[5,256,128]{2,1,0:T(8,128)(2,1)S(1)}, u32[]{:S(2)}, u32[]{:S(2)}) %collective-permute-start.1) | collective-permute-done | bytes 327712 | tf_op jit(solution)/shard_map/ppermute | solution.py:333
  12.9 1.8 %collective-permute-start.4 = (bf16[5,256,128]{2,1,0:T(8,128)(2,1)S(1)}, bf16[5,256,128]{2,1,0:T(8,128)(2,1)S(1)}, u32[]{:S(2)}, u32[]{:S(2)}) collective-permute-start(bf16[5,256,128]{2,1,0:T(8,128)(2,1)S(1)} %collective-permute-done.1.refs_1_), channel_id=1, source_target_pairs={{0,4},{2,6},{4,0},{6,2},{8,12},{10,14},{12,8},{14,10},{1,17},{3,19... | collective-permute-start | bytes 983048 | tf_op jit(solution)/shard_map/ppermute | solution.py:333
  14.7 1.5 %collective-permute-start.5 = (bf16[5,256,128]{2,1,0:T(8,128)(2,1)S(1)}, bf16[5,256,128]{2,1,0:T(8,128)(2,1)S(1)}, u32[]{:S(2)}, u32[]{:S(2)}) collective-permute-start(bf16[5,256,128]{2,1,0:T(8,128)(2,1)S(1)} %collective-permute-done.1.refs_1_), channel_id=1, source_target_pairs={{0,16},{2,18},{4,8},{6,10},{8,4},{10,6},{12,28},{14,30},{1,5},{3,7... | collective-permute-start | bytes 983048 | tf_op jit(solution)/shard_map/ppermute | solution.py:333
  16.3 0.0 collective-permute-done.2.refs_2_
  16.3 0.0 collective-permute-done.3.refs_3_
  16.3 0.0 collective-permute-done.extra
  16.3 2.5 %near_part.1 = (f32[256,256]{1,0:T(8,128)S(1)}, bf16[8,256,256]{2,1,0:T(8,128)(2,1)S(1)}) custom-call(s32[5,8]{1,0:T(8,128)S(4)} %get-tuple-element.12.meta, bf16[8,4,256,256]{3,2,1,0:T(8,128)(2,1)S(1)} %bitcast.6, bf16[8,256,256]{2,1,0:T(8,128)(2,1)S(1)} %collective-permute-done.extra, bf16[5,256,128]{2,1,0:T(8,128)(2,1)S(1)} %get-tuple-element.14.refs_0_, ...), custom_call_target="tpu_custom_call" | custom-call | tf_op jit(solution)/shard_map/near_part/pallas_call | solution.py:143
  18.8 0.0 copy-start.1
  18.8 0.0 copy-start.2
  18.8 0.0 copy-start.3
  18.8 4.5 %collective-permute-done.4.refs_0_ = bf16[5,256,128]{2,1,0:T(8,128)(2,1)S(1)} collective-permute-done((bf16[5,256,128]{2,1,0:T(8,128)(2,1)S(1)}, bf16[5,256,128]{2,1,0:T(8,128)(2,1)S(1)}, u32[]{:S(2)}, u32[]{:S(2)}) %collective-permute-start.4) | collective-permute-done | bytes 327712 | tf_op jit(solution)/shard_map/ppermute | solution.py:333
  23.3 0.0 collective-permute-done.5.refs_1_
  23.3 1.1 %relayed_part.1 = (f32[256,128]{1,0:T(8,128)S(1)}, f32[256,128]{1,0:T(8,128)S(1)}) custom-call(s32[5,8]{1,0:T(8,128)S(4)} %get-tuple-element.12.meta, bf16[8,4,256,256]{3,2,1,0:T(8,128)(2,1)S(1)} %bitcast.7, bf16[8,256,256]{2,1,0:T(8,128)(2,1)S(1)} %collective-permute-done.extra, f32[256,256]{1,0:T(8,128)S(1)} %get-tuple-element.15.acc, ...), custom_call_target="tpu_custom_call" | custom-call | tf_op jit(solution)/shard_map/relayed_part/pallas_call | solution.py:212
  24.4 0.1 collective-permute-start.6
  24.5 1.3 %collective-permute-done.6.other = f32[256,128]{1,0:T(8,128)S(1)} collective-permute-done((f32[256,128]{1,0:T(8,128)S(1)}, f32[256,128]{1,0:T(8,128)S(1)}, u32[]{:S(2)}, u32[]{:S(2)}) %collective-permute-start.6) | collective-permute-done | bytes 131104 | tf_op jit(solution)/shard_map/ppermute | solution.py:52
  25.8 0.0 copy-done.1
  25.8 0.0 copy-done.3
  25.8 0.2 first_currents.1.own.first
  26.0 2.1 %collective-permute-start.7 = (bf16[256,128]{1,0:T(8,128)(2,1)S(1)}, bf16[256,128]{1,0:T(8,128)(2,1)S(1)}, u32[]{:S(2)}, u32[]{:S(2)}) collective-permute-start(bf16[256,128]{1,0:T(8,128)(2,1)S(1)} %first_currents.1.own.first), channel_id=1, source_target_pairs={{0,4},{2,6},{4,0},{6,2},{8,12},{10,14},{12,8},{14,10},{1,17},{3,19... | collective-permute-start | bytes 196616 | tf_op jit(solution)/shard_map/ppermute | solution.py:333
  28.1 2.2 %collective-permute-done.7.other = bf16[256,128]{1,0:T(8,128)(2,1)S(1)} collective-permute-done((bf16[256,128]{1,0:T(8,128)(2,1)S(1)}, bf16[256,128]{1,0:T(8,128)(2,1)S(1)}, u32[]{:S(2)}, u32[]{:S(2)}) %collective-permute-start.7) | collective-permute-done | bytes 65568 | tf_op jit(solution)/shard_map/ppermute | solution.py:333
  30.3 1.6 %collective-permute-start.8 = (bf16[384,128]{1,0:T(8,128)(2,1)S(1)}, bf16[384,128]{1,0:T(8,128)(2,1)S(1)}, u32[]{:S(2)}, u32[]{:S(2)}) collective-permute-start(bf16[384,128]{1,0:T(8,128)(2,1)S(1)} %pack.1.source), channel_id=1, source_target_pairs={{0,2},{2,0},{4,6},{6,4},{8,10},{10,8},{12,14},{14,12},{1,3},{3,1},... | collective-permute-start | bytes 294920 | tf_op jit(solution)/shard_map/ppermute | solution.py:333
  31.9 0.7 %fresh_part.2.acc = f32[256,128]{1,0:T(8,128)S(1)} custom-call(s32[5,8]{1,0:T(8,128)S(4)} %get-tuple-element.12.meta, bf16[8,256,256]{2,1,0:T(8,128)(2,1)S(1)} %get-tuple-element.17.tiles, bf16[384,128]{1,0:T(8,128)(2,1)S(1)} %pack.1.source, f32[256,128]{1,0:T(8,128)S(1)} %get-tuple-element.18.acc), custom_call_target="tpu_custom_call" | custom-call | tf_op jit(solution)/shard_map/fresh_part/pallas_call | solution.py:301
  32.6 2.4 %collective-permute-done.8.source = bf16[384,128]{1,0:T(8,128)(2,1)S(1)} collective-permute-done((bf16[384,128]{1,0:T(8,128)(2,1)S(1)}, bf16[384,128]{1,0:T(8,128)(2,1)S(1)}, u32[]{:S(2)}, u32[]{:S(2)}) %collective-permute-start.8) | collective-permute-done | bytes 98336 | tf_op jit(solution)/shard_map/ppermute | solution.py:333
  35.0 0.6 %fresh_part.3.mine = f32[256,128]{1,0:T(8,128)S(1)} custom-call(s32[5,8]{1,0:T(8,128)S(4)} %get-tuple-element.12.meta, bf16[8,256,256]{2,1,0:T(8,128)(2,1)S(1)} %get-tuple-element.17.tiles, bf16[384,128]{1,0:T(8,128)(2,1)S(1)} %collective-permute-done.8.source, f32[256,128]{1,0:T(8,128)S(1)} %fresh_part.2.acc), custom_call_target="tpu_custom_call" | custom-call | tf_op jit(solution)/shard_map/fresh_part/pallas_call | solution.py:301
  35.6 0.1 collective-permute-start.9
  35.7 1.3 %collective-permute-done.9.other = f32[256,128]{1,0:T(8,128)S(1)} collective-permute-done((f32[256,128]{1,0:T(8,128)S(1)}, f32[256,128]{1,0:T(8,128)S(1)}, u32[]{:S(2)}, u32[]{:S(2)}) %collective-permute-start.9) | collective-permute-done | bytes 131104 | tf_op jit(solution)/shard_map/ppermute | solution.py:52
  37.0 0.9 %second_currents.1 = bf16[2,256,128]{2,1,0:T(8,128)(2,1)} custom-call(s32[5,8]{1,0:T(8,128)S(4)} %get-tuple-element.12.meta, bf16[256,128]{1,0:T(8,128)(2,1)S(1)} %first_currents.1.own.first, f32[256,128]{1,0:T(8,128)S(1)} %fresh_part.3.mine, f32[256,128]{1,0:T(8,128)S(1)} %collective-permute-done.9.other, bf16[256,256]{1,0:T(8,128)(2,1)S(1)} %bitcast.9, ...), custom_call_target="tpu_custom_call" | custom-call | tf_op jit(solution)/shard_map/second_currents/pallas_call | solution.py:385
  (4 shorter events, 0.0 us)
Async XLA Ops:
  0.0 16.3 %copy-start = (bf16[1,8,4,256,256]{4,3,2,1,0:T(8,128)(2,1)S(1)}, bf16[1,8,4,256,256]{4,3,2,1,0:T(8,128)(2,1)}, u32[]{:S(2)}) copy-start(bf16[1,8,4,256,256]{4,3,2,1,0:T(8,128)(2,1)} %param.7) | copy-start | bytes 12582916
  1.5 14.8 %collective-permute-start = (bf16[8,256,256]{2,1,0:T(8,128)(2,1)S(1)}, bf16[8,256,256]{2,1,0:T(8,128)(2,1)S(1)}, u32[]{:S(2)}, u32[]{:S(2)}) collective-permute-start(bf16[8,256,256]{2,1,0:T(8,128)(2,1)S(1)} %get-tuple-element.13), channel_id=1, source_target_pairs={{0,1},{1,0},{2,3},{3,2},{4,5},{5,4},{6,7},{7,6},{8,9},{9,8},{10,11... | collective-permute-start | bytes 3145736 | tf_op jit(solution)/shard_map/ppermute | solution.py:52
  2.0 10.9 %collective-permute-start.1 = (bf16[5,256,128]{2,1,0:T(8,128)(2,1)S(1)}, bf16[5,256,128]{2,1,0:T(8,128)(2,1)S(1)}, u32[]{:S(2)}, u32[]{:S(2)}) collective-permute-start(bf16[5,256,128]{2,1,0:T(8,128)(2,1)S(1)} %get-tuple-element.14.refs_0_), channel_id=1, source_target_pairs={{0,2},{2,0},{4,6},{6,4},{8,10},{10,8},{12,14},{14,12},{1,3},{3,1},... | collective-permute-start | bytes 983048 | tf_op jit(solution)/shard_map/ppermute | solution.py:333
  4.6 11.7 %collective-permute-start.2 = (bf16[5,256,128]{2,1,0:T(8,128)(2,1)S(1)}, bf16[5,256,128]{2,1,0:T(8,128)(2,1)S(1)}, u32[]{:S(2)}, u32[]{:S(2)}) collective-permute-start(bf16[5,256,128]{2,1,0:T(8,128)(2,1)S(1)} %get-tuple-element.14.refs_0_), channel_id=1, source_target_pairs={{0,4},{2,6},{4,0},{6,2},{8,12},{10,14},{12,8},{14,10},{1,17},{3,19... | collective-permute-start | bytes 983048 | tf_op jit(solution)/shard_map/ppermute | solution.py:333
  6.2 10.1 %collective-permute-start.3 = (bf16[5,256,128]{2,1,0:T(8,128)(2,1)S(1)}, bf16[5,256,128]{2,1,0:T(8,128)(2,1)S(1)}, u32[]{:S(2)}, u32[]{:S(2)}) collective-permute-start(bf16[5,256,128]{2,1,0:T(8,128)(2,1)S(1)} %get-tuple-element.14.refs_0_), channel_id=1, source_target_pairs={{0,16},{2,18},{4,8},{6,10},{8,4},{10,6},{12,28},{14,30},{1,5},{3,7... | collective-permute-start | bytes 983048 | tf_op jit(solution)/shard_map/ppermute | solution.py:333
  12.9 10.4 %collective-permute-start.4 = (bf16[5,256,128]{2,1,0:T(8,128)(2,1)S(1)}, bf16[5,256,128]{2,1,0:T(8,128)(2,1)S(1)}, u32[]{:S(2)}, u32[]{:S(2)}) collective-permute-start(bf16[5,256,128]{2,1,0:T(8,128)(2,1)S(1)} %collective-permute-done.1.refs_1_), channel_id=1, source_target_pairs={{0,4},{2,6},{4,0},{6,2},{8,12},{10,14},{12,8},{14,10},{1,17},{3,19... | collective-permute-start | bytes 983048 | tf_op jit(solution)/shard_map/ppermute | solution.py:333
  14.7 8.5 %collective-permute-start.5 = (bf16[5,256,128]{2,1,0:T(8,128)(2,1)S(1)}, bf16[5,256,128]{2,1,0:T(8,128)(2,1)S(1)}, u32[]{:S(2)}, u32[]{:S(2)}) collective-permute-start(bf16[5,256,128]{2,1,0:T(8,128)(2,1)S(1)} %collective-permute-done.1.refs_1_), channel_id=1, source_target_pairs={{0,16},{2,18},{4,8},{6,10},{8,4},{10,6},{12,28},{14,30},{1,5},{3,7... | collective-permute-start | bytes 983048 | tf_op jit(solution)/shard_map/ppermute | solution.py:333
  18.8 7.0 %copy-start.1 = (bf16[1,256,256]{2,1,0:T(8,128)(2,1)S(1)}, bf16[1,256,256]{2,1,0:T(8,128)(2,1)}, u32[]{:S(2)}) copy-start(bf16[1,256,256]{2,1,0:T(8,128)(2,1)} %param.9) | copy-start | bytes 393220
  18.8 7.0 %copy-start.2 = (f32[2,128]{1,0:T(2,128)S(1)}, f32[2,128]{1,0:T(2,128)}, u32[]{:S(2)}) copy-start(f32[2,128]{1,0:T(2,128)} %wave.3) | copy-start | bytes 3076
  18.8 7.0 %copy-start.3 = (s32[128]{0:T(128)S(1)}, s32[128]{0:T(128)}, u32[]{:S(2)}) copy-start(s32[128]{0:T(128)} %param.12) | copy-start | bytes 1540
  24.4 1.4 %collective-permute-start.6 = (f32[256,128]{1,0:T(8,128)S(1)}, f32[256,128]{1,0:T(8,128)S(1)}, u32[]{:S(2)}, u32[]{:S(2)}) collective-permute-start(f32[256,128]{1,0:T(8,128)S(1)} %get-tuple-element.16.mine), channel_id=1, source_target_pairs={{0,1},{1,0},{2,3},{3,2},{4,5},{5,4},{6,7},{7,6},{8,9},{9,8},{10,11... | collective-permute-start | bytes 393224 | tf_op jit(solution)/shard_map/ppermute | solution.py:52
  26.0 4.3 %collective-permute-start.7 = (bf16[256,128]{1,0:T(8,128)(2,1)S(1)}, bf16[256,128]{1,0:T(8,128)(2,1)S(1)}, u32[]{:S(2)}, u32[]{:S(2)}) collective-permute-start(bf16[256,128]{1,0:T(8,128)(2,1)S(1)} %first_currents.1.own.first), channel_id=1, source_target_pairs={{0,4},{2,6},{4,0},{6,2},{8,12},{10,14},{12,8},{14,10},{1,17},{3,19... | collective-permute-start | bytes 196616 | tf_op jit(solution)/shard_map/ppermute | solution.py:333
  30.3 4.7 %collective-permute-start.8 = (bf16[384,128]{1,0:T(8,128)(2,1)S(1)}, bf16[384,128]{1,0:T(8,128)(2,1)S(1)}, u32[]{:S(2)}, u32[]{:S(2)}) collective-permute-start(bf16[384,128]{1,0:T(8,128)(2,1)S(1)} %pack.1.source), channel_id=1, source_target_pairs={{0,2},{2,0},{4,6},{6,4},{8,10},{10,8},{12,14},{14,12},{1,3},{3,1},... | collective-permute-start | bytes 294920 | tf_op jit(solution)/shard_map/ppermute | solution.py:333
  35.6 1.4 %collective-permute-start.9 = (f32[256,128]{1,0:T(8,128)S(1)}, f32[256,128]{1,0:T(8,128)S(1)}, u32[]{:S(2)}, u32[]{:S(2)}) collective-permute-start(f32[256,128]{1,0:T(8,128)S(1)} %fresh_part.3.mine), channel_id=1, source_target_pairs={{0,1},{1,0},{2,3},{3,2},{4,5},{5,4},{6,7},{7,6},{8,9},{9,8},{10,11... | collective-permute-start | bytes 393224 | tf_op jit(solution)/shard_map/ppermute | solution.py:52

commit v4 on v3

--- a/solution.py
+++ b/solution.py
@@ -16,6 +16,7 @@
 
 SLOT, LATE, NEWS, ORDER, PLACE = range(5)
 CHUNK = 4
+PIECES = 4
 
 
 def held(x):
@@ -52,22 +53,34 @@
     return lax.ppermute(x, "sub", [(0, 1), (1, 0)])
 
 
-def start_kernel(slots, sites, groups, *refs):
-    src, delay, history, tiles, planes, taps, meta, src_buf, delay_buf, sem = refs
+def planes_kernel(history, planes, sem):
+    core = lax.axis_index("sub")
+    count = planes.shape[0]
+    copy = pltpu.make_async_copy(
+        history.at[pl.ds(core * (count - 1), count)], planes, sem
+    )
+    copy.start()
+    copy.wait()
+
+
+def table_kernel(slots, sites, groups, *refs):
+    src, delay, tiles, after = refs[:4]
+    *taps, whole, meta, src_buf, delay_buf, sem = refs[4:]
+    part = taps[0].shape[0]
     site, member, core = (lax.axis_index(a) for a in GRID_AXES)
-    count, rows = planes.shape[:2]
+    rows = tiles.shape[2]
     copies = [
-        pltpu.make_async_copy(
-            history.at[pl.ds(core * (count - 1), count)], planes, sem.at[0]
-        ),
-        pltpu.make_async_copy(src, src_buf, sem.at[1]),
-        pltpu.make_async_copy(delay, delay_buf, sem.at[2]),
-        pltpu.make_async_copy(tiles.at[:, 0], taps, sem.at[3]),
+        pltpu.make_async_copy(src, src_buf, sem.at[0]),
+        pltpu.make_async_copy(delay, delay_buf, sem.at[1]),
+    ] + [
+        pltpu.make_async_copy(tiles.at[pl.ds(n * part, part), 0], out, sem.at[2 + n])
+        for n, out in enumerate(taps)
     ]
+    copies.append(pltpu.make_async_copy(tiles, whole, sem.at[2 + len(taps)]))
     for copy in copies:
         copy.start()
+    copies[0].wait()
     copies[1].wait()
-    copies[2].wait()
     even_step = jnp.where(site % 2 == 0, 1, -1)
     ahead = jnp.int32(0)
     behind = jnp.int32(src.shape[1])
@@ -93,15 +106,56 @@
         meta[PLACE, p] = core
     meta[PLACE, 0] = (site * groups + member) * rows
     meta[PLACE, 2] = ahead
-    copies[0].wait()
-    copies[3].wait()
-
-
-def near_kernel(count, meta, tiles, extra, *refs):
-    sources, (total, newest) = refs[:count], refs[count:]
+    for copy in copies[2:]:
+        copy.wait()
+
+
+def swapped_kernel(count, meta, tiles, acc, *refs):
+    sources, pieces = refs[:count], refs[count:-3]
+    extra, newest, total = refs[-3:]
+    part = pieces[0].shape[0]
+    taps = tiles.shape[1]
     width = sources[0].shape[2]
+    core = meta[PLACE, 1]
+    total[...] = acc[...]
+    for n, piece in enumerate(pieces):
+        extra[n * part : (n + 1) * part] = piece[...]
+
+    @pl.when(core == 1)
+    def _():
+        newest[...] = extra[...]
+
+    @pl.when(core == 0)
+    def _():
+        newest[...] = tiles[:, 0]
+
+        @pl.loop(0, tiles.shape[0])
+        def _(p):
+            for slot, source in enumerate(sources):
+                used = jnp.logical_and(meta[SLOT, p] == slot, meta[LATE, p] == 0)
+
+                @pl.when(used)
+                def _():
+                    total[:, width:] += jnp.dot(
+                        extra[p], source[taps - 1], preferred_element_type=jnp.float32
+                    )
+
+
+def swapped_part(meta, tiles, acc, sources, pieces):
+    whole = pltpu.VMEM(tiles.shape[:1] + tiles.shape[2:], tiles.dtype)
+    return pl.pallas_call(
+        functools.partial(swapped_kernel, len(sources)),
+        out_shape=[whole, whole, pltpu.VMEM(acc.shape, acc.dtype)],
+        in_specs=[SMEM] + [VMEM] * (2 + len(sources) + len(pieces)),
+        out_specs=[VMEM] * 3,
+        compiler_params=SMALL,
+        name="swapped_part",
+    )(table(meta), held(tiles), held(acc), *[held(x) for x in sources + pieces])
+
+
+def near_kernel(count, meta, tiles, *refs):
+    sources, (total,) = refs[:count], refs[count:]
     taps = tiles.shape[1]
-    core = meta[PLACE, 1]
     total[...] = jnp.zeros_like(total)
 
     def one(p, source):
@@ -118,39 +172,22 @@
             preferred_element_type=jnp.float32,
         )
 
-        @pl.when(jnp.logical_and(core == 0, late == 0))
-        def _():
-            total[:, width:] += jnp.dot(
-                extra[p], source[taps - 1], preferred_element_type=jnp.float32
-            )
-
     @pl.loop(0, tiles.shape[0])
     def _(p):
-        @pl.when(core == 0)
-        def _():
-            newest[p] = tiles[p, 0]
-
-        @pl.when(core == 1)
-        def _():
-            newest[p] = extra[p]
-
         for slot, source in enumerate(sources):
             pl.when(meta[SLOT, p] == slot)(functools.partial(one, p, source))
 
 
-def near_part(meta, tiles, extra, sources):
+def near_part(meta, tiles, sources):
     rows, width = sources[0].shape[1:]
     return pl.pallas_call(
         functools.partial(near_kernel, len(sources)),
-        out_shape=[
-            pltpu.VMEM((rows, 2 * width), jnp.float32),
-            pltpu.VMEM(extra.shape, extra.dtype),
-        ],
-        in_specs=[SMEM] + [VMEM] * (2 + len(sources)),
-        out_specs=[VMEM, VMEM],
+        out_shape=pltpu.VMEM((rows, 2 * width), jnp.float32),
+        in_specs=[SMEM] + [VMEM] * (1 + len(sources)),
+        out_specs=VMEM,
         compiler_params=SMALL,
         name="near_part",
-    )(table(meta), held(tiles), held(extra), *[held(x) for x in sources])
+    )(table(meta), held(tiles), *[held(x) for x in sources])
 
 
 def relayed_kernel(first, count, meta, tiles, extra, acc, *refs):
@@ -339,32 +376,40 @@
             for n, kind in enumerate(("even", "odd")):
                 slots[c][key[kind, t]] = groups + 2 * t + (n ^ c)
 
-    planes, taps0, meta = pl.pallas_call(
-        functools.partial(start_kernel, slots, sites, groups),
-        out_shape=[
-            pltpu.VMEM((taps + 1, rows, width), history.dtype),
-            pltpu.VMEM((pairs, rows, cols), tiles.dtype),
-            pltpu.SMEM((5, pairs), jnp.int32),
-        ],
+    planes = pl.pallas_call(
+        planes_kernel,
+        out_shape=pltpu.VMEM((taps + 1, rows, width), history.dtype),
+        in_specs=[ANY],
+        out_specs=VMEM,
+        scratch_shapes=[pltpu.SemaphoreType.DMA],
+        compiler_params=SMALL,
+        name="own_planes",
+    )(far(history))
+    *taps0, tiles, meta = pl.pallas_call(
+        functools.partial(table_kernel, slots, sites, groups),
+        out_shape=[pltpu.VMEM((pairs // PIECES, rows, cols), tiles.dtype)] * PIECES
+        + [pltpu.VMEM(tiles.shape, tiles.dtype), pltpu.SMEM((5, pairs), jnp.int32)],
         in_specs=[ANY] * 4,
-        out_specs=[VMEM, VMEM, SMEM],
+        out_specs=[VMEM] * (PIECES + 1) + [SMEM],
         scratch_shapes=[
             pltpu.SMEM((1, pairs), jnp.int32),
             pltpu.SMEM((1, pairs), jnp.int32),
-            pltpu.SemaphoreType.DMA((4,)),
+            pltpu.SemaphoreType.DMA((3 + PIECES,)),
         ],
         compiler_params=SMALL,
-        name="start",
-    )(far(pair_src), far(pair_delay), far(history), far(tiles))
+        name="table",
+    )(far(pair_src), far(pair_delay), far(tiles), planes)
 
     own = [planes] + [send(planes, *[("own", t)] * 2) for t in range(1, groups)]
     partners = []
     for x in own:
         partners.append(send(x, ("even", 0), ("odd", 0)))
         partners.append(send(x, ("odd", 0), ("even", 0)))
-    extra = swap_cores(taps0)
-
-    acc, newest = near_part(meta, tiles, extra, own + partners[:2])
+    pieces = [swap_cores(x) for x in taps0]
+
+    near = own + partners[:2]
+    acc = near_part(meta, tiles, near)
+    extra, newest, acc = swapped_part(meta, tiles, acc, near, pieces)
     mine0, mine1 = relayed_part(meta, tiles, extra, acc, partners[2:], groups + 2)
 
     strike, inverse, wave = held(strike_seg[None, :]), held(inverse), held(waveform)

time: 38 us -> 36.6 us (0.963)
  waiting for transfers between devices: 17.1 us -> 12.7 us
  Pallas kernels: 7.33 us -> 10.5 us
    ppermute x7, waiting for transfers between devices: 14.4 us -> 9.99 us  [send(): return lax.ppermute(x, ALL_AXES, pairs)]
    pallas_call x2 -> x4, Pallas kernels: 3.97 us -> 7.17 us  [the longest x1 2.58 us: per_device(): pl.pallas_call(functools.partial(table_kernel, slots, sites, groups), out...]
    ppermute x3 -> x6, starting transfers between devices: 0.66 us -> 0.79 us  [swap_cores(): return lax.ppermute(x, 'sub', [(0, 1), (1, 0)])]
    ppermute x3 -> x6, waiting for transfers between devices: 2.67 us -> 2.68 us  [swap_cores(): return lax.ppermute(x, 'sub', [(0, 1), (1, 0)])]
  transfers between devices with their start and end apart: 10 -> 13, of which waited for: 6 -> 6; matrix products, arithmetic and copies ran while one was open for 0% -> 0% of each run, Pallas kernels for 8% -> 18%
where the time goes in v4:
time: 36.6 us; the launch traced here: 36.4 us
  starting transfers between devices  13.1 us (36%)
  waiting for transfers between devices  12.7 us (35%)
  Pallas kernels  10.5 us (29%)
    ppermute x7, starting transfers between devices, send(): return lax.ppermute(x, ALL_AXES, pairs)  12.3 us
    ppermute x7, waiting for transfers between devices, send(): return lax.ppermute(x, ALL_AXES, pairs)  9.99 us
    ppermute x6, waiting for transfers between devices, swap_cores(): return lax.ppermute(x, 'sub', [(0, 1), (1, 0)])  2.68 us
    pallas_call x1, Pallas kernels, per_device(): pl.pallas_call(functools.partial(table_kernel, slots, sites, groups), out...  2.58 us
    pallas_call x1, Pallas kernels, near_part(): pl.pallas_call(functools.partial(near_kernel, len(sources)), out_shape=pl...  2.45 us
    pallas_call x2, Pallas kernels, fresh_part(): pl.pallas_call(functools.partial(fresh_kernel, turn), out_shape=pltpu.VME...  1.18 us
    pallas_call x1, Pallas kernels, swapped_part(): pl.pallas_call(functools.partial(swapped_kernel, len(sources)), out_shape...  1.17 us
    pallas_call x1, Pallas kernels, relayed_part(): pl.pallas_call(functools.partial(relayed_kernel, first, len(sources)), ou...  1.08 us
  transfers between devices with their start and end apart: 13, of which 6 were waited for; matrix products, arithmetic and copies ran while one was open for 0% of the time, Pallas kernels for 18%

profile of v4, /device:TPU:0, one launch (start us, length us, event | category | flops | bytes accessed | tf_op | source)
XLA Modules:
  0.0 36.4 jit_solution(2473238005207019435)
XLA Ops:
  0.0 1.0 %own_planes.1.refs_3_.refs_0_ = bf16[5,256,128]{2,1,0:T(8,128)(2,1)S(1)} custom-call(bf16[9,256,128]{2,1,0:T(8,128)(2,1)} %bitcast.10), custom_call_target="tpu_custom_call" | custom-call | tf_op jit(solution)/shard_map/own_planes/pallas_call | solution.py:379
  1.0 3.0 %collective-permute-start = (bf16[5,256,128]{2,1,0:T(8,128)(2,1)S(1)}, bf16[5,256,128]{2,1,0:T(8,128)(2,1)S(1)}, u32[]{:S(2)}, u32[]{:S(2)}) collective-permute-start(bf16[5,256,128]{2,1,0:T(8,128)(2,1)S(1)} %own_planes.1.refs_3_.refs_0_), channel_id=1, source_target_pairs={{0,2},{2,0},{4,6},{6,4},{8,10},{10,8},{12,14},{14,12},{1,3},{3,1},... | collective-permute-start | bytes 983048 | tf_op jit(solution)/shard_map/ppermute | solution.py:370
  4.0 1.6 %collective-permute-start.1 = (bf16[5,256,128]{2,1,0:T(8,128)(2,1)S(1)}, bf16[5,256,128]{2,1,0:T(8,128)(2,1)S(1)}, u32[]{:S(2)}, u32[]{:S(2)}) collective-permute-start(bf16[5,256,128]{2,1,0:T(8,128)(2,1)S(1)} %own_planes.1.refs_3_.refs_0_), channel_id=1, source_target_pairs={{0,4},{2,6},{4,0},{6,2},{8,12},{10,14},{12,8},{14,10},{1,17},{3,19... | collective-permute-start | bytes 983048 | tf_op jit(solution)/shard_map/ppermute | solution.py:370
  5.6 1.5 %collective-permute-start.2 = (bf16[5,256,128]{2,1,0:T(8,128)(2,1)S(1)}, bf16[5,256,128]{2,1,0:T(8,128)(2,1)S(1)}, u32[]{:S(2)}, u32[]{:S(2)}) collective-permute-start(bf16[5,256,128]{2,1,0:T(8,128)(2,1)S(1)} %own_planes.1.refs_3_.refs_0_), channel_id=1, source_target_pairs={{0,16},{2,18},{4,8},{6,10},{8,4},{10,6},{12,28},{14,30},{1,5},{3,7... | collective-permute-start | bytes 983048 | tf_op jit(solution)/shard_map/ppermute | solution.py:370
  7.1 2.6 %table.1 = (bf16[2,256,256]{2,1,0:T(8,128)(2,1)S(1)}, bf16[2,256,256]{2,1,0:T(8,128)(2,1)S(1)}, bf16[2,256,256]{2,1,0:T(8,128)(2,1)S(1)}, bf16[2,256,256]{2,1,0:...) custom-call(s32[1,8]{1,0:T(1,128)} %refs_0_.1, s32[1,8]{1,0:T(1,128)} %refs_1_.1, ...), custom_call_target="tpu_custom_call" | custom-call | tf_op jit(solution)/shard_map/table/pallas_call | solution.py:388
  9.7 0.1 collective-permute-start.3
  9.8 1.9 %collective-permute-done.refs_1_ = bf16[5,256,128]{2,1,0:T(8,128)(2,1)S(1)} collective-permute-done((bf16[5,256,128]{2,1,0:T(8,128)(2,1)S(1)}, bf16[5,256,128]{2,1,0:T(8,128)(2,1)S(1)}, u32[]{:S(2)}, u32[]{:S(2)}) %collective-permute-start) | collective-permute-done | bytes 327712 | tf_op jit(solution)/shard_map/ppermute | solution.py:370
  11.7 1.8 %collective-permute-start.7 = (bf16[5,256,128]{2,1,0:T(8,128)(2,1)S(1)}, bf16[5,256,128]{2,1,0:T(8,128)(2,1)S(1)}, u32[]{:S(2)}, u32[]{:S(2)}) collective-permute-start(bf16[5,256,128]{2,1,0:T(8,128)(2,1)S(1)} %collective-permute-done.refs_1_), channel_id=1, source_target_pairs={{0,4},{2,6},{4,0},{6,2},{8,12},{10,14},{12,8},{14,10},{1,17},{3,19... | collective-permute-start | bytes 983048 | tf_op jit(solution)/shard_map/ppermute | solution.py:370
  13.5 1.5 %collective-permute-start.8 = (bf16[5,256,128]{2,1,0:T(8,128)(2,1)S(1)}, bf16[5,256,128]{2,1,0:T(8,128)(2,1)S(1)}, u32[]{:S(2)}, u32[]{:S(2)}) collective-permute-start(bf16[5,256,128]{2,1,0:T(8,128)(2,1)S(1)} %collective-permute-done.refs_1_), channel_id=1, source_target_pairs={{0,16},{2,18},{4,8},{6,10},{8,4},{10,6},{12,28},{14,30},{1,5},{3,7... | collective-permute-start | bytes 983048 | tf_op jit(solution)/shard_map/ppermute | solution.py:370
  15.1 0.0 collective-permute-done.1.refs_2_
  15.1 0.5 %collective-permute-start.5 = (bf16[2,256,256]{2,1,0:T(8,128)(2,1)S(1)}, bf16[2,256,256]{2,1,0:T(8,128)(2,1)S(1)}, u32[]{:S(2)}, u32[]{:S(2)}) collective-permute-start(bf16[2,256,256]{2,1,0:T(8,128)(2,1)S(1)} %get-tuple-element.20), channel_id=1, source_target_pairs={{0,1},{1,0},{2,3},{3,2},{4,5},{5,4},{6,7},{7,6},{8,9},{9,8},{10,11... | collective-permute-start | bytes 786440 | tf_op jit(solution)/shard_map/ppermute | solution.py:53
  15.6 0.1 collective-permute-start.6
  15.6 2.4 %near_part.1.acc = f32[256,256]{1,0:T(8,128)S(1)} custom-call(s32[5,8]{1,0:T(8,128)S(4)} %get-tuple-element.16.meta, bf16[8,4,256,256]{3,2,1,0:T(8,128)(2,1)S(1)} %get-tuple-element.17.tiles, bf16[5,256,128]{2,1,0:T(8,128)(2,1)S(1)} %own_planes.1.refs_3_.refs_0_, bf16[5,256,128]{2,1,0:T(8,128)(2,1)S(1)} %collective-permute-done.refs_1_, ...), custom_call_target="tpu_custom_call" | custom-call | tf_op jit(solution)/shard_map/near_part/pallas_call | solution.py:183
  18.1 0.0 collective-permute-done.5.refs_6_
  18.1 1.2 %swapped_part.1 = (bf16[8,256,256]{2,1,0:T(8,128)(2,1)S(1)}, bf16[8,256,256]{2,1,0:T(8,128)(2,1)S(1)}, f32[256,256]{1,0:T(8,128)S(1)}) custom-call(s32[5,8]{1,0:T(8,128)S(4)} %get-tuple-element.16.meta, bf16[8,4,256,256]{3,2,1,0:T(8,128)(2,1)S(1)} %get-tuple-element.17.tiles, f32[256,256]{1,0:T(8,128)S(1)} %near_part.1.acc, ...), custom_call_target="tpu_custom_call" | custom-call | tf_op jit(solution)/shard_map/swapped_part/pallas_call | solution.py:146
  19.3 0.0 copy-start
  19.3 0.0 copy-start.1
  19.3 0.0 copy-start.2
  19.3 2.4 %collective-permute-done.7.refs_0_ = bf16[5,256,128]{2,1,0:T(8,128)(2,1)S(1)} collective-permute-done((bf16[5,256,128]{2,1,0:T(8,128)(2,1)S(1)}, bf16[5,256,128]{2,1,0:T(8,128)(2,1)S(1)}, u32[]{:S(2)}, u32[]{:S(2)}) %collective-permute-start.7) | collective-permute-done | bytes 327712 | tf_op jit(solution)/shard_map/ppermute | solution.py:370
  21.8 1.1 %relayed_part.1 = (f32[256,128]{1,0:T(8,128)S(1)}, f32[256,128]{1,0:T(8,128)S(1)}) custom-call(s32[5,8]{1,0:T(8,128)S(4)} %get-tuple-element.16.meta, bf16[8,4,256,256]{3,2,1,0:T(8,128)(2,1)S(1)} %get-tuple-element.17.tiles, bf16[8,256,256]{2,1,0:T(8,128)(2,1)S(1)} %get-tuple-element.22.extra, f32[256,256]{1,0:T(8,128)S(1)} %get-tuple-element.23.acc, ...), custom_call_target="tpu_custom_call" | custom-call | tf_op jit(solution)/shard_map/relayed_part/pallas_call | solution.py:249
  22.9 0.1 collective-permute-start.9
  22.9 1.3 %collective-permute-done.9.other = f32[256,128]{1,0:T(8,128)S(1)} collective-permute-done((f32[256,128]{1,0:T(8,128)S(1)}, f32[256,128]{1,0:T(8,128)S(1)}, u32[]{:S(2)}, u32[]{:S(2)}) %collective-permute-start.9) | collective-permute-done | bytes 131104 | tf_op jit(solution)/shard_map/ppermute | solution.py:53
  24.3 0.2 first_currents.1.own.first
  24.5 1.7 %collective-permute-start.10 = (bf16[256,128]{1,0:T(8,128)(2,1)S(1)}, bf16[256,128]{1,0:T(8,128)(2,1)S(1)}, u32[]{:S(2)}, u32[]{:S(2)}) collective-permute-start(bf16[256,128]{1,0:T(8,128)(2,1)S(1)} %first_currents.1.own.first), channel_id=1, source_target_pairs={{0,4},{2,6},{4,0},{6,2},{8,12},{10,14},{12,8},{14,10},{1,17},{3,19... | collective-permute-start | bytes 196616 | tf_op jit(solution)/shard_map/ppermute | solution.py:370
  26.2 2.6 %collective-permute-done.10.other = bf16[256,128]{1,0:T(8,128)(2,1)S(1)} collective-permute-done((bf16[256,128]{1,0:T(8,128)(2,1)S(1)}, bf16[256,128]{1,0:T(8,128)(2,1)S(1)}, u32[]{:S(2)}, u32[]{:S(2)}) %collective-permute-start.10) | collective-permute-done | bytes 65568 | tf_op jit(solution)/shard_map/ppermute | solution.py:370
  28.8 1.2 %collective-permute-start.11 = (bf16[384,128]{1,0:T(8,128)(2,1)S(1)}, bf16[384,128]{1,0:T(8,128)(2,1)S(1)}, u32[]{:S(2)}, u32[]{:S(2)}) collective-permute-start(bf16[384,128]{1,0:T(8,128)(2,1)S(1)} %pack.1.source), channel_id=1, source_target_pairs={{0,2},{2,0},{4,6},{6,4},{8,10},{10,8},{12,14},{14,12},{1,3},{3,1},... | collective-permute-start | bytes 294920 | tf_op jit(solution)/shard_map/ppermute | solution.py:370
  30.0 0.5 %fresh_part.2.acc = f32[256,128]{1,0:T(8,128)S(1)} custom-call(s32[5,8]{1,0:T(8,128)S(4)} %get-tuple-element.16.meta, bf16[8,256,256]{2,1,0:T(8,128)(2,1)S(1)} %get-tuple-element.25.tiles, bf16[384,128]{1,0:T(8,128)(2,1)S(1)} %pack.1.source, f32[256,128]{1,0:T(8,128)S(1)} %get-tuple-element.26.acc), custom_call_target="tpu_custom_call" | custom-call | tf_op jit(solution)/shard_map/fresh_part/pallas_call | solution.py:338
  30.5 3.0 %collective-permute-done.11.source = bf16[384,128]{1,0:T(8,128)(2,1)S(1)} collective-permute-done((bf16[384,128]{1,0:T(8,128)(2,1)S(1)}, bf16[384,128]{1,0:T(8,128)(2,1)S(1)}, u32[]{:S(2)}, u32[]{:S(2)}) %collective-permute-start.11) | collective-permute-done | bytes 98336 | tf_op jit(solution)/shard_map/ppermute | solution.py:370
  33.5 0.7 %fresh_part.3.mine = f32[256,128]{1,0:T(8,128)S(1)} custom-call(s32[5,8]{1,0:T(8,128)S(4)} %get-tuple-element.16.meta, bf16[8,256,256]{2,1,0:T(8,128)(2,1)S(1)} %get-tuple-element.25.tiles, bf16[384,128]{1,0:T(8,128)(2,1)S(1)} %collective-permute-done.11.source, f32[256,128]{1,0:T(8,128)S(1)} %fresh_part.2.acc), custom_call_target="tpu_custom_call" | custom-call | tf_op jit(solution)/shard_map/fresh_part/pallas_call | solution.py:338
  34.2 0.1 collective-permute-start.12
  34.2 1.3 %collective-permute-done.12.other = f32[256,128]{1,0:T(8,128)S(1)} collective-permute-done((f32[256,128]{1,0:T(8,128)S(1)}, f32[256,128]{1,0:T(8,128)S(1)}, u32[]{:S(2)}, u32[]{:S(2)}) %collective-permute-start.12) | collective-permute-done | bytes 131104 | tf_op jit(solution)/shard_map/ppermute | solution.py:53
  35.6 0.9 %second_currents.1 = bf16[2,256,128]{2,1,0:T(8,128)(2,1)} custom-call(s32[5,8]{1,0:T(8,128)S(4)} %get-tuple-element.16.meta, bf16[256,128]{1,0:T(8,128)(2,1)S(1)} %first_currents.1.own.first, f32[256,128]{1,0:T(8,128)S(1)} %fresh_part.3.mine, f32[256,128]{1,0:T(8,128)S(1)} %collective-permute-done.12.other, bf16[256,256]{1,0:T(8,128)(2,1)S(1)} %bitcast.6, ...), custom_call_target="tpu_custom_call" | custom-call | tf_op jit(solution)/shard_map/second_currents/pallas_call | solution.py:430
  (10 shorter events, 0.0 us)
Async XLA Ops:
  1.0 10.7 %collective-permute-start = (bf16[5,256,128]{2,1,0:T(8,128)(2,1)S(1)}, bf16[5,256,128]{2,1,0:T(8,128)(2,1)S(1)}, u32[]{:S(2)}, u32[]{:S(2)}) collective-permute-start(bf16[5,256,128]{2,1,0:T(8,128)(2,1)S(1)} %own_planes.1.refs_3_.refs_0_), channel_id=1, source_target_pairs={{0,2},{2,0},{4,6},{6,4},{8,10},{10,8},{12,14},{14,12},{1,3},{3,1},... | collective-permute-start | bytes 983048 | tf_op jit(solution)/shard_map/ppermute | solution.py:370
  4.0 11.1 %collective-permute-start.1 = (bf16[5,256,128]{2,1,0:T(8,128)(2,1)S(1)}, bf16[5,256,128]{2,1,0:T(8,128)(2,1)S(1)}, u32[]{:S(2)}, u32[]{:S(2)}) collective-permute-start(bf16[5,256,128]{2,1,0:T(8,128)(2,1)S(1)} %own_planes.1.refs_3_.refs_0_), channel_id=1, source_target_pairs={{0,4},{2,6},{4,0},{6,2},{8,12},{10,14},{12,8},{14,10},{1,17},{3,19... | collective-permute-start | bytes 983048 | tf_op jit(solution)/shard_map/ppermute | solution.py:370
  5.6 10.0 %collective-permute-start.2 = (bf16[5,256,128]{2,1,0:T(8,128)(2,1)S(1)}, bf16[5,256,128]{2,1,0:T(8,128)(2,1)S(1)}, u32[]{:S(2)}, u32[]{:S(2)}) collective-permute-start(bf16[5,256,128]{2,1,0:T(8,128)(2,1)S(1)} %own_planes.1.refs_3_.refs_0_), channel_id=1, source_target_pairs={{0,16},{2,18},{4,8},{6,10},{8,4},{10,6},{12,28},{14,30},{1,5},{3,7... | collective-permute-start | bytes 983048 | tf_op jit(solution)/shard_map/ppermute | solution.py:370
  9.7 5.4 %collective-permute-start.3 = (bf16[2,256,256]{2,1,0:T(8,128)(2,1)S(1)}, bf16[2,256,256]{2,1,0:T(8,128)(2,1)S(1)}, u32[]{:S(2)}, u32[]{:S(2)}) collective-permute-start(bf16[2,256,256]{2,1,0:T(8,128)(2,1)S(1)} %get-tuple-element.18), channel_id=1, source_target_pairs={{0,1},{1,0},{2,3},{3,2},{4,5},{5,4},{6,7},{7,6},{8,9},{9,8},{10,11... | collective-permute-start | bytes 786440 | tf_op jit(solution)/shard_map/ppermute | solution.py:53
  11.7 10.1 %collective-permute-start.7 = (bf16[5,256,128]{2,1,0:T(8,128)(2,1)S(1)}, bf16[5,256,128]{2,1,0:T(8,128)(2,1)S(1)}, u32[]{:S(2)}, u32[]{:S(2)}) collective-permute-start(bf16[5,256,128]{2,1,0:T(8,128)(2,1)S(1)} %collective-permute-done.refs_1_), channel_id=1, source_target_pairs={{0,4},{2,6},{4,0},{6,2},{8,12},{10,14},{12,8},{14,10},{1,17},{3,19... | collective-permute-start | bytes 983048 | tf_op jit(solution)/shard_map/ppermute | solution.py:370
  13.5 8.2 %collective-permute-start.8 = (bf16[5,256,128]{2,1,0:T(8,128)(2,1)S(1)}, bf16[5,256,128]{2,1,0:T(8,128)(2,1)S(1)}, u32[]{:S(2)}, u32[]{:S(2)}) collective-permute-start(bf16[5,256,128]{2,1,0:T(8,128)(2,1)S(1)} %collective-permute-done.refs_1_), channel_id=1, source_target_pairs={{0,16},{2,18},{4,8},{6,10},{8,4},{10,6},{12,28},{14,30},{1,5},{3,7... | collective-permute-start | bytes 983048 | tf_op jit(solution)/shard_map/ppermute | solution.py:370
  15.1 3.0 %collective-permute-start.4 = (bf16[2,256,256]{2,1,0:T(8,128)(2,1)S(1)}, bf16[2,256,256]{2,1,0:T(8,128)(2,1)S(1)}, u32[]{:S(2)}, u32[]{:S(2)}) collective-permute-start(bf16[2,256,256]{2,1,0:T(8,128)(2,1)S(1)} %get-tuple-element.19), channel_id=1, source_target_pairs={{0,1},{1,0},{2,3},{3,2},{4,5},{5,4},{6,7},{7,6},{8,9},{9,8},{10,11... | collective-permute-start | bytes 786440 | tf_op jit(solution)/shard_map/ppermute | solution.py:53
  15.1 3.0 %collective-permute-start.5 = (bf16[2,256,256]{2,1,0:T(8,128)(2,1)S(1)}, bf16[2,256,256]{2,1,0:T(8,128)(2,1)S(1)}, u32[]{:S(2)}, u32[]{:S(2)}) collective-permute-start(bf16[2,256,256]{2,1,0:T(8,128)(2,1)S(1)} %get-tuple-element.20), channel_id=1, source_target_pairs={{0,1},{1,0},{2,3},{3,2},{4,5},{5,4},{6,7},{7,6},{8,9},{9,8},{10,11... | collective-permute-start | bytes 786440 | tf_op jit(solution)/shard_map/ppermute | solution.py:53
  15.6 2.5 %collective-permute-start.6 = (bf16[2,256,256]{2,1,0:T(8,128)(2,1)S(1)}, bf16[2,256,256]{2,1,0:T(8,128)(2,1)S(1)}, u32[]{:S(2)}, u32[]{:S(2)}) collective-permute-start(bf16[2,256,256]{2,1,0:T(8,128)(2,1)S(1)} %get-tuple-element.21), channel_id=1, source_target_pairs={{0,1},{1,0},{2,3},{3,2},{4,5},{5,4},{6,7},{7,6},{8,9},{9,8},{10,11... | collective-permute-start | bytes 786440 | tf_op jit(solution)/shard_map/ppermute | solution.py:53
  19.3 5.0 %copy-start = (bf16[1,256,256]{2,1,0:T(8,128)(2,1)S(1)}, bf16[1,256,256]{2,1,0:T(8,128)(2,1)}, u32[]{:S(2)}) copy-start(bf16[1,256,256]{2,1,0:T(8,128)(2,1)} %param.9) | copy-start | bytes 393220
  19.3 5.0 %copy-start.1 = (f32[2,128]{1,0:T(2,128)S(1)}, f32[2,128]{1,0:T(2,128)}, u32[]{:S(2)}) copy-start(f32[2,128]{1,0:T(2,128)} %wave.3) | copy-start | bytes 3076
  19.3 5.0 %copy-start.2 = (s32[128]{0:T(128)S(1)}, s32[128]{0:T(128)}, u32[]{:S(2)}) copy-start(s32[128]{0:T(128)} %param.12) | copy-start | bytes 1540
  22.9 1.4 %collective-permute-start.9 = (f32[256,128]{1,0:T(8,128)S(1)}, f32[256,128]{1,0:T(8,128)S(1)}, u32[]{:S(2)}, u32[]{:S(2)}) collective-permute-start(f32[256,128]{1,0:T(8,128)S(1)} %get-tuple-element.24.mine), channel_id=1, source_target_pairs={{0,1},{1,0},{2,3},{3,2},{4,5},{5,4},{6,7},{7,6},{8,9},{9,8},{10,11... | collective-permute-start | bytes 393224 | tf_op jit(solution)/shard_map/ppermute | solution.py:53
  24.5 4.3 %collective-permute-start.10 = (bf16[256,128]{1,0:T(8,128)(2,1)S(1)}, bf16[256,128]{1,0:T(8,128)(2,1)S(1)}, u32[]{:S(2)}, u32[]{:S(2)}) collective-permute-start(bf16[256,128]{1,0:T(8,128)(2,1)S(1)} %first_currents.1.own.first), channel_id=1, source_target_pairs={{0,4},{2,6},{4,0},{6,2},{8,12},{10,14},{12,8},{14,10},{1,17},{3,19... | collective-permute-start | bytes 196616 | tf_op jit(solution)/shard_map/ppermute | solution.py:370
  28.8 4.7 %collective-permute-start.11 = (bf16[384,128]{1,0:T(8,128)(2,1)S(1)}, bf16[384,128]{1,0:T(8,128)(2,1)S(1)}, u32[]{:S(2)}, u32[]{:S(2)}) collective-permute-start(bf16[384,128]{1,0:T(8,128)(2,1)S(1)} %pack.1.source), channel_id=1, source_target_pairs={{0,2},{2,0},{4,6},{6,4},{8,10},{10,8},{12,14},{14,12},{1,3},{3,1},... | collective-permute-start | bytes 294920 | tf_op jit(solution)/shard_map/ppermute | solution.py:370
  34.2 1.4 %collective-permute-start.12 = (f32[256,128]{1,0:T(8,128)S(1)}, f32[256,128]{1,0:T(8,128)S(1)}, u32[]{:S(2)}, u32[]{:S(2)}) collective-permute-start(f32[256,128]{1,0:T(8,128)S(1)} %fresh_part.3.mine), channel_id=1, source_target_pairs={{0,1},{1,0},{2,3},{3,2},{4,5},{5,4},{6,7},{7,6},{8,9},{9,8},{10,11... | collective-permute-start | bytes 393224 | tf_op jit(solution)/shard_map/ppermute | solution.py:53

commit v5 on v4

--- a/solution.py
+++ b/solution.py
@@ -1,4 +1,5 @@
 import functools
+import itertools
 
 import jax
 import jax.numpy as jnp
@@ -17,6 +18,7 @@
 SLOT, LATE, NEWS, ORDER, PLACE = range(5)
 CHUNK = 4
 PIECES = 4
+HALVES = 1
 
 
 def held(x):
@@ -63,7 +65,7 @@
     copy.wait()
 
 
-def table_kernel(slots, sites, groups, *refs):
+def table_kernel(slots, news, sites, groups, *refs):
     src, delay, tiles, after = refs[:4]
     *taps, whole, meta, src_buf, delay_buf, sem = refs[4:]
     part = taps[0].shape[0]
@@ -90,15 +92,14 @@
         dist = value // groups - site
         kind = jnp.where(dist == 0, 2, jnp.where(dist == even_step, 1, 0))
         key = kind * groups + turn
-        slot = jnp.int32(-1)
+        slot, fresh = jnp.int32(-1), jnp.int32(-1)
         for n in range(3 * groups):
-            mine = jnp.where(core == 0, slots[0][n], slots[1][n])
-            slot = jnp.where(key == n, mine, slot)
-        mine = jnp.where(kind == 2, 0, jnp.where(kind == 1 - core, 1, -1))
-        news = jnp.logical_and(wait == 1, mine >= 0)
+            mine = [jnp.where(core == 0, t[0][n], t[1][n]) for t in (slots, news)]
+            slot = jnp.where(key == n, mine[0], slot)
+            fresh = jnp.where(key == n, mine[1], fresh)
         meta[SLOT, p] = slot
         meta[LATE, p] = wait - 1
-        meta[NEWS, p] = jnp.where(news, 2 * turn + mine, -1)
+        meta[NEWS, p] = jnp.where(wait == 1, fresh, -1)
         relayed = slot >= groups + 2
         behind = behind - jnp.where(relayed, 0, 1)
         meta[ORDER, jnp.where(relayed, ahead, behind)] = p
@@ -151,6 +152,50 @@
         compiler_params=SMALL,
         name="swapped_part",
     )(table(meta), held(tiles), held(acc), *[held(x) for x in sources + pieces])
+
+
+def row_pieces(rows, start, stop):
+    for plane in range(start // rows, -(-stop // rows)):
+        low, high = max(start, plane * rows), min(stop, (plane + 1) * rows)
+        yield plane, low - plane * rows, high - plane * rows, low - start
+
+
+def heads_kernel(head, *refs):
+    sources, out = refs[:-1], refs[-1]
+    for n, source in enumerate(sources):
+        for plane, low, high, place in row_pieces(source.shape[1], 0, head):
+            place += n * head
+            out[place : place + high - low] = source[plane, low:high]
+
+
+def heads(sources, head):
+    width = sources[0].shape[2]
+    return pl.pallas_call(
+        functools.partial(heads_kernel, head),
+        out_shape=pltpu.VMEM((len(sources) * head, width), sources[0].dtype),
+        in_specs=[VMEM] * len(sources),
+        out_specs=VMEM,
+        compiler_params=SMALL,
+        name="heads",
+    )(*[held(x) for x in sources])
+
+
+def tail_kernel(head, source, out):
+    planes, rows, _ = source.shape
+    for plane, low, high, place in row_pieces(rows, head, planes * rows):
+        out[place : place + high - low] = source[plane, low:high]
+
+
+def tail(source, head):
+    planes, rows, width = source.shape
+    return pl.pallas_call(
+        functools.partial(tail_kernel, head),
+        out_shape=pltpu.VMEM((planes * rows - head, width), source.dtype),
+        in_specs=[VMEM],
+        out_specs=VMEM,
+        compiler_params=SMALL,
+        name="tail",
+    )(held(source))
 
 
 def near_kernel(count, meta, tiles, *refs):
@@ -190,13 +235,20 @@
     )(table(meta), held(tiles), *[held(x) for x in sources])
 
 
-def relayed_kernel(first, count, meta, tiles, extra, acc, *refs):
-    sources, (out0, out1, total, store) = refs[:count], refs[count:]
-    planes, _, width = sources[0].shape
-    pairs, taps = tiles.shape[:2]
-    none = count * planes
-    for n, source in enumerate(sources):
-        store[n * planes : (n + 1) * planes] = source[...]
+def relayed_kernel(first, turns, head, meta, tiles, extra, acc, *refs):
+    sources, (out0, out1, total, store) = refs[: 3 * turns], refs[3 * turns :]
+    pairs, taps, rows = tiles.shape[:3]
+    planes, width = taps + 1, acc.shape[1] // 2
+    none = 2 * turns * planes
+    for turn in range(turns):
+        tops, *rests = sources[3 * turn : 3 * turn + 3]
+        for n, rest in enumerate(rests):
+            base = (2 * turn + n) * planes
+            for plane, low, high, place in row_pieces(rows, 0, head):
+                place += n * head
+                store[base + plane, low:high] = tops[place : place + high - low]
+            for plane, low, high, place in row_pieces(rows, head, planes * rows):
+                store[base + plane, low:high] = rest[place : place + high - low]
     store[none] = jnp.zeros(store.shape[1:], store.dtype)
     total[...] = acc[...]
 
@@ -241,13 +293,14 @@
     out1[...] = total[:, width:]
 
 
-def relayed_part(meta, tiles, extra, acc, sources, first):
-    planes, rows, width = sources[0].shape
-    store = (len(sources) * planes + 1, rows, width)
+def relayed_part(meta, tiles, extra, acc, sources, head, first):
+    taps, rows = tiles.shape[1:3]
+    width, turns = acc.shape[1] // 2, len(sources) // 3
+    store = (2 * turns * (taps + 1) + 1, rows, width)
     half = pltpu.VMEM((rows, width), jnp.float32)
     room = 2 * store[0] * rows * width + 4 * acc.size
     return pl.pallas_call(
-        functools.partial(relayed_kernel, first, len(sources)),
+        functools.partial(relayed_kernel, first, turns, head),
         out_shape=[half, half],
         in_specs=[SMEM] + [VMEM] * (3 + len(sources)),
         out_specs=[VMEM, VMEM],
@@ -283,60 +336,21 @@
     )
 
 
-def pack_kernel(meta, own, other, out):
-    half = own.shape[0] // 2
-
-    @pl.when(meta[PLACE, 1] == 0)
-    def _():
-        out[:half] = own[:half]
-
-    @pl.when(meta[PLACE, 1] == 1)
-    def _():
-        out[:half] = own[half:]
-
-    out[half:] = other[...]
-
-
-def pack(meta, own, other):
-    rows, width = own.shape
-    return pl.pallas_call(
-        pack_kernel,
-        out_shape=pltpu.VMEM((rows // 2 + rows, width), own.dtype),
-        in_specs=[SMEM] + [VMEM] * 2,
-        out_specs=VMEM,
-        compiler_params=SMALL,
-        name="pack",
-    )(table(meta), held(own), held(other))
-
-
-def fresh_kernel(turn, meta, tiles, source, acc, out):
+def fresh_kernel(number, meta, tiles, source, acc, out):
     out[...] = acc[...]
-    half = tiles.shape[2] // 2
-    core = meta[PLACE, 1]
-
-    def add(left, right):
-        out[...] += jnp.dot(left, right, preferred_element_type=jnp.float32)
 
     @pl.loop(0, tiles.shape[0])
     def _(p):
-        news = meta[NEWS, p]
-
-        @pl.when(jnp.logical_and(news == 2 * turn, core == 0))
+        @pl.when(meta[NEWS, p] == number)
         def _():
-            add(tiles[p, :, :half], source[:half])
-
-        @pl.when(jnp.logical_and(news == 2 * turn, core == 1))
-        def _():
-            add(tiles[p, :, half:], source[:half])
-
-        @pl.when(news == 2 * turn + 1)
-        def _():
-            add(tiles[p], source[half:])
-
-
-def fresh_part(meta, tiles, source, turn, acc):
-    return pl.pallas_call(
-        functools.partial(fresh_kernel, turn),
+            out[...] += jnp.dot(
+                tiles[p], source[...], preferred_element_type=jnp.float32
+            )
+
+
+def fresh_part(meta, tiles, source, number, acc):
+    return pl.pallas_call(
+        functools.partial(fresh_kernel, number),
         out_shape=pltpu.VMEM(acc.shape, acc.dtype),
         in_specs=[SMEM] + [VMEM] * 3,
         out_specs=VMEM,
@@ -360,7 +374,7 @@
         for scenario in range(scenarios):
             twin = scenario ^ 1
             for c, m in enumerate(messages):
-                moves = dict(link_pairs(*m, sites, groups))
+                moves = dict(link_pairs(*m, sites, groups)) if m else {}
                 for a in range(sites * groups):
                     source = scenario * grid + 2 * a + c
                     if a in moves:
@@ -376,6 +390,18 @@
             for n, kind in enumerate(("even", "odd")):
                 slots[c][key[kind, t]] = groups + 2 * t + (n ^ c)
 
+    straight = [("own", t) for t in range(1, groups)] + [("even", 0), ("odd", 0)]
+    diagonal = [(kind, t) for t in range(1, groups) for kind in ("even", "odd")]
+    while len(diagonal) > len(straight):
+        straight.append(diagonal.pop())
+    rounds = list(itertools.zip_longest(straight, diagonal))
+    news = [[-1] * (3 * groups) for _ in range(2)]
+    news[1][key["own", 0]] = 0
+    for n, messages in enumerate(rounds):
+        for c, m in enumerate(messages):
+            if m is not None:
+                news[c][key[m]] = 1 + n
+
     planes = pl.pallas_call(
         planes_kernel,
         out_shape=pltpu.VMEM((taps + 1, rows, width), history.dtype),
@@ -386,7 +412,7 @@
         name="own_planes",
     )(far(history))
     *taps0, tiles, meta = pl.pallas_call(
-        functools.partial(table_kernel, slots, sites, groups),
+        functools.partial(table_kernel, slots, news, sites, groups),
         out_shape=[pltpu.VMEM((pairs // PIECES, rows, cols), tiles.dtype)] * PIECES
         + [pltpu.VMEM(tiles.shape, tiles.dtype), pltpu.SMEM((5, pairs), jnp.int32)],
         in_specs=[ANY] * 4,
@@ -401,16 +427,28 @@
     )(far(pair_src), far(pair_delay), far(tiles), planes)
 
     own = [planes] + [send(planes, *[("own", t)] * 2) for t in range(1, groups)]
-    partners = []
-    for x in own:
-        partners.append(send(x, ("even", 0), ("odd", 0)))
-        partners.append(send(x, ("odd", 0), ("even", 0)))
+    partners = [
+        send(planes, ("even", 0), ("odd", 0)),
+        send(planes, ("odd", 0), ("even", 0)),
+    ]
+    head = HALVES * rows // 2
+    tops = heads(partners, head)
+    relayed = []
+    for t in range(1, groups):
+        rest = tail(own[t], head)
+        relayed += [
+            send(tops, *[("own", t)] * 2),
+            send(rest, ("even", 0), ("odd", 0)),
+            send(rest, ("odd", 0), ("even", 0)),
+        ]
     pieces = [swap_cores(x) for x in taps0]
 
-    near = own + partners[:2]
+    near = own + partners
     acc = near_part(meta, tiles, near)
     extra, newest, acc = swapped_part(meta, tiles, acc, near, pieces)
-    mine0, mine1 = relayed_part(meta, tiles, extra, acc, partners[2:], groups + 2)
+    mine0, mine1 = relayed_part(
+        meta, tiles, extra, acc, relayed, head, groups + 2
+    )
 
     strike, inverse, wave = held(strike_seg[None, :]), held(inverse), held(waveform)
     current0 = pl.pallas_call(
@@ -422,10 +460,9 @@
         name="first_currents",
     )(table(meta), held(mine0), held(swap_cores(mine0)), inverse, strike, wave)
 
-    packed = pack(meta, current0, send(current0, ("even", 0), ("odd", 0)))
-    passed = [send(packed, *[("own", t)] * 2) for t in range(1, groups)]
-    for turn, block in enumerate([packed] + passed):
-        mine1 = fresh_part(meta, newest, block, turn, mine1)
+    fresh = [send(current0, *messages) for messages in rounds]
+    for number, block in enumerate([current0] + fresh):
+        mine1 = fresh_part(meta, newest, block, number, mine1)
 
     currents = pl.pallas_call(
         second_kernel,

time: 36.6 us -> 34.2 us (0.934)
  waiting for transfers between devices: 12.7 us -> 6.98 us
  starting transfers between devices: 13.1 us -> 17 us
  Pallas kernels: 10.5 us -> 9.84 us
    ppermute x7 -> x9, waiting for transfers between devices: 9.99 us -> 4.3 us  [send(): return lax.ppermute(x, ALL_AXES, pairs)]
    ppermute x7 -> x9, starting transfers between devices: 12.3 us -> 15.8 us  [send(): return lax.ppermute(x, ALL_AXES, pairs)]
    ppermute x6, starting transfers between devices: 0.79 us -> 1.22 us  [swap_cores(): return lax.ppermute(x, 'sub', [(0, 1), (1, 0)])]
    pallas_call x5 -> x8, Pallas kernels: 4.84 us -> 4.54 us  [the longest x1 2.58 us: per_device(): pl.pallas_call(functools.partial(table_kernel, slots, news, sites, groups...]
  transfers between devices with their start and end apart: 13 -> 15, of which waited for: 6 -> 7; matrix products, arithmetic and copies ran while one was open for 0% -> 0% of each run, Pallas kernels for 18% -> 19%
where the time goes in v5:
time: 34.2 us; the launch traced here: 34 us
  starting transfers between devices  17 us (50%)
  Pallas kernels  9.84 us (29%)
  waiting for transfers between devices  6.98 us (20%)
    ppermute x9, starting transfers between devices, send(): return lax.ppermute(x, ALL_AXES, pairs)  15.8 us
    ppermute x9, waiting for transfers between devices, send(): return lax.ppermute(x, ALL_AXES, pairs)  4.3 us
    ppermute x6, waiting for transfers between devices, swap_cores(): return lax.ppermute(x, 'sub', [(0, 1), (1, 0)])  2.68 us
    pallas_call x1, Pallas kernels, per_device(): pl.pallas_call(functools.partial(table_kernel, slots, news, sites, groups...  2.58 us
    pallas_call x1, Pallas kernels, near_part(): pl.pallas_call(functools.partial(near_kernel, len(sources)), out_shape=pl...  2.45 us
    ppermute x6, starting transfers between devices, swap_cores(): return lax.ppermute(x, 'sub', [(0, 1), (1, 0)])  1.22 us
    pallas_call x1, Pallas kernels, relayed_part(): pl.pallas_call(functools.partial(relayed_kernel, first, turns, head), out...  1.08 us
    pallas_call x1, Pallas kernels, per_device(): pl.pallas_call(planes_kernel, out_shape=pltpu.VMEM((taps + 1, rows, width...  0.98 us
  transfers between devices with their start and end apart: 15, of which 7 were waited for; matrix products, arithmetic and copies ran while one was open for 0% of the time, Pallas kernels for 19%

profile of v5, /device:TPU:0, one launch (start us, length us, event | category | flops | bytes accessed | tf_op | source)
XLA Modules:
  0.0 34.0 jit_solution(17901869236442427134)
XLA Ops:
  0.0 1.0 %own_planes.1.refs_3_.refs_0_ = bf16[5,256,128]{2,1,0:T(8,128)(2,1)S(1)} custom-call(bf16[9,256,128]{2,1,0:T(8,128)(2,1)} %bitcast.10), custom_call_target="tpu_custom_call" | custom-call | tf_op jit(solution)/shard_map/own_planes/pallas_call | solution.py:405
  1.0 3.0 %collective-permute-start = (bf16[5,256,128]{2,1,0:T(8,128)(2,1)S(1)}, bf16[5,256,128]{2,1,0:T(8,128)(2,1)S(1)}, u32[]{:S(2)}, u32[]{:S(2)}) collective-permute-start(bf16[5,256,128]{2,1,0:T(8,128)(2,1)S(1)} %own_planes.1.refs_3_.refs_0_), channel_id=1, source_target_pairs={{0,2},{2,0},{4,6},{6,4},{8,10},{10,8},{12,14},{14,12},{1,3},{3,1},... | collective-permute-start | bytes 983048 | tf_op jit(solution)/shard_map/ppermute | solution.py:384
  4.0 1.6 %collective-permute-start.1 = (bf16[5,256,128]{2,1,0:T(8,128)(2,1)S(1)}, bf16[5,256,128]{2,1,0:T(8,128)(2,1)S(1)}, u32[]{:S(2)}, u32[]{:S(2)}) collective-permute-start(bf16[5,256,128]{2,1,0:T(8,128)(2,1)S(1)} %own_planes.1.refs_3_.refs_0_), channel_id=1, source_target_pairs={{0,4},{2,6},{4,0},{6,2},{8,12},{10,14},{12,8},{14,10},{1,17},{3,19... | collective-permute-start | bytes 983048 | tf_op jit(solution)/shard_map/ppermute | solution.py:384
  5.6 1.5 %collective-permute-start.2 = (bf16[5,256,128]{2,1,0:T(8,128)(2,1)S(1)}, bf16[5,256,128]{2,1,0:T(8,128)(2,1)S(1)}, u32[]{:S(2)}, u32[]{:S(2)}) collective-permute-start(bf16[5,256,128]{2,1,0:T(8,128)(2,1)S(1)} %own_planes.1.refs_3_.refs_0_), channel_id=1, source_target_pairs={{0,16},{2,18},{4,8},{6,10},{8,4},{10,6},{12,28},{14,30},{1,5},{3,7... | collective-permute-start | bytes 983048 | tf_op jit(solution)/shard_map/ppermute | solution.py:384
  7.1 2.6 %table.1 = (bf16[2,256,256]{2,1,0:T(8,128)(2,1)S(1)}, bf16[2,256,256]{2,1,0:T(8,128)(2,1)S(1)}, bf16[2,256,256]{2,1,0:T(8,128)(2,1)S(1)}, bf16[2,256,256]{2,1,0:...) custom-call(s32[1,8]{1,0:T(1,128)} %refs_0_.1, s32[1,8]{1,0:T(1,128)} %refs_1_.1, ...), custom_call_target="tpu_custom_call" | custom-call | tf_op jit(solution)/shard_map/table/pallas_call | solution.py:414
  9.7 0.1 collective-permute-start.3
  9.8 0.5 %collective-permute-start.4 = (bf16[2,256,256]{2,1,0:T(8,128)(2,1)S(1)}, bf16[2,256,256]{2,1,0:T(8,128)(2,1)S(1)}, u32[]{:S(2)}, u32[]{:S(2)}) collective-permute-start(bf16[2,256,256]{2,1,0:T(8,128)(2,1)S(1)} %get-tuple-element.19), channel_id=1, source_target_pairs={{0,1},{1,0},{2,3},{3,2},{4,5},{5,4},{6,7},{7,6},{8,9},{9,8},{10,11... | collective-permute-start | bytes 786440 | tf_op jit(solution)/shard_map/ppermute | solution.py:55
  10.3 1.4 %collective-permute-done.refs_1_.source = bf16[5,256,128]{2,1,0:T(8,128)(2,1)S(1)} collective-permute-done((bf16[5,256,128]{2,1,0:T(8,128)(2,1)S(1)}, bf16[5,256,128]{2,1,0:T(8,128)(2,1)S(1)}, u32[]{:S(2)}, u32[]{:S(2)}) %collective-permute-start) | collective-permute-done | bytes 327712 | tf_op jit(solution)/shard_map/ppermute | solution.py:384
  11.7 1.9 %collective-permute-start.8 = (bf16[1152,128]{1,0:T(8,128)(2,1)S(1)}, bf16[1152,128]{1,0:T(8,128)(2,1)S(1)}, u32[]{:S(2)}, u32[]{:S(2)}) collective-permute-start(bf16[1152,128]{1,0:T(8,128)(2,1)S(1)} %tail.1), channel_id=1, source_target_pairs={{0,4},{2,6},{4,0},{6,2},{8,12},{10,14},{12,8},{14,10},{1,17},{3,19... | collective-permute-start | bytes 884744 | tf_op jit(solution)/shard_map/ppermute | solution.py:384
  13.6 1.5 %collective-permute-start.9 = (bf16[1152,128]{1,0:T(8,128)(2,1)S(1)}, bf16[1152,128]{1,0:T(8,128)(2,1)S(1)}, u32[]{:S(2)}, u32[]{:S(2)}) collective-permute-start(bf16[1152,128]{1,0:T(8,128)(2,1)S(1)} %tail.1), channel_id=1, source_target_pairs={{0,16},{2,18},{4,8},{6,10},{8,4},{10,6},{12,28},{14,30},{1,5},{3,7... | collective-permute-start | bytes 884744 | tf_op jit(solution)/shard_map/ppermute | solution.py:384
  15.2 0.5 %collective-permute-start.6 = (bf16[2,256,256]{2,1,0:T(8,128)(2,1)S(1)}, bf16[2,256,256]{2,1,0:T(8,128)(2,1)S(1)}, u32[]{:S(2)}, u32[]{:S(2)}) collective-permute-start(bf16[2,256,256]{2,1,0:T(8,128)(2,1)S(1)} %get-tuple-element.21), channel_id=1, source_target_pairs={{0,1},{1,0},{2,3},{3,2},{4,5},{5,4},{6,7},{7,6},{8,9},{9,8},{10,11... | collective-permute-start | bytes 786440 | tf_op jit(solution)/shard_map/ppermute | solution.py:55
  15.7 1.6 %collective-permute-start.7 = (bf16[256,128]{1,0:T(8,128)(2,1)S(1)}, bf16[256,128]{1,0:T(8,128)(2,1)S(1)}, u32[]{:S(2)}, u32[]{:S(2)}) collective-permute-start(bf16[256,128]{1,0:T(8,128)(2,1)S(1)} %heads.1), channel_id=1, source_target_pairs={{0,2},{2,0},{4,6},{6,4},{8,10},{10,8},{12,14},{14,12},{1,3},{3,1},... | collective-permute-start | bytes 196616 | tf_op jit(solution)/shard_map/ppermute | solution.py:384
  17.2 2.4 %near_part.1.acc = f32[256,256]{1,0:T(8,128)S(1)} custom-call(s32[5,8]{1,0:T(8,128)S(4)} %get-tuple-element.16.meta, bf16[8,4,256,256]{3,2,1,0:T(8,128)(2,1)S(1)} %get-tuple-element.17.tiles, bf16[5,256,128]{2,1,0:T(8,128)(2,1)S(1)} %own_planes.1.refs_3_.refs_0_, bf16[5,256,128]{2,1,0:T(8,128)(2,1)S(1)} %collective-permute-done.refs_1_.source, ...), custom_call_target="tpu_custom_call" | custom-call | tf_op jit(solution)/shard_map/near_part/pallas_call | solution.py:228
  19.7 0.8 %swapped_part.1 = (bf16[8,256,256]{2,1,0:T(8,128)(2,1)S(1)}, bf16[8,256,256]{2,1,0:T(8,128)(2,1)S(1)}, f32[256,256]{1,0:T(8,128)S(1)}) custom-call(s32[5,8]{1,0:T(8,128)S(4)} %get-tuple-element.16.meta, bf16[8,4,256,256]{3,2,1,0:T(8,128)(2,1)S(1)} %get-tuple-element.17.tiles, f32[256,256]{1,0:T(8,128)S(1)} %near_part.1.acc, ...), custom_call_target="tpu_custom_call" | custom-call | tf_op jit(solution)/shard_map/swapped_part/pallas_call | solution.py:147
  20.6 0.6 %collective-permute-done.8.refs_1_ = bf16[1152,128]{1,0:T(8,128)(2,1)S(1)} collective-permute-done((bf16[1152,128]{1,0:T(8,128)(2,1)S(1)}, bf16[1152,128]{1,0:T(8,128)(2,1)S(1)}, u32[]{:S(2)}, u32[]{:S(2)}) %collective-permute-start.8) | collective-permute-done | bytes 294944 | tf_op jit(solution)/shard_map/ppermute | solution.py:384
  21.2 1.1 %relayed_part.1 = (f32[256,128]{1,0:T(8,128)S(1)}, f32[256,128]{1,0:T(8,128)S(1)}) custom-call(s32[5,8]{1,0:T(8,128)S(4)} %get-tuple-element.16.meta, bf16[8,4,256,256]{3,2,1,0:T(8,128)(2,1)S(1)} %get-tuple-element.17.tiles, bf16[8,256,256]{2,1,0:T(8,128)(2,1)S(1)} %get-tuple-element.22.extra, f32[256,256]{1,0:T(8,128)S(1)} %get-tuple-element.23.acc, ...), custom_call_target="tpu_custom_call" | custom-call | tf_op jit(solution)/shard_map/relayed_part/pallas_call | solution.py:302
  22.3 0.1 collective-permute-start.10
  22.3 1.3 %collective-permute-done.10.other = f32[256,128]{1,0:T(8,128)S(1)} collective-permute-done((f32[256,128]{1,0:T(8,128)S(1)}, f32[256,128]{1,0:T(8,128)S(1)}, u32[]{:S(2)}, u32[]{:S(2)}) %collective-permute-start.10) | collective-permute-done | bytes 131104 | tf_op jit(solution)/shard_map/ppermute | solution.py:55
  23.7 0.2 first_currents.1.source.first
  23.9 1.6 %collective-permute-start.13 = (bf16[256,128]{1,0:T(8,128)(2,1)S(1)}, bf16[256,128]{1,0:T(8,128)(2,1)S(1)}, u32[]{:S(2)}, u32[]{:S(2)}) collective-permute-start(bf16[256,128]{1,0:T(8,128)(2,1)S(1)} %first_currents.1.source.first), channel_id=1, source_target_pairs={{0,2},{2,0},{4,6},{6,4},{8,10},{10,8},{12,14},{14,12},{1,7},{3,5},... | collective-permute-start | bytes 196616 | tf_op jit(solution)/shard_map/ppermute | solution.py:384
  25.4 1.6 %collective-permute-start.12 = (bf16[256,128]{1,0:T(8,128)(2,1)S(1)}, bf16[256,128]{1,0:T(8,128)(2,1)S(1)}, u32[]{:S(2)}, u32[]{:S(2)}) collective-permute-start(bf16[256,128]{1,0:T(8,128)(2,1)S(1)} %first_currents.1.source.first), channel_id=1, source_target_pairs={{0,4},{2,6},{4,0},{6,2},{8,12},{10,14},{12,8},{14,10},{1,17},{3,19... | collective-permute-start | bytes 196616 | tf_op jit(solution)/shard_map/ppermute | solution.py:384
  27.1 1.5 %collective-permute-start.11 = (bf16[256,128]{1,0:T(8,128)(2,1)S(1)}, bf16[256,128]{1,0:T(8,128)(2,1)S(1)}, u32[]{:S(2)}, u32[]{:S(2)}) collective-permute-start(bf16[256,128]{1,0:T(8,128)(2,1)S(1)} %first_currents.1.source.first), channel_id=1, source_target_pairs={{0,16},{2,18},{4,8},{6,10},{8,4},{10,6},{12,28},{14,30},{1,17},{3,... | collective-permute-start | bytes 196616 | tf_op jit(solution)/shard_map/ppermute | solution.py:384
  28.6 0.1 fresh_part.4.acc
  28.7 0.2 collective-permute-done.13.source
  28.9 0.3 fresh_part.5.acc
  29.2 0.5 %collective-permute-done.12.source = bf16[256,128]{1,0:T(8,128)(2,1)S(1)} collective-permute-done((bf16[256,128]{1,0:T(8,128)(2,1)S(1)}, bf16[256,128]{1,0:T(8,128)(2,1)S(1)}, u32[]{:S(2)}, u32[]{:S(2)}) %collective-permute-start.12) | collective-permute-done | bytes 65568 | tf_op jit(solution)/shard_map/ppermute | solution.py:384
  29.7 0.3 fresh_part.6.acc
  30.0 1.6 %collective-permute-done.11.source = bf16[256,128]{1,0:T(8,128)(2,1)S(1)} collective-permute-done((bf16[256,128]{1,0:T(8,128)(2,1)S(1)}, bf16[256,128]{1,0:T(8,128)(2,1)S(1)}, u32[]{:S(2)}, u32[]{:S(2)}) %collective-permute-start.11) | collective-permute-done | bytes 65568 | tf_op jit(solution)/shard_map/ppermute | solution.py:384
  31.6 0.1 fresh_part.7.mine
  31.7 0.1 collective-permute-start.14
  31.8 1.3 %collective-permute-done.14.other = f32[256,128]{1,0:T(8,128)S(1)} collective-permute-done((f32[256,128]{1,0:T(8,128)S(1)}, f32[256,128]{1,0:T(8,128)S(1)}, u32[]{:S(2)}, u32[]{:S(2)}) %collective-permute-start.14) | collective-permute-done | bytes 131104 | tf_op jit(solution)/shard_map/ppermute | solution.py:55
  33.2 0.9 %second_currents.1 = bf16[2,256,128]{2,1,0:T(8,128)(2,1)} custom-call(s32[5,8]{1,0:T(8,128)S(4)} %get-tuple-element.16.meta, bf16[256,128]{1,0:T(8,128)(2,1)S(1)} %first_currents.1.source.first, f32[256,128]{1,0:T(8,128)S(1)} %fresh_part.7.mine, f32[256,128]{1,0:T(8,128)S(1)} %collective-permute-done.14.other, bf16[256,256]{1,0:T(8,128)(2,1)S(1)} %bitcast.6, ...), custom_call_target="tpu_custom_call" | custom-call | tf_op jit(solution)/shard_map/second_currents/pallas_call | solution.py:467
  (17 shorter events, 0.1 us)
Async XLA Ops:
  1.0 10.7 %collective-permute-start = (bf16[5,256,128]{2,1,0:T(8,128)(2,1)S(1)}, bf16[5,256,128]{2,1,0:T(8,128)(2,1)S(1)}, u32[]{:S(2)}, u32[]{:S(2)}) collective-permute-start(bf16[5,256,128]{2,1,0:T(8,128)(2,1)S(1)} %own_planes.1.refs_3_.refs_0_), channel_id=1, source_target_pairs={{0,2},{2,0},{4,6},{6,4},{8,10},{10,8},{12,14},{14,12},{1,3},{3,1},... | collective-permute-start | bytes 983048 | tf_op jit(solution)/shard_map/ppermute | solution.py:384
  4.0 11.2 %collective-permute-start.1 = (bf16[5,256,128]{2,1,0:T(8,128)(2,1)S(1)}, bf16[5,256,128]{2,1,0:T(8,128)(2,1)S(1)}, u32[]{:S(2)}, u32[]{:S(2)}) collective-permute-start(bf16[5,256,128]{2,1,0:T(8,128)(2,1)S(1)} %own_planes.1.refs_3_.refs_0_), channel_id=1, source_target_pairs={{0,4},{2,6},{4,0},{6,2},{8,12},{10,14},{12,8},{14,10},{1,17},{3,19... | collective-permute-start | bytes 983048 | tf_op jit(solution)/shard_map/ppermute | solution.py:384
  5.6 9.6 %collective-permute-start.2 = (bf16[5,256,128]{2,1,0:T(8,128)(2,1)S(1)}, bf16[5,256,128]{2,1,0:T(8,128)(2,1)S(1)}, u32[]{:S(2)}, u32[]{:S(2)}) collective-permute-start(bf16[5,256,128]{2,1,0:T(8,128)(2,1)S(1)} %own_planes.1.refs_3_.refs_0_), channel_id=1, source_target_pairs={{0,16},{2,18},{4,8},{6,10},{8,4},{10,6},{12,28},{14,30},{1,5},{3,7... | collective-permute-start | bytes 983048 | tf_op jit(solution)/shard_map/ppermute | solution.py:384
  9.7 3.9 %collective-permute-start.3 = (bf16[2,256,256]{2,1,0:T(8,128)(2,1)S(1)}, bf16[2,256,256]{2,1,0:T(8,128)(2,1)S(1)}, u32[]{:S(2)}, u32[]{:S(2)}) collective-permute-start(bf16[2,256,256]{2,1,0:T(8,128)(2,1)S(1)} %get-tuple-element.18), channel_id=1, source_target_pairs={{0,1},{1,0},{2,3},{3,2},{4,5},{5,4},{6,7},{7,6},{8,9},{9,8},{10,11... | collective-permute-start | bytes 786440 | tf_op jit(solution)/shard_map/ppermute | solution.py:55
  9.8 5.9 %collective-permute-start.4 = (bf16[2,256,256]{2,1,0:T(8,128)(2,1)S(1)}, bf16[2,256,256]{2,1,0:T(8,128)(2,1)S(1)}, u32[]{:S(2)}, u32[]{:S(2)}) collective-permute-start(bf16[2,256,256]{2,1,0:T(8,128)(2,1)S(1)} %get-tuple-element.19), channel_id=1, source_target_pairs={{0,1},{1,0},{2,3},{3,2},{4,5},{5,4},{6,7},{7,6},{8,9},{9,8},{10,11... | collective-permute-start | bytes 786440 | tf_op jit(solution)/shard_map/ppermute | solution.py:55
  11.7 9.4 %collective-permute-start.8 = (bf16[1152,128]{1,0:T(8,128)(2,1)S(1)}, bf16[1152,128]{1,0:T(8,128)(2,1)S(1)}, u32[]{:S(2)}, u32[]{:S(2)}) collective-permute-start(bf16[1152,128]{1,0:T(8,128)(2,1)S(1)} %tail.1), channel_id=1, source_target_pairs={{0,4},{2,6},{4,0},{6,2},{8,12},{10,14},{12,8},{14,10},{1,17},{3,19... | collective-permute-start | bytes 884744 | tf_op jit(solution)/shard_map/ppermute | solution.py:384
  13.6 7.5 %collective-permute-start.9 = (bf16[1152,128]{1,0:T(8,128)(2,1)S(1)}, bf16[1152,128]{1,0:T(8,128)(2,1)S(1)}, u32[]{:S(2)}, u32[]{:S(2)}) collective-permute-start(bf16[1152,128]{1,0:T(8,128)(2,1)S(1)} %tail.1), channel_id=1, source_target_pairs={{0,16},{2,18},{4,8},{6,10},{8,4},{10,6},{12,28},{14,30},{1,5},{3,7... | collective-permute-start | bytes 884744 | tf_op jit(solution)/shard_map/ppermute | solution.py:384
  15.1 4.5 %collective-permute-start.5 = (bf16[2,256,256]{2,1,0:T(8,128)(2,1)S(1)}, bf16[2,256,256]{2,1,0:T(8,128)(2,1)S(1)}, u32[]{:S(2)}, u32[]{:S(2)}) collective-permute-start(bf16[2,256,256]{2,1,0:T(8,128)(2,1)S(1)} %get-tuple-element.20), channel_id=1, source_target_pairs={{0,1},{1,0},{2,3},{3,2},{4,5},{5,4},{6,7},{7,6},{8,9},{9,8},{10,11... | collective-permute-start | bytes 786440 | tf_op jit(solution)/shard_map/ppermute | solution.py:55
  15.2 4.5 %collective-permute-start.6 = (bf16[2,256,256]{2,1,0:T(8,128)(2,1)S(1)}, bf16[2,256,256]{2,1,0:T(8,128)(2,1)S(1)}, u32[]{:S(2)}, u32[]{:S(2)}) collective-permute-start(bf16[2,256,256]{2,1,0:T(8,128)(2,1)S(1)} %get-tuple-element.21), channel_id=1, source_target_pairs={{0,1},{1,0},{2,3},{3,2},{4,5},{5,4},{6,7},{7,6},{8,9},{9,8},{10,11... | collective-permute-start | bytes 786440 | tf_op jit(solution)/shard_map/ppermute | solution.py:55
  15.7 4.9 %collective-permute-start.7 = (bf16[256,128]{1,0:T(8,128)(2,1)S(1)}, bf16[256,128]{1,0:T(8,128)(2,1)S(1)}, u32[]{:S(2)}, u32[]{:S(2)}) collective-permute-start(bf16[256,128]{1,0:T(8,128)(2,1)S(1)} %heads.1), channel_id=1, source_target_pairs={{0,2},{2,0},{4,6},{6,4},{8,10},{10,8},{12,14},{14,12},{1,3},{3,1},... | collective-permute-start | bytes 196616 | tf_op jit(solution)/shard_map/ppermute | solution.py:384
  20.5 3.1 %copy-start = (bf16[1,256,256]{2,1,0:T(8,128)(2,1)S(1)}, bf16[1,256,256]{2,1,0:T(8,128)(2,1)}, u32[]{:S(2)}) copy-start(bf16[1,256,256]{2,1,0:T(8,128)(2,1)} %param.9) | copy-start | bytes 393220
  20.6 3.1 %copy-start.1 = (f32[2,128]{1,0:T(2,128)S(1)}, f32[2,128]{1,0:T(2,128)}, u32[]{:S(2)}) copy-start(f32[2,128]{1,0:T(2,128)} %wave.3) | copy-start | bytes 3076
  20.6 3.1 %copy-start.2 = (s32[128]{0:T(128)S(1)}, s32[128]{0:T(128)}, u32[]{:S(2)}) copy-start(s32[128]{0:T(128)} %param.12) | copy-start | bytes 1540
  22.3 1.4 %collective-permute-start.10 = (f32[256,128]{1,0:T(8,128)S(1)}, f32[256,128]{1,0:T(8,128)S(1)}, u32[]{:S(2)}, u32[]{:S(2)}) collective-permute-start(f32[256,128]{1,0:T(8,128)S(1)} %get-tuple-element.24.mine), channel_id=1, source_target_pairs={{0,1},{1,0},{2,3},{3,2},{4,5},{5,4},{6,7},{7,6},{8,9},{9,8},{10,11... | collective-permute-start | bytes 393224 | tf_op jit(solution)/shard_map/ppermute | solution.py:55
  23.9 5.0 %collective-permute-start.13 = (bf16[256,128]{1,0:T(8,128)(2,1)S(1)}, bf16[256,128]{1,0:T(8,128)(2,1)S(1)}, u32[]{:S(2)}, u32[]{:S(2)}) collective-permute-start(bf16[256,128]{1,0:T(8,128)(2,1)S(1)} %first_currents.1.source.first), channel_id=1, source_target_pairs={{0,2},{2,0},{4,6},{6,4},{8,10},{10,8},{12,14},{14,12},{1,7},{3,5},... | collective-permute-start | bytes 196616 | tf_op jit(solution)/shard_map/ppermute | solution.py:384
  25.4 4.3 %collective-permute-start.12 = (bf16[256,128]{1,0:T(8,128)(2,1)S(1)}, bf16[256,128]{1,0:T(8,128)(2,1)S(1)}, u32[]{:S(2)}, u32[]{:S(2)}) collective-permute-start(bf16[256,128]{1,0:T(8,128)(2,1)S(1)} %first_currents.1.source.first), channel_id=1, source_target_pairs={{0,4},{2,6},{4,0},{6,2},{8,12},{10,14},{12,8},{14,10},{1,17},{3,19... | collective-permute-start | bytes 196616 | tf_op jit(solution)/shard_map/ppermute | solution.py:384
  27.1 4.5 %collective-permute-start.11 = (bf16[256,128]{1,0:T(8,128)(2,1)S(1)}, bf16[256,128]{1,0:T(8,128)(2,1)S(1)}, u32[]{:S(2)}, u32[]{:S(2)}) collective-permute-start(bf16[256,128]{1,0:T(8,128)(2,1)S(1)} %first_currents.1.source.first), channel_id=1, source_target_pairs={{0,16},{2,18},{4,8},{6,10},{8,4},{10,6},{12,28},{14,30},{1,17},{3,... | collective-permute-start | bytes 196616 | tf_op jit(solution)/shard_map/ppermute | solution.py:384
  31.7 1.4 %collective-permute-start.14 = (f32[256,128]{1,0:T(8,128)S(1)}, f32[256,128]{1,0:T(8,128)S(1)}, u32[]{:S(2)}, u32[]{:S(2)}) collective-permute-start(f32[256,128]{1,0:T(8,128)S(1)} %fresh_part.7.mine), channel_id=1, source_target_pairs={{0,1},{1,0},{2,3},{3,2},{4,5},{5,4},{6,7},{7,6},{8,9},{9,8},{10,11... | collective-permute-start | bytes 393224 | tf_op jit(solution)/shard_map/ppermute | solution.py:55

commit v6 on v5

--- a/solution.py
+++ b/solution.py
@@ -18,7 +18,6 @@
 SLOT, LATE, NEWS, ORDER, PLACE = range(5)
 CHUNK = 4
 PIECES = 4
-HALVES = 1
 
 
 def held(x):
@@ -57,32 +56,52 @@
 
 def planes_kernel(history, planes, sem):
     core = lax.axis_index("sub")
-    count = planes.shape[0]
-    copy = pltpu.make_async_copy(
-        history.at[pl.ds(core * (count - 1), count)], planes, sem
-    )
-    copy.start()
-    copy.wait()
+    count, rows, _ = history.shape
+    taps, half = count // 2, rows // 2
+    copies = [
+        pltpu.make_async_copy(
+            history.at[core * taps + n], planes.at[pl.ds(n * rows, rows)], sem.at[n]
+        )
+        for n in range(taps)
+    ]
+    copies.append(
+        pltpu.make_async_copy(
+            history.at[count - 1, pl.ds(core * half, half)],
+            planes.at[pl.ds(taps * rows, half)],
+            sem.at[taps],
+        )
+    )
+    for copy in copies:
+        copy.start()
+    for copy in copies:
+        copy.wait()
 
 
 def table_kernel(slots, news, sites, groups, *refs):
     src, delay, tiles, after = refs[:4]
-    *taps, whole, meta, src_buf, delay_buf, sem = refs[4:]
-    part = taps[0].shape[0]
+    *ends, whole, meta, src_buf, delay_buf, sem = refs[4:]
+    part = ends[0].shape[0]
     site, member, core = (lax.axis_index(a) for a in GRID_AXES)
     rows = tiles.shape[2]
     copies = [
         pltpu.make_async_copy(src, src_buf, sem.at[0]),
         pltpu.make_async_copy(delay, delay_buf, sem.at[1]),
-    ] + [
-        pltpu.make_async_copy(tiles.at[pl.ds(n * part, part), 0], out, sem.at[2 + n])
-        for n, out in enumerate(taps)
+        pltpu.make_async_copy(tiles, whole, sem.at[2]),
     ]
-    copies.append(pltpu.make_async_copy(tiles, whole, sem.at[2 + len(taps)]))
     for copy in copies:
         copy.start()
     copies[0].wait()
     copies[1].wait()
+    last = tiles.shape[1] - 1
+    for p in range(src.shape[1]):
+        copies.append(
+            pltpu.make_async_copy(
+                tiles.at[p, jnp.where(delay_buf[0, p] == 1, 0, last)],
+                ends[p // part].at[p % part],
+                sem.at[3 + p],
+            )
+        )
+        copies[-1].start()
     even_step = jnp.where(site % 2 == 0, 1, -1)
     ahead = jnp.int32(0)
     behind = jnp.int32(src.shape[1])
@@ -112,108 +131,96 @@
 
 
 def swapped_kernel(count, meta, tiles, acc, *refs):
-    sources, pieces = refs[:count], refs[count:-3]
-    extra, newest, total = refs[-3:]
+    sources, pieces = refs[:count], refs[count:-4]
+    cross, halves, newest, total = refs[-4:]
     part = pieces[0].shape[0]
-    taps = tiles.shape[1]
-    width = sources[0].shape[2]
+    taps, rows = tiles.shape[1:3]
+    half = rows // 2
     core = meta[PLACE, 1]
     total[...] = acc[...]
     for n, piece in enumerate(pieces):
-        extra[n * part : (n + 1) * part] = piece[...]
-
-    @pl.when(core == 1)
-    def _():
-        newest[...] = extra[...]
+        cross[n * part : (n + 1) * part] = piece[...]
 
     @pl.when(core == 0)
     def _():
         newest[...] = tiles[:, 0]
-
-        @pl.loop(0, tiles.shape[0])
-        def _(p):
-            for slot, source in enumerate(sources):
-                used = jnp.logical_and(meta[SLOT, p] == slot, meta[LATE, p] == 0)
-
-                @pl.when(used)
-                def _():
-                    total[:, width:] += jnp.dot(
-                        extra[p], source[taps - 1], preferred_element_type=jnp.float32
-                    )
+        halves[...] = cross[:, :, :half]
+
+    @pl.when(core == 1)
+    def _():
+        newest[...] = cross[...]
+        halves[...] = tiles[:, taps - 1, :, half:]
+
+    @pl.loop(0, tiles.shape[0])
+    def _(p):
+        for slot, source in enumerate(sources):
+            used, late = meta[SLOT, p] == slot, meta[LATE, p]
+            width = source.shape[1]
+
+            @pl.when(used & (late == 0) & (core == 0))
+            def _():
+                total[:, width:] += jnp.dot(
+                    cross[p],
+                    source[(taps - 1) * rows : taps * rows],
+                    preferred_element_type=jnp.float32,
+                )
+
+            @pl.when(used & (late == 1))
+            def _():
+                total[:, :width] += jnp.dot(
+                    halves[p],
+                    source[taps * rows :],
+                    preferred_element_type=jnp.float32,
+                )
+
+            @pl.when(used & (late == 1) & (core == 1))
+            def _():
+                total[:, :width] += jnp.dot(
+                    cross[p], source[:rows], preferred_element_type=jnp.float32
+                )
 
 
 def swapped_part(meta, tiles, acc, sources, pieces):
-    whole = pltpu.VMEM(tiles.shape[:1] + tiles.shape[2:], tiles.dtype)
+    pairs, _, rows, cols = tiles.shape
+    whole = pltpu.VMEM((pairs, rows, cols), tiles.dtype)
     return pl.pallas_call(
         functools.partial(swapped_kernel, len(sources)),
-        out_shape=[whole, whole, pltpu.VMEM(acc.shape, acc.dtype)],
+        out_shape=[
+            whole,
+            pltpu.VMEM((pairs, rows, cols // 2), tiles.dtype),
+            whole,
+            pltpu.VMEM(acc.shape, acc.dtype),
+        ],
         in_specs=[SMEM] + [VMEM] * (2 + len(sources) + len(pieces)),
-        out_specs=[VMEM] * 3,
+        out_specs=[VMEM] * 4,
         compiler_params=SMALL,
         name="swapped_part",
     )(table(meta), held(tiles), held(acc), *[held(x) for x in sources + pieces])
 
 
-def row_pieces(rows, start, stop):
-    for plane in range(start // rows, -(-stop // rows)):
-        low, high = max(start, plane * rows), min(stop, (plane + 1) * rows)
-        yield plane, low - plane * rows, high - plane * rows, low - start
-
-
-def heads_kernel(head, *refs):
-    sources, out = refs[:-1], refs[-1]
-    for n, source in enumerate(sources):
-        for plane, low, high, place in row_pieces(source.shape[1], 0, head):
-            place += n * head
-            out[place : place + high - low] = source[plane, low:high]
-
-
-def heads(sources, head):
-    width = sources[0].shape[2]
-    return pl.pallas_call(
-        functools.partial(heads_kernel, head),
-        out_shape=pltpu.VMEM((len(sources) * head, width), sources[0].dtype),
-        in_specs=[VMEM] * len(sources),
-        out_specs=VMEM,
-        compiler_params=SMALL,
-        name="heads",
-    )(*[held(x) for x in sources])
-
-
-def tail_kernel(head, source, out):
-    planes, rows, _ = source.shape
-    for plane, low, high, place in row_pieces(rows, head, planes * rows):
-        out[place : place + high - low] = source[plane, low:high]
-
-
-def tail(source, head):
-    planes, rows, width = source.shape
-    return pl.pallas_call(
-        functools.partial(tail_kernel, head),
-        out_shape=pltpu.VMEM((planes * rows - head, width), source.dtype),
-        in_specs=[VMEM],
-        out_specs=VMEM,
-        compiler_params=SMALL,
-        name="tail",
-    )(held(source))
-
-
 def near_kernel(count, meta, tiles, *refs):
     sources, (total,) = refs[:count], refs[count:]
-    taps = tiles.shape[1]
+    taps, rows = tiles.shape[1:3]
     total[...] = jnp.zeros_like(total)
 
     def one(p, source):
         late = meta[LATE, p]
-        empty = jnp.zeros(source.shape[1:], source.dtype)
-        right = jnp.where(late == 1, source[0], empty)
-        planes = []
-        for k in range(taps):
-            planes.append(jnp.concatenate([source[late + k], right], axis=1))
-            right = source[late + k]
+        planes = [source[k * rows : (k + 1) * rows] for k in range(taps)]
+        empty = jnp.zeros_like(planes[0])
+        planes = [empty] + planes + [empty]
+        both = [
+            jnp.concatenate(
+                [
+                    jnp.where(late == 1, planes[k + 2], planes[k + 1]),
+                    jnp.where(late == 1, planes[k + 1], planes[k]),
+                ],
+                axis=1,
+            )
+            for k in range(taps)
+        ]
         total[...] += jnp.dot(
             jnp.concatenate([tiles[p, k] for k in range(taps)], axis=1),
-            jnp.concatenate(planes, axis=0),
+            jnp.concatenate(both, axis=0),
             preferred_element_type=jnp.float32,
         )
 
@@ -224,7 +231,7 @@
 
 
 def near_part(meta, tiles, sources):
-    rows, width = sources[0].shape[1:]
+    rows, width = tiles.shape[2], sources[0].shape[1]
     return pl.pallas_call(
         functools.partial(near_kernel, len(sources)),
         out_shape=pltpu.VMEM((rows, 2 * width), jnp.float32),
@@ -235,57 +242,54 @@
     )(table(meta), held(tiles), *[held(x) for x in sources])
 
 
-def relayed_kernel(first, turns, head, meta, tiles, extra, acc, *refs):
-    sources, (out0, out1, total, store) = refs[: 3 * turns], refs[3 * turns :]
+def relayed_kernel(first, count, meta, tiles, cross, halves, acc, *refs):
+    sources, (out0, out1, total, store) = refs[:count], refs[count:]
     pairs, taps, rows = tiles.shape[:3]
-    planes, width = taps + 1, acc.shape[1] // 2
-    none = 2 * turns * planes
-    for turn in range(turns):
-        tops, *rests = sources[3 * turn : 3 * turn + 3]
-        for n, rest in enumerate(rests):
-            base = (2 * turn + n) * planes
-            for plane, low, high, place in row_pieces(rows, 0, head):
-                place += n * head
-                store[base + plane, low:high] = tops[place : place + high - low]
-            for plane, low, high, place in row_pieces(rows, head, planes * rows):
-                store[base + plane, low:high] = rest[place : place + high - low]
-    store[none] = jnp.zeros(store.shape[1:], store.dtype)
+    half, width = rows // 2, acc.shape[1] // 2
+    block = taps * rows + half
+    none = count * block
+    core = meta[PLACE, 1]
+    for n, source in enumerate(sources):
+        store[n * block : (n + 1) * block] = source[...]
+    store[none:] = jnp.zeros((rows, width), store.dtype)
     total[...] = acc[...]
 
+    def plane(at, count):
+        return store[pl.ds(pl.multiple_of(at, half), count)]
+
+    def pair(a, b, count):
+        return jnp.concatenate([plane(a, count), plane(b, count)], axis=1)
+
     def chunk(start):
-        numbers, left, right, swapped = [], [], [], []
+        lefts, rights = [], []
         for i in range(start, start + CHUNK):
             p = meta[ORDER, i]
             used = i < meta[PLACE, 2]
             late = meta[LATE, p]
-            base = (meta[SLOT, p] - first) * planes
-            numbers.append(p)
-            places = [jnp.where(used, base + late + k, none) for k in range(taps)]
-            before = jnp.where(jnp.logical_and(used, late == 1), base, none)
-            left += places
-            right += [before] + places[:-1]
-            swapped.append(
-                jnp.where(jnp.logical_and(used, late == 0), base + taps - 1, none)
+            base = (meta[SLOT, p] - first) * block
+            early = jnp.logical_and(used, late == 0)
+            after = jnp.logical_and(used, late == 1)
+            ats = [jnp.where(used, base + k * rows, none) for k in range(taps)]
+            before = [none] + ats + [none]
+            for k in range(taps):
+                lefts.append(tiles[p, k])
+                a = jnp.where(late == 1, before[k + 2], before[k + 1])
+                b = jnp.where(late == 1, before[k + 1], before[k])
+                rights.append(pair(a, b, rows))
+            lefts.append(cross[p])
+            a = jnp.where(jnp.logical_and(after, core == 1), base, none)
+            b = jnp.where(
+                jnp.logical_and(early, core == 0), base + (taps - 1) * rows, none
             )
+            rights.append(pair(a, b, rows))
+            lefts.append(halves[p])
+            a = jnp.where(after, base + taps * rows, none)
+            rights.append(pair(a, none, half))
         total[...] += jnp.dot(
-            jnp.concatenate([tiles[p, k] for p in numbers for k in range(taps)], axis=1),
-            jnp.concatenate(
-                [
-                    jnp.concatenate([store[a], store[b]], axis=1)
-                    for a, b in zip(left, right)
-                ],
-                axis=0,
-            ),
+            jnp.concatenate(lefts, axis=1),
+            jnp.concatenate(rights, axis=0),
             preferred_element_type=jnp.float32,
         )
-
-        @pl.when(meta[PLACE, 1] == 0)
-        def _():
-            total[:, width:] += jnp.dot(
-                jnp.concatenate([extra[p] for p in numbers], axis=1),
-                jnp.concatenate([store[a] for a in swapped], axis=0),
-                preferred_element_type=jnp.float32,
-            )
 
     for start in range(0, pairs, CHUNK):
         pl.when(meta[PLACE, 2] > start)(functools.partial(chunk, start))
@@ -293,16 +297,16 @@
     out1[...] = total[:, width:]
 
 
-def relayed_part(meta, tiles, extra, acc, sources, head, first):
+def relayed_part(meta, tiles, cross, halves, acc, sources, first):
     taps, rows = tiles.shape[1:3]
-    width, turns = acc.shape[1] // 2, len(sources) // 3
-    store = (2 * turns * (taps + 1) + 1, rows, width)
+    width, count = acc.shape[1] // 2, len(sources)
+    store = (count * (taps * rows + rows // 2) + rows, width)
     half = pltpu.VMEM((rows, width), jnp.float32)
-    room = 2 * store[0] * rows * width + 4 * acc.size
+    room = 2 * store[0] * width + 4 * acc.size
     return pl.pallas_call(
-        functools.partial(relayed_kernel, first, turns, head),
+        functools.partial(relayed_kernel, first, count),
         out_shape=[half, half],
-        in_specs=[SMEM] + [VMEM] * (3 + len(sources)),
+        in_specs=[SMEM] + [VMEM] * (4 + len(sources)),
         out_specs=[VMEM, VMEM],
         scratch_shapes=[
             pltpu.VMEM(acc.shape, acc.dtype),
@@ -310,7 +314,14 @@
         ],
         compiler_params=pltpu.CompilerParams(vmem_limit_bytes=room + (4 << 20)),
         name="relayed_part",
-    )(table(meta), held(tiles), held(extra), held(acc), *[held(x) for x in sources])
+    )(
+        table(meta),
+        held(tiles),
+        held(cross),
+        held(halves),
+        held(acc),
+        *[held(x) for x in sources],
+    )
 
 
 def solve_rows(base, mine, other, inverse, strike, wave):
@@ -404,14 +415,14 @@
 
     planes = pl.pallas_call(
         planes_kernel,
-        out_shape=pltpu.VMEM((taps + 1, rows, width), history.dtype),
+        out_shape=pltpu.VMEM((taps * rows + rows // 2, width), history.dtype),
         in_specs=[ANY],
         out_specs=VMEM,
-        scratch_shapes=[pltpu.SemaphoreType.DMA],
+        scratch_shapes=[pltpu.SemaphoreType.DMA((taps + 1,))],
         compiler_params=SMALL,
         name="own_planes",
     )(far(history))
-    *taps0, tiles, meta = pl.pallas_call(
+    *ends, tiles, meta = pl.pallas_call(
         functools.partial(table_kernel, slots, news, sites, groups),
         out_shape=[pltpu.VMEM((pairs // PIECES, rows, cols), tiles.dtype)] * PIECES
         + [pltpu.VMEM(tiles.shape, tiles.dtype), pltpu.SMEM((5, pairs), jnp.int32)],
@@ -420,7 +431,7 @@
         scratch_shapes=[
             pltpu.SMEM((1, pairs), jnp.int32),
             pltpu.SMEM((1, pairs), jnp.int32),
-            pltpu.SemaphoreType.DMA((3 + PIECES,)),
+            pltpu.SemaphoreType.DMA((3 + pairs,)),
         ],
         compiler_params=SMALL,
         name="table",
@@ -431,23 +442,17 @@
         send(planes, ("even", 0), ("odd", 0)),
         send(planes, ("odd", 0), ("even", 0)),
     ]
-    head = HALVES * rows // 2
-    tops = heads(partners, head)
     relayed = []
-    for t in range(1, groups):
-        rest = tail(own[t], head)
-        relayed += [
-            send(tops, *[("own", t)] * 2),
-            send(rest, ("even", 0), ("odd", 0)),
-            send(rest, ("odd", 0), ("even", 0)),
-        ]
-    pieces = [swap_cores(x) for x in taps0]
+    for x in own[1:]:
+        relayed.append(send(x, ("even", 0), ("odd", 0)))
+        relayed.append(send(x, ("odd", 0), ("even", 0)))
+    pieces = [swap_cores(x) for x in ends]
 
     near = own + partners
     acc = near_part(meta, tiles, near)
-    extra, newest, acc = swapped_part(meta, tiles, acc, near, pieces)
+    cross, halves, newest, acc = swapped_part(meta, tiles, acc, near, pieces)
     mine0, mine1 = relayed_part(
-        meta, tiles, extra, acc, relayed, head, groups + 2
+        meta, tiles, cross, halves, acc, relayed, groups + 2
     )
 
     strike, inverse, wave = held(strike_seg[None, :]), held(inverse), held(waveform)

time: 34.2 us -> 33.8 us (0.988); the launches traced: 34 us -> 34.1 us
  starting transfers between devices: 17 us -> 15.9 us
  Pallas kernels: 9.84 us -> 10.6 us
  waiting for transfers between devices: 6.98 us -> 7.36 us
    pallas_call x1, Pallas kernels: 0.84 us -> 1.92 us  [swapped_part(): pl.pallas_call(functools.partial(swapped_kernel, len(sources)), out_shape...]
    ppermute x9 -> x8, starting transfers between devices: 15.8 us -> 15.1 us  [send(): return lax.ppermute(x, ALL_AXES, pairs)]
    ppermute x6, starting transfers between devices: 1.22 us -> 0.79 us  [swap_cores(): return lax.ppermute(x, 'sub', [(0, 1), (1, 0)])]
    ppermute x9 -> x8, waiting for transfers between devices: 4.3 us -> 4.68 us  [send(): return lax.ppermute(x, ALL_AXES, pairs)]
    pallas_call x4 -> x2, Pallas kernels: 2.08 us -> 1.99 us  [the longest x1 1.02 us: relayed_part(): pl.pallas_call(functools.partial(relayed_kernel, first, count), out_shape...]
  transfers between devices with their start and end apart: 15 -> 14, of which waited for: 7 -> 6; matrix products, arithmetic and copies ran while one was open for 0% -> 0% of each run, Pallas kernels for 19% -> 22%
where the time goes in v6:
time: 33.8 us; the launch traced here: 34.1 us
  starting transfers between devices  15.9 us (47%)
  Pallas kernels  10.6 us (31%)
  waiting for transfers between devices  7.36 us (22%)
    ppermute x8, starting transfers between devices, send(): return lax.ppermute(x, ALL_AXES, pairs)  15.1 us
    ppermute x8, waiting for transfers between devices, send(): return lax.ppermute(x, ALL_AXES, pairs)  4.68 us
    ppermute x6, waiting for transfers between devices, swap_cores(): return lax.ppermute(x, 'sub', [(0, 1), (1, 0)])  2.68 us
    pallas_call x1, Pallas kernels, per_device(): pl.pallas_call(functools.partial(table_kernel, slots, news, sites, groups...  2.68 us
    pallas_call x1, Pallas kernels, near_part(): pl.pallas_call(functools.partial(near_kernel, len(sources)), out_shape=pl...  2.16 us
    pallas_call x1, Pallas kernels, swapped_part(): pl.pallas_call(functools.partial(swapped_kernel, len(sources)), out_shape...  1.92 us
    pallas_call x1, Pallas kernels, relayed_part(): pl.pallas_call(functools.partial(relayed_kernel, first, count), out_shape...  1.02 us
    pallas_call x1, Pallas kernels, per_device(): pl.pallas_call(planes_kernel, out_shape=pltpu.VMEM((taps * rows + rows //...  0.98 us
  transfers between devices with their start and end apart: 14, of which 6 were waited for; matrix products, arithmetic and copies ran while one was open for 0% of the time, Pallas kernels for 22%

profile of v6, /device:TPU:0, one launch (start us, length us, event | category | flops | bytes accessed | tf_op | source)
XLA Modules:
  0.0 34.1 jit_solution(17432568338921204749)
XLA Ops:
  0.0 1.0 %own_planes.1.refs_3_.refs_0_ = bf16[1152,128]{1,0:T(8,128)(2,1)S(1)} custom-call(bf16[9,256,128]{2,1,0:T(8,128)(2,1)} %bitcast.10), custom_call_target="tpu_custom_call" | custom-call | tf_op jit(solution)/shard_map/own_planes/pallas_call | solution.py:416
  1.0 3.0 %collective-permute-start = (bf16[1152,128]{1,0:T(8,128)(2,1)S(1)}, bf16[1152,128]{1,0:T(8,128)(2,1)S(1)}, u32[]{:S(2)}, u32[]{:S(2)}) collective-permute-start(bf16[1152,128]{1,0:T(8,128)(2,1)S(1)} %own_planes.1.refs_3_.refs_0_), channel_id=1, source_target_pairs={{0,2},{2,0},{4,6},{6,4},{8,10},{10,8},{12,14},{14,12},{1,3},{3,1},... | collective-permute-start | bytes 884744 | tf_op jit(solution)/shard_map/ppermute | solution.py:395
  4.0 1.6 %collective-permute-start.1 = (bf16[1152,128]{1,0:T(8,128)(2,1)S(1)}, bf16[1152,128]{1,0:T(8,128)(2,1)S(1)}, u32[]{:S(2)}, u32[]{:S(2)}) collective-permute-start(bf16[1152,128]{1,0:T(8,128)(2,1)S(1)} %own_planes.1.refs_3_.refs_0_), channel_id=1, source_target_pairs={{0,4},{2,6},{4,0},{6,2},{8,12},{10,14},{12,8},{14,10},{1,17},{3,19... | collective-permute-start | bytes 884744 | tf_op jit(solution)/shard_map/ppermute | solution.py:395
  5.6 1.5 %collective-permute-start.2 = (bf16[1152,128]{1,0:T(8,128)(2,1)S(1)}, bf16[1152,128]{1,0:T(8,128)(2,1)S(1)}, u32[]{:S(2)}, u32[]{:S(2)}) collective-permute-start(bf16[1152,128]{1,0:T(8,128)(2,1)S(1)} %own_planes.1.refs_3_.refs_0_), channel_id=1, source_target_pairs={{0,16},{2,18},{4,8},{6,10},{8,4},{10,6},{12,28},{14,30},{1,5},{3,7... | collective-permute-start | bytes 884744 | tf_op jit(solution)/shard_map/ppermute | solution.py:395
  7.1 2.7 %table.1 = (bf16[2,256,256]{2,1,0:T(8,128)(2,1)S(1)}, bf16[2,256,256]{2,1,0:T(8,128)(2,1)S(1)}, bf16[2,256,256]{2,1,0:T(8,128)(2,1)S(1)}, bf16[2,256,256]{2,1,0:...) custom-call(s32[1,8]{1,0:T(1,128)} %refs_0_.1, s32[1,8]{1,0:T(1,128)} %refs_1_.1, ...), custom_call_target="tpu_custom_call" | custom-call | tf_op jit(solution)/shard_map/table/pallas_call | solution.py:425
  9.8 0.1 collective-permute-start.3
  9.8 1.1 %collective-permute-done.refs_1_ = bf16[1152,128]{1,0:T(8,128)(2,1)S(1)} collective-permute-done((bf16[1152,128]{1,0:T(8,128)(2,1)S(1)}, bf16[1152,128]{1,0:T(8,128)(2,1)S(1)}, u32[]{:S(2)}, u32[]{:S(2)}) %collective-permute-start) | collective-permute-done | bytes 294944 | tf_op jit(solution)/shard_map/ppermute | solution.py:395
  11.0 1.8 %collective-permute-start.7 = (bf16[1152,128]{1,0:T(8,128)(2,1)S(1)}, bf16[1152,128]{1,0:T(8,128)(2,1)S(1)}, u32[]{:S(2)}, u32[]{:S(2)}) collective-permute-start(bf16[1152,128]{1,0:T(8,128)(2,1)S(1)} %collective-permute-done.refs_1_), channel_id=1, source_target_pairs={{0,4},{2,6},{4,0},{6,2},{8,12},{10,14},{12,8},{14,10},{1,17},{3,19... | collective-permute-start | bytes 884744 | tf_op jit(solution)/shard_map/ppermute | solution.py:395
  12.8 1.5 %collective-permute-start.8 = (bf16[1152,128]{1,0:T(8,128)(2,1)S(1)}, bf16[1152,128]{1,0:T(8,128)(2,1)S(1)}, u32[]{:S(2)}, u32[]{:S(2)}) collective-permute-start(bf16[1152,128]{1,0:T(8,128)(2,1)S(1)} %collective-permute-done.refs_1_), channel_id=1, source_target_pairs={{0,16},{2,18},{4,8},{6,10},{8,4},{10,6},{12,28},{14,30},{1,5},{3,7... | collective-permute-start | bytes 884744 | tf_op jit(solution)/shard_map/ppermute | solution.py:395
  14.4 0.5 %collective-permute-start.5 = (bf16[2,256,256]{2,1,0:T(8,128)(2,1)S(1)}, bf16[2,256,256]{2,1,0:T(8,128)(2,1)S(1)}, u32[]{:S(2)}, u32[]{:S(2)}) collective-permute-start(bf16[2,256,256]{2,1,0:T(8,128)(2,1)S(1)} %get-tuple-element.21), channel_id=1, source_target_pairs={{0,1},{1,0},{2,3},{3,2},{4,5},{5,4},{6,7},{7,6},{8,9},{9,8},{10,11... | collective-permute-start | bytes 786440 | tf_op jit(solution)/shard_map/ppermute | solution.py:54
  14.9 0.1 collective-permute-start.6
  14.9 2.2 %near_part.1.acc = f32[256,256]{1,0:T(8,128)S(1)} custom-call(s32[5,8]{1,0:T(8,128)S(4)} %get-tuple-element.17.meta, bf16[8,4,256,256]{3,2,1,0:T(8,128)(2,1)S(1)} %get-tuple-element.18.tiles, bf16[1152,128]{1,0:T(8,128)(2,1)S(1)} %own_planes.1.refs_3_.refs_0_, bf16[1152,128]{1,0:T(8,128)(2,1)S(1)} %collective-permute-done.refs_1_, ...), custom_call_target="tpu_custom_call" | custom-call | tf_op jit(solution)/shard_map/near_part/pallas_call | solution.py:235
  17.1 1.9 %swapped_part.1 = (bf16[8,256,256]{2,1,0:T(8,128)(2,1)S(1)}, bf16[8,256,128]{2,1,0:T(8,128)(2,1)S(1)}, bf16[8,256,256]{2,1,0:T(8,128)(2,1)S(1)}, f32[256,256]{1,0:T(8,128)S(1)}) custom-call(s32[5,8]{1,0:T(8,128)S(4)} %get-tuple-element.17.meta, bf16[8,4,256,256]{3,2,1,0:T(8,128)(2,1)S(1)} %get-tuple-element.18.tiles, f32[256,256]{1,0:T(8,128)S(1)} %near_part.1.acc, ...), custom_call_target="tpu_custom_call" | custom-call | tf_op jit(solution)/shard_map/swapped_part/pallas_call | solution.py:186
  19.1 0.0 copy-start.1
  19.1 0.0 copy-start.2
  19.1 1.3 %collective-permute-done.7.refs_0_ = bf16[1152,128]{1,0:T(8,128)(2,1)S(1)} collective-permute-done((bf16[1152,128]{1,0:T(8,128)(2,1)S(1)}, bf16[1152,128]{1,0:T(8,128)(2,1)S(1)}, u32[]{:S(2)}, u32[]{:S(2)}) %collective-permute-start.7) | collective-permute-done | bytes 294944 | tf_op jit(solution)/shard_map/ppermute | solution.py:395
  20.4 1.0 %relayed_part.1 = (f32[256,128]{1,0:T(8,128)S(1)}, f32[256,128]{1,0:T(8,128)S(1)}) custom-call(s32[5,8]{1,0:T(8,128)S(4)} %get-tuple-element.17.meta, bf16[8,4,256,256]{3,2,1,0:T(8,128)(2,1)S(1)} %get-tuple-element.18.tiles, bf16[8,256,256]{2,1,0:T(8,128)(2,1)S(1)} %get-tuple-element.23.cross, bf16[8,256,128]{2,1,0:T(8,128)(2,1)S(1)} %get-tuple-element.24.halves, ...), custom_call_target="tpu_custom_call" | custom-call | tf_op jit(solution)/shard_map/relayed_part/pallas_call | solution.py:306
  21.4 0.1 collective-permute-start.9
  21.5 1.3 %collective-permute-done.9.other = f32[256,128]{1,0:T(8,128)S(1)} collective-permute-done((f32[256,128]{1,0:T(8,128)S(1)}, f32[256,128]{1,0:T(8,128)S(1)}, u32[]{:S(2)}, u32[]{:S(2)}) %collective-permute-start.9) | collective-permute-done | bytes 131104 | tf_op jit(solution)/shard_map/ppermute | solution.py:54
  22.8 0.2 first_currents.1.source.first
  23.0 1.6 %collective-permute-start.12 = (bf16[256,128]{1,0:T(8,128)(2,1)S(1)}, bf16[256,128]{1,0:T(8,128)(2,1)S(1)}, u32[]{:S(2)}, u32[]{:S(2)}) collective-permute-start(bf16[256,128]{1,0:T(8,128)(2,1)S(1)} %first_currents.1.source.first), channel_id=1, source_target_pairs={{0,2},{2,0},{4,6},{6,4},{8,10},{10,8},{12,14},{14,12},{1,7},{3,5},... | collective-permute-start | bytes 196616 | tf_op jit(solution)/shard_map/ppermute | solution.py:395
  24.6 2.6 %collective-permute-start.11 = (bf16[256,128]{1,0:T(8,128)(2,1)S(1)}, bf16[256,128]{1,0:T(8,128)(2,1)S(1)}, u32[]{:S(2)}, u32[]{:S(2)}) collective-permute-start(bf16[256,128]{1,0:T(8,128)(2,1)S(1)} %first_currents.1.source.first), channel_id=1, source_target_pairs={{0,4},{2,6},{4,0},{6,2},{8,12},{10,14},{12,8},{14,10},{1,17},{3,19... | collective-permute-start | bytes 196616 | tf_op jit(solution)/shard_map/ppermute | solution.py:395
  27.1 1.5 %collective-permute-start.10 = (bf16[256,128]{1,0:T(8,128)(2,1)S(1)}, bf16[256,128]{1,0:T(8,128)(2,1)S(1)}, u32[]{:S(2)}, u32[]{:S(2)}) collective-permute-start(bf16[256,128]{1,0:T(8,128)(2,1)S(1)} %first_currents.1.source.first), channel_id=1, source_target_pairs={{0,16},{2,18},{4,8},{6,10},{8,4},{10,6},{12,28},{14,30},{1,17},{3,... | collective-permute-start | bytes 196616 | tf_op jit(solution)/shard_map/ppermute | solution.py:395
  28.6 0.1 fresh_part.4.acc
  28.8 0.5 %fresh_part.5.acc = f32[256,128]{1,0:T(8,128)S(1)} custom-call(s32[5,8]{1,0:T(8,128)S(4)} %get-tuple-element.17.meta, bf16[8,256,256]{2,1,0:T(8,128)(2,1)S(1)} %get-tuple-element.27.tiles, bf16[256,128]{1,0:T(8,128)(2,1)S(1)} %collective-permute-done.12.source, f32[256,128]{1,0:T(8,128)S(1)} %fresh_part.4.acc), custom_call_target="tpu_custom_call" | custom-call | tf_op jit(solution)/shard_map/fresh_part/pallas_call | solution.py:363
  29.3 0.1 collective-permute-done.11.source
  29.4 0.1 fresh_part.6.acc
  29.5 2.1 %collective-permute-done.10.source = bf16[256,128]{1,0:T(8,128)(2,1)S(1)} collective-permute-done((bf16[256,128]{1,0:T(8,128)(2,1)S(1)}, bf16[256,128]{1,0:T(8,128)(2,1)S(1)}, u32[]{:S(2)}, u32[]{:S(2)}) %collective-permute-start.10) | collective-permute-done | bytes 65568 | tf_op jit(solution)/shard_map/ppermute | solution.py:395
  31.7 0.1 fresh_part.7.mine
  31.8 0.1 collective-permute-start.13
  31.9 1.3 %collective-permute-done.13.other = f32[256,128]{1,0:T(8,128)S(1)} collective-permute-done((f32[256,128]{1,0:T(8,128)S(1)}, f32[256,128]{1,0:T(8,128)S(1)}, u32[]{:S(2)}, u32[]{:S(2)}) %collective-permute-start.13) | collective-permute-done | bytes 131104 | tf_op jit(solution)/shard_map/ppermute | solution.py:54
  33.2 0.9 %second_currents.1 = bf16[2,256,128]{2,1,0:T(8,128)(2,1)} custom-call(s32[5,8]{1,0:T(8,128)S(4)} %get-tuple-element.17.meta, bf16[256,128]{1,0:T(8,128)(2,1)S(1)} %first_currents.1.source.first, f32[256,128]{1,0:T(8,128)S(1)} %fresh_part.7.mine, f32[256,128]{1,0:T(8,128)S(1)} %collective-permute-done.13.other, bf16[256,256]{1,0:T(8,128)(2,1)S(1)} %bitcast.6, ...), custom_call_target="tpu_custom_call" | custom-call | tf_op jit(solution)/shard_map/second_currents/pallas_call | solution.py:472
  (13 shorter events, 0.0 us)
Async XLA Ops:
  1.0 10.0 %collective-permute-start = (bf16[1152,128]{1,0:T(8,128)(2,1)S(1)}, bf16[1152,128]{1,0:T(8,128)(2,1)S(1)}, u32[]{:S(2)}, u32[]{:S(2)}) collective-permute-start(bf16[1152,128]{1,0:T(8,128)(2,1)S(1)} %own_planes.1.refs_3_.refs_0_), channel_id=1, source_target_pairs={{0,2},{2,0},{4,6},{6,4},{8,10},{10,8},{12,14},{14,12},{1,3},{3,1},... | collective-permute-start | bytes 884744 | tf_op jit(solution)/shard_map/ppermute | solution.py:395
  4.0 10.4 %collective-permute-start.1 = (bf16[1152,128]{1,0:T(8,128)(2,1)S(1)}, bf16[1152,128]{1,0:T(8,128)(2,1)S(1)}, u32[]{:S(2)}, u32[]{:S(2)}) collective-permute-start(bf16[1152,128]{1,0:T(8,128)(2,1)S(1)} %own_planes.1.refs_3_.refs_0_), channel_id=1, source_target_pairs={{0,4},{2,6},{4,0},{6,2},{8,12},{10,14},{12,8},{14,10},{1,17},{3,19... | collective-permute-start | bytes 884744 | tf_op jit(solution)/shard_map/ppermute | solution.py:395
  5.6 9.3 %collective-permute-start.2 = (bf16[1152,128]{1,0:T(8,128)(2,1)S(1)}, bf16[1152,128]{1,0:T(8,128)(2,1)S(1)}, u32[]{:S(2)}, u32[]{:S(2)}) collective-permute-start(bf16[1152,128]{1,0:T(8,128)(2,1)S(1)} %own_planes.1.refs_3_.refs_0_), channel_id=1, source_target_pairs={{0,16},{2,18},{4,8},{6,10},{8,4},{10,6},{12,28},{14,30},{1,5},{3,7... | collective-permute-start | bytes 884744 | tf_op jit(solution)/shard_map/ppermute | solution.py:395
  9.8 4.6 %collective-permute-start.3 = (bf16[2,256,256]{2,1,0:T(8,128)(2,1)S(1)}, bf16[2,256,256]{2,1,0:T(8,128)(2,1)S(1)}, u32[]{:S(2)}, u32[]{:S(2)}) collective-permute-start(bf16[2,256,256]{2,1,0:T(8,128)(2,1)S(1)} %get-tuple-element.19), channel_id=1, source_target_pairs={{0,1},{1,0},{2,3},{3,2},{4,5},{5,4},{6,7},{7,6},{8,9},{9,8},{10,11... | collective-permute-start | bytes 786440 | tf_op jit(solution)/shard_map/ppermute | solution.py:54
  11.0 9.4 %collective-permute-start.7 = (bf16[1152,128]{1,0:T(8,128)(2,1)S(1)}, bf16[1152,128]{1,0:T(8,128)(2,1)S(1)}, u32[]{:S(2)}, u32[]{:S(2)}) collective-permute-start(bf16[1152,128]{1,0:T(8,128)(2,1)S(1)} %collective-permute-done.refs_1_), channel_id=1, source_target_pairs={{0,4},{2,6},{4,0},{6,2},{8,12},{10,14},{12,8},{14,10},{1,17},{3,19... | collective-permute-start | bytes 884744 | tf_op jit(solution)/shard_map/ppermute | solution.py:395
  12.8 7.5 %collective-permute-start.8 = (bf16[1152,128]{1,0:T(8,128)(2,1)S(1)}, bf16[1152,128]{1,0:T(8,128)(2,1)S(1)}, u32[]{:S(2)}, u32[]{:S(2)}) collective-permute-start(bf16[1152,128]{1,0:T(8,128)(2,1)S(1)} %collective-permute-done.refs_1_), channel_id=1, source_target_pairs={{0,16},{2,18},{4,8},{6,10},{8,4},{10,6},{12,28},{14,30},{1,5},{3,7... | collective-permute-start | bytes 884744 | tf_op jit(solution)/shard_map/ppermute | solution.py:395
  14.3 2.8 %collective-permute-start.4 = (bf16[2,256,256]{2,1,0:T(8,128)(2,1)S(1)}, bf16[2,256,256]{2,1,0:T(8,128)(2,1)S(1)}, u32[]{:S(2)}, u32[]{:S(2)}) collective-permute-start(bf16[2,256,256]{2,1,0:T(8,128)(2,1)S(1)} %get-tuple-element.20), channel_id=1, source_target_pairs={{0,1},{1,0},{2,3},{3,2},{4,5},{5,4},{6,7},{7,6},{8,9},{9,8},{10,11... | collective-permute-start | bytes 786440 | tf_op jit(solution)/shard_map/ppermute | solution.py:54
  14.4 2.8 %collective-permute-start.5 = (bf16[2,256,256]{2,1,0:T(8,128)(2,1)S(1)}, bf16[2,256,256]{2,1,0:T(8,128)(2,1)S(1)}, u32[]{:S(2)}, u32[]{:S(2)}) collective-permute-start(bf16[2,256,256]{2,1,0:T(8,128)(2,1)S(1)} %get-tuple-element.21), channel_id=1, source_target_pairs={{0,1},{1,0},{2,3},{3,2},{4,5},{5,4},{6,7},{7,6},{8,9},{9,8},{10,11... | collective-permute-start | bytes 786440 | tf_op jit(solution)/shard_map/ppermute | solution.py:54
  14.9 2.3 %collective-permute-start.6 = (bf16[2,256,256]{2,1,0:T(8,128)(2,1)S(1)}, bf16[2,256,256]{2,1,0:T(8,128)(2,1)S(1)}, u32[]{:S(2)}, u32[]{:S(2)}) collective-permute-start(bf16[2,256,256]{2,1,0:T(8,128)(2,1)S(1)} %get-tuple-element.22), channel_id=1, source_target_pairs={{0,1},{1,0},{2,3},{3,2},{4,5},{5,4},{6,7},{7,6},{8,9},{9,8},{10,11... | collective-permute-start | bytes 786440 | tf_op jit(solution)/shard_map/ppermute | solution.py:54
  19.1 3.7 %copy-start = (bf16[1,256,256]{2,1,0:T(8,128)(2,1)S(1)}, bf16[1,256,256]{2,1,0:T(8,128)(2,1)}, u32[]{:S(2)}) copy-start(bf16[1,256,256]{2,1,0:T(8,128)(2,1)} %param.9) | copy-start | bytes 393220
  19.1 3.7 %copy-start.1 = (f32[2,128]{1,0:T(2,128)S(1)}, f32[2,128]{1,0:T(2,128)}, u32[]{:S(2)}) copy-start(f32[2,128]{1,0:T(2,128)} %wave.3) | copy-start | bytes 3076
  19.1 3.7 %copy-start.2 = (s32[128]{0:T(128)S(1)}, s32[128]{0:T(128)}, u32[]{:S(2)}) copy-start(s32[128]{0:T(128)} %param.12) | copy-start | bytes 1540
  21.4 1.4 %collective-permute-start.9 = (f32[256,128]{1,0:T(8,128)S(1)}, f32[256,128]{1,0:T(8,128)S(1)}, u32[]{:S(2)}, u32[]{:S(2)}) collective-permute-start(f32[256,128]{1,0:T(8,128)S(1)} %get-tuple-element.26.mine), channel_id=1, source_target_pairs={{0,1},{1,0},{2,3},{3,2},{4,5},{5,4},{6,7},{7,6},{8,9},{9,8},{10,11... | collective-permute-start | bytes 393224 | tf_op jit(solution)/shard_map/ppermute | solution.py:54
  23.0 5.8 %collective-permute-start.12 = (bf16[256,128]{1,0:T(8,128)(2,1)S(1)}, bf16[256,128]{1,0:T(8,128)(2,1)S(1)}, u32[]{:S(2)}, u32[]{:S(2)}) collective-permute-start(bf16[256,128]{1,0:T(8,128)(2,1)S(1)} %first_currents.1.source.first), channel_id=1, source_target_pairs={{0,2},{2,0},{4,6},{6,4},{8,10},{10,8},{12,14},{14,12},{1,7},{3,5},... | collective-permute-start | bytes 196616 | tf_op jit(solution)/shard_map/ppermute | solution.py:395
  24.6 4.8 %collective-permute-start.11 = (bf16[256,128]{1,0:T(8,128)(2,1)S(1)}, bf16[256,128]{1,0:T(8,128)(2,1)S(1)}, u32[]{:S(2)}, u32[]{:S(2)}) collective-permute-start(bf16[256,128]{1,0:T(8,128)(2,1)S(1)} %first_currents.1.source.first), channel_id=1, source_target_pairs={{0,4},{2,6},{4,0},{6,2},{8,12},{10,14},{12,8},{14,10},{1,17},{3,19... | collective-permute-start | bytes 196616 | tf_op jit(solution)/shard_map/ppermute | solution.py:395
  27.1 4.5 %collective-permute-start.10 = (bf16[256,128]{1,0:T(8,128)(2,1)S(1)}, bf16[256,128]{1,0:T(8,128)(2,1)S(1)}, u32[]{:S(2)}, u32[]{:S(2)}) collective-permute-start(bf16[256,128]{1,0:T(8,128)(2,1)S(1)} %first_currents.1.source.first), channel_id=1, source_target_pairs={{0,16},{2,18},{4,8},{6,10},{8,4},{10,6},{12,28},{14,30},{1,17},{3,... | collective-permute-start | bytes 196616 | tf_op jit(solution)/shard_map/ppermute | solution.py:395
  31.8 1.4 %collective-permute-start.13 = (f32[256,128]{1,0:T(8,128)S(1)}, f32[256,128]{1,0:T(8,128)S(1)}, u32[]{:S(2)}, u32[]{:S(2)}) collective-permute-start(f32[256,128]{1,0:T(8,128)S(1)} %fresh_part.7.mine), channel_id=1, source_target_pairs={{0,1},{1,0},{2,3},{3,2},{4,5},{5,4},{6,7},{7,6},{8,9},{9,8},{10,11... | collective-permute-start | bytes 393224 | tf_op jit(solution)/shard_map/ppermute | solution.py:54

commit v7 on v6

--- a/solution.py
+++ b/solution.py
@@ -18,6 +18,7 @@
 SLOT, LATE, NEWS, ORDER, PLACE = range(5)
 CHUNK = 4
 PIECES = 4
+HEAD = 96
 
 
 def held(x):
@@ -198,6 +199,24 @@
     )(table(meta), held(tiles), held(acc), *[held(x) for x in sources + pieces])
 
 
+def cut_kernel(start, count, *refs):
+    sources, out = refs[:-1], refs[-1]
+    for n, source in enumerate(sources):
+        out[n * count : (n + 1) * count] = source[start : start + count]
+
+
+def cut(sources, start, count):
+    width = sources[0].shape[1]
+    return pl.pallas_call(
+        functools.partial(cut_kernel, start, count),
+        out_shape=pltpu.VMEM((len(sources) * count, width), sources[0].dtype),
+        in_specs=[VMEM] * len(sources),
+        out_specs=VMEM,
+        compiler_params=SMALL,
+        name="cut",
+    )(*[held(x) for x in sources])
+
+
 def near_kernel(count, meta, tiles, *refs):
     sources, (total,) = refs[:count], refs[count:]
     taps, rows = tiles.shape[1:3]
@@ -242,15 +261,19 @@
     )(table(meta), held(tiles), *[held(x) for x in sources])
 
 
-def relayed_kernel(first, count, meta, tiles, cross, halves, acc, *refs):
-    sources, (out0, out1, total, store) = refs[:count], refs[count:]
+def relayed_kernel(first, turns, meta, tiles, cross, halves, acc, *refs):
+    sources, (out0, out1, total, store) = refs[: 3 * turns], refs[3 * turns :]
     pairs, taps, rows = tiles.shape[:3]
     half, width = rows // 2, acc.shape[1] // 2
     block = taps * rows + half
-    none = count * block
+    none = 2 * turns * block
     core = meta[PLACE, 1]
-    for n, source in enumerate(sources):
-        store[n * block : (n + 1) * block] = source[...]
+    for turn in range(turns):
+        tops, *rests = sources[3 * turn : 3 * turn + 3]
+        for n, rest in enumerate(rests):
+            base = (2 * turn + n) * block
+            store[base : base + HEAD] = tops[n * HEAD : (n + 1) * HEAD]
+            store[base + HEAD : base + block] = rest[...]
     store[none:] = jnp.zeros((rows, width), store.dtype)
     total[...] = acc[...]
 
@@ -299,12 +322,12 @@
 
 def relayed_part(meta, tiles, cross, halves, acc, sources, first):
     taps, rows = tiles.shape[1:3]
-    width, count = acc.shape[1] // 2, len(sources)
-    store = (count * (taps * rows + rows // 2) + rows, width)
+    width, turns = acc.shape[1] // 2, len(sources) // 3
+    store = (2 * turns * (taps * rows + rows // 2) + rows, width)
     half = pltpu.VMEM((rows, width), jnp.float32)
     room = 2 * store[0] * width + 4 * acc.size
     return pl.pallas_call(
-        functools.partial(relayed_kernel, first, count),
+        functools.partial(relayed_kernel, first, turns),
         out_shape=[half, half],
         in_specs=[SMEM] + [VMEM] * (4 + len(sources)),
         out_specs=[VMEM, VMEM],
@@ -394,14 +417,15 @@
                         pairs.append((source, twin * grid + 2 * a + c))
         return lax.ppermute(x, ALL_AXES, pairs)
 
+    swaps = ((("even", "odd"), ("odd", "even")), (("even", "odd"), ("odd", "even")))
     slots = [[-1] * (3 * groups) for _ in range(2)]
     for c in range(2):
         for t in range(groups):
             slots[c][key["own", t]] = t
-            for n, kind in enumerate(("even", "odd")):
-                slots[c][key[kind, t]] = groups + 2 * t + (n ^ c)
-
-    straight = [("own", t) for t in range(1, groups)] + [("even", 0), ("odd", 0)]
+            for n, pair in enumerate(swaps[min(t, 1)]):
+                slots[c][key[pair[c], t]] = groups + 2 * t + n
+
+    straight = [("odd", 0)]+[("own", t) for t in range(1, groups)]+[("even", 0)]
     diagonal = [(kind, t) for t in range(1, groups) for kind in ("even", "odd")]
     while len(diagonal) > len(straight):
         straight.append(diagonal.pop())
@@ -438,14 +462,13 @@
     )(far(pair_src), far(pair_delay), far(tiles), planes)
 
     own = [planes] + [send(planes, *[("own", t)] * 2) for t in range(1, groups)]
-    partners = [
-        send(planes, ("even", 0), ("odd", 0)),
-        send(planes, ("odd", 0), ("even", 0)),
-    ]
+    partners = [send(planes, *[(kind, 0) for kind in pair]) for pair in swaps[0]]
+    tops = cut(partners, 0, HEAD)
     relayed = []
     for x in own[1:]:
-        relayed.append(send(x, ("even", 0), ("odd", 0)))
-        relayed.append(send(x, ("odd", 0), ("even", 0)))
+        rest = cut([x], HEAD, x.shape[0] - HEAD)
+        relayed.append(send(tops, *[("own", len(relayed) // 3 + 1)] * 2))
+        relayed += [send(rest, *[(kind, 0) for kind in pair]) for pair in swaps[1]]
     pieces = [swap_cores(x) for x in ends]
 
     near = own + partners

time: 33.8 us -> 32.4 us (0.959); the launches traced: 34.1 us -> 32.2 us
  waiting for transfers between devices: 7.36 us -> 5.43 us
  Pallas kernels: 10.6 us -> 11 us
    ppermute x8 -> x9, waiting for transfers between devices: 4.68 us -> 2.75 us  [send(): return lax.ppermute(x, ALL_AXES, pairs)]
    ppermute x8 -> x9, starting transfers between devices: 15.1 us -> 14.4 us  [send(): return lax.ppermute(x, ALL_AXES, pairs)]
    ppermute x6, starting transfers between devices: 0.79 us -> 1.22 us  [swap_cores(): return lax.ppermute(x, 'sub', [(0, 1), (1, 0)])]
    pallas_call x1 -> x3, Pallas kernels: 1.02 us -> 1.04 us  [the longest x1 1.02 us: relayed_part(): pl.pallas_call(functools.partial(relayed_kernel, first, turns), out_shape...]
  transfers between devices with their start and end apart: 14 -> 15, of which waited for: 6 -> 5; matrix products, arithmetic and copies ran while one was open for 0% -> 0% of each run, Pallas kernels for 22% -> 24%
where the time goes in v7:
time: 32.4 us; the launch traced here: 32.2 us
  starting transfers between devices  15.6 us (48%)
  Pallas kernels  11 us (34%)
  waiting for transfers between devices  5.43 us (17%)
    ppermute x9, starting transfers between devices, send(): return lax.ppermute(x, ALL_AXES, pairs)  14.4 us
    ppermute x9, waiting for transfers between devices, send(): return lax.ppermute(x, ALL_AXES, pairs)  2.75 us
    ppermute x6, waiting for transfers between devices, swap_cores(): return lax.ppermute(x, 'sub', [(0, 1), (1, 0)])  2.68 us
    pallas_call x1, Pallas kernels, per_device(): pl.pallas_call(functools.partial(table_kernel, slots, news, sites, groups...  2.67 us
    pallas_call x1, Pallas kernels, near_part(): pl.pallas_call(functools.partial(near_kernel, len(sources)), out_shape=pl...  2.47 us
    pallas_call x1, Pallas kernels, swapped_part(): pl.pallas_call(functools.partial(swapped_kernel, len(sources)), out_shape...  2.09 us
    ppermute x6, starting transfers between devices, swap_cores(): return lax.ppermute(x, 'sub', [(0, 1), (1, 0)])  1.22 us
    pallas_call x1, Pallas kernels, relayed_part(): pl.pallas_call(functools.partial(relayed_kernel, first, turns), out_shape...  1.02 us
  transfers between devices with their start and end apart: 15, of which 5 were waited for; matrix products, arithmetic and copies ran while one was open for 0% of the time, Pallas kernels for 24%

profile of v7, /device:TPU:0, one launch (start us, length us, event | category | flops | bytes accessed | tf_op | source)
XLA Modules:
  0.0 32.2 jit_solution(13588171096990091281)
XLA Ops:
  0.0 1.0 %own_planes.1.refs_3_.refs_0_ = bf16[1152,128]{1,0:T(8,128)(2,1)S(1)} custom-call(bf16[9,256,128]{2,1,0:T(8,128)(2,1)} %bitcast.10), custom_call_target="tpu_custom_call" | custom-call | tf_op jit(solution)/shard_map/own_planes/pallas_call | solution.py:440
  1.0 3.0 %collective-permute-start = (bf16[1152,128]{1,0:T(8,128)(2,1)S(1)}, bf16[1152,128]{1,0:T(8,128)(2,1)S(1)}, u32[]{:S(2)}, u32[]{:S(2)}) collective-permute-start(bf16[1152,128]{1,0:T(8,128)(2,1)S(1)} %own_planes.1.refs_3_.refs_0_), channel_id=1, source_target_pairs={{0,2},{2,0},{4,6},{6,4},{8,10},{10,8},{12,14},{14,12},{1,3},{3,1},... | collective-permute-start | bytes 884744 | tf_op jit(solution)/shard_map/ppermute | solution.py:418
  4.0 1.6 %collective-permute-start.1 = (bf16[1152,128]{1,0:T(8,128)(2,1)S(1)}, bf16[1152,128]{1,0:T(8,128)(2,1)S(1)}, u32[]{:S(2)}, u32[]{:S(2)}) collective-permute-start(bf16[1152,128]{1,0:T(8,128)(2,1)S(1)} %own_planes.1.refs_3_.refs_0_), channel_id=1, source_target_pairs={{0,4},{2,6},{4,0},{6,2},{8,12},{10,14},{12,8},{14,10},{1,17},{3,19... | collective-permute-start | bytes 884744 | tf_op jit(solution)/shard_map/ppermute | solution.py:418
  5.6 1.5 %collective-permute-start.2 = (bf16[1152,128]{1,0:T(8,128)(2,1)S(1)}, bf16[1152,128]{1,0:T(8,128)(2,1)S(1)}, u32[]{:S(2)}, u32[]{:S(2)}) collective-permute-start(bf16[1152,128]{1,0:T(8,128)(2,1)S(1)} %own_planes.1.refs_3_.refs_0_), channel_id=1, source_target_pairs={{0,16},{2,18},{4,8},{6,10},{8,4},{10,6},{12,28},{14,30},{1,5},{3,7... | collective-permute-start | bytes 884744 | tf_op jit(solution)/shard_map/ppermute | solution.py:418
  7.1 2.7 %table.1 = (bf16[2,256,256]{2,1,0:T(8,128)(2,1)S(1)}, bf16[2,256,256]{2,1,0:T(8,128)(2,1)S(1)}, bf16[2,256,256]{2,1,0:T(8,128)(2,1)S(1)}, bf16[2,256,256]{2,1,0:...) custom-call(s32[1,8]{1,0:T(1,128)} %refs_0_.1, s32[1,8]{1,0:T(1,128)} %refs_1_.1, ...), custom_call_target="tpu_custom_call" | custom-call | tf_op jit(solution)/shard_map/table/pallas_call | solution.py:449
  9.8 0.1 collective-permute-start.3
  9.8 0.5 %collective-permute-start.4 = (bf16[2,256,256]{2,1,0:T(8,128)(2,1)S(1)}, bf16[2,256,256]{2,1,0:T(8,128)(2,1)S(1)}, u32[]{:S(2)}, u32[]{:S(2)}) collective-permute-start(bf16[2,256,256]{2,1,0:T(8,128)(2,1)S(1)} %get-tuple-element.20), channel_id=1, source_target_pairs={{0,1},{1,0},{2,3},{3,2},{4,5},{5,4},{6,7},{7,6},{8,9},{9,8},{10,11... | collective-permute-start | bytes 786440 | tf_op jit(solution)/shard_map/ppermute | solution.py:55
  10.3 0.7 %collective-permute-done.refs_1_.refs_0_ = bf16[1152,128]{1,0:T(8,128)(2,1)S(1)} collective-permute-done((bf16[1152,128]{1,0:T(8,128)(2,1)S(1)}, bf16[1152,128]{1,0:T(8,128)(2,1)S(1)}, u32[]{:S(2)}, u32[]{:S(2)}) %collective-permute-start) | collective-permute-done | bytes 294944 | tf_op jit(solution)/shard_map/ppermute | solution.py:418
  11.0 1.9 %collective-permute-start.8 = (bf16[1056,128]{1,0:T(8,128)(2,1)S(1)}, bf16[1056,128]{1,0:T(8,128)(2,1)S(1)}, u32[]{:S(2)}, u32[]{:S(2)}) collective-permute-start(bf16[1056,128]{1,0:T(8,128)(2,1)S(1)} %cut.3), channel_id=1, source_target_pairs={{0,4},{2,6},{4,0},{6,2},{8,12},{10,14},{12,8},{14,10},{1,17},{3,19... | collective-permute-start | bytes 811016 | tf_op jit(solution)/shard_map/ppermute | solution.py:418
  12.9 1.5 %collective-permute-start.9 = (bf16[1056,128]{1,0:T(8,128)(2,1)S(1)}, bf16[1056,128]{1,0:T(8,128)(2,1)S(1)}, u32[]{:S(2)}, u32[]{:S(2)}) collective-permute-start(bf16[1056,128]{1,0:T(8,128)(2,1)S(1)} %cut.3), channel_id=1, source_target_pairs={{0,16},{2,18},{4,8},{6,10},{8,4},{10,6},{12,28},{14,30},{1,5},{3,7... | collective-permute-start | bytes 811016 | tf_op jit(solution)/shard_map/ppermute | solution.py:418
  14.4 0.5 %collective-permute-start.6 = (bf16[2,256,256]{2,1,0:T(8,128)(2,1)S(1)}, bf16[2,256,256]{2,1,0:T(8,128)(2,1)S(1)}, u32[]{:S(2)}, u32[]{:S(2)}) collective-permute-start(bf16[2,256,256]{2,1,0:T(8,128)(2,1)S(1)} %get-tuple-element.22), channel_id=1, source_target_pairs={{0,1},{1,0},{2,3},{3,2},{4,5},{5,4},{6,7},{7,6},{8,9},{9,8},{10,11... | collective-permute-start | bytes 786440 | tf_op jit(solution)/shard_map/ppermute | solution.py:55
  15.0 1.6 %collective-permute-start.7 = (bf16[192,128]{1,0:T(8,128)(2,1)S(1)}, bf16[192,128]{1,0:T(8,128)(2,1)S(1)}, u32[]{:S(2)}, u32[]{:S(2)}) collective-permute-start(bf16[192,128]{1,0:T(8,128)(2,1)S(1)} %cut.2), channel_id=1, source_target_pairs={{0,2},{2,0},{4,6},{6,4},{8,10},{10,8},{12,14},{14,12},{1,3},{3,1},... | collective-permute-start | bytes 147464 | tf_op jit(solution)/shard_map/ppermute | solution.py:418
  16.5 2.5 %near_part.1.acc = f32[256,256]{1,0:T(8,128)S(1)} custom-call(s32[5,8]{1,0:T(8,128)S(4)} %get-tuple-element.17.meta, bf16[8,4,256,256]{3,2,1,0:T(8,128)(2,1)S(1)} %get-tuple-element.18.tiles, bf16[1152,128]{1,0:T(8,128)(2,1)S(1)} %own_planes.1.refs_3_.refs_0_, bf16[1152,128]{1,0:T(8,128)(2,1)S(1)} %collective-permute-done.refs_1_.refs_0_, ...), custom_call_target="tpu_custom_call" | custom-call | tf_op jit(solution)/shard_map/near_part/pallas_call | solution.py:254
  19.0 2.1 %swapped_part.1 = (bf16[8,256,256]{2,1,0:T(8,128)(2,1)S(1)}, bf16[8,256,128]{2,1,0:T(8,128)(2,1)S(1)}, bf16[8,256,256]{2,1,0:T(8,128)(2,1)S(1)}, f32[256,256]{1,0:T(8,128)S(1)}) custom-call(s32[5,8]{1,0:T(8,128)S(4)} %get-tuple-element.17.meta, bf16[8,4,256,256]{3,2,1,0:T(8,128)(2,1)S(1)} %get-tuple-element.18.tiles, f32[256,256]{1,0:T(8,128)S(1)} %near_part.1.acc, ...), custom_call_target="tpu_custom_call" | custom-call | tf_op jit(solution)/shard_map/swapped_part/pallas_call | solution.py:187
  21.1 0.0 copy-start
  21.1 0.0 copy-start.1
  21.2 1.0 %relayed_part.1 = (f32[256,128]{1,0:T(8,128)S(1)}, f32[256,128]{1,0:T(8,128)S(1)}) custom-call(s32[5,8]{1,0:T(8,128)S(4)} %get-tuple-element.17.meta, bf16[8,4,256,256]{3,2,1,0:T(8,128)(2,1)S(1)} %get-tuple-element.18.tiles, bf16[8,256,256]{2,1,0:T(8,128)(2,1)S(1)} %get-tuple-element.23.cross, bf16[8,256,128]{2,1,0:T(8,128)(2,1)S(1)} %get-tuple-element.24.halves, ...), custom_call_target="tpu_custom_call" | custom-call | tf_op jit(solution)/shard_map/relayed_part/pallas_call | solution.py:329
  22.2 0.1 collective-permute-start.10
  22.3 1.3 %collective-permute-done.10.other = f32[256,128]{1,0:T(8,128)S(1)} collective-permute-done((f32[256,128]{1,0:T(8,128)S(1)}, f32[256,128]{1,0:T(8,128)S(1)}, u32[]{:S(2)}, u32[]{:S(2)}) %collective-permute-start.10) | collective-permute-done | bytes 131104 | tf_op jit(solution)/shard_map/ppermute | solution.py:55
  23.6 0.2 first_currents.1.source.first
  23.8 0.6 %collective-permute-start.13 = (bf16[256,128]{1,0:T(8,128)(2,1)S(1)}, bf16[256,128]{1,0:T(8,128)(2,1)S(1)}, u32[]{:S(2)}, u32[]{:S(2)}) collective-permute-start(bf16[256,128]{1,0:T(8,128)(2,1)S(1)} %first_currents.1.source.first), channel_id=1, source_target_pairs={{0,16},{2,18},{4,8},{6,10},{8,4},{10,6},{12,28},{14,30},{1,7},{3,5... | collective-permute-start | bytes 196616 | tf_op jit(solution)/shard_map/ppermute | solution.py:418
  24.4 1.1 %collective-permute-start.12 = (bf16[256,128]{1,0:T(8,128)(2,1)S(1)}, bf16[256,128]{1,0:T(8,128)(2,1)S(1)}, u32[]{:S(2)}, u32[]{:S(2)}) collective-permute-start(bf16[256,128]{1,0:T(8,128)(2,1)S(1)} %first_currents.1.source.first), channel_id=1, source_target_pairs={{0,2},{2,0},{4,6},{6,4},{8,10},{10,8},{12,14},{14,12},{1,17},{3,19... | collective-permute-start | bytes 196616 | tf_op jit(solution)/shard_map/ppermute | solution.py:418
  25.5 1.6 %collective-permute-start.11 = (bf16[256,128]{1,0:T(8,128)(2,1)S(1)}, bf16[256,128]{1,0:T(8,128)(2,1)S(1)}, u32[]{:S(2)}, u32[]{:S(2)}) collective-permute-start(bf16[256,128]{1,0:T(8,128)(2,1)S(1)} %first_currents.1.source.first), channel_id=1, source_target_pairs={{0,4},{2,6},{4,0},{6,2},{8,12},{10,14},{12,8},{14,10},{1,17},{3,19... | collective-permute-start | bytes 196616 | tf_op jit(solution)/shard_map/ppermute | solution.py:418
  27.1 0.1 fresh_part.4.acc
  27.3 1.6 %collective-permute-done.13.source = bf16[256,128]{1,0:T(8,128)(2,1)S(1)} collective-permute-done((bf16[256,128]{1,0:T(8,128)(2,1)S(1)}, bf16[256,128]{1,0:T(8,128)(2,1)S(1)}, u32[]{:S(2)}, u32[]{:S(2)}) %collective-permute-start.13) | collective-permute-done | bytes 65568 | tf_op jit(solution)/shard_map/ppermute | solution.py:418
  28.8 0.1 fresh_part.5.acc
  29.0 0.3 fresh_part.6.acc
  29.3 0.5 %collective-permute-done.11.source = bf16[256,128]{1,0:T(8,128)(2,1)S(1)} collective-permute-done((bf16[256,128]{1,0:T(8,128)(2,1)S(1)}, bf16[256,128]{1,0:T(8,128)(2,1)S(1)}, u32[]{:S(2)}, u32[]{:S(2)}) %collective-permute-start.11) | collective-permute-done | bytes 65568 | tf_op jit(solution)/shard_map/ppermute | solution.py:418
  29.8 0.1 fresh_part.7.mine
  29.9 0.1 collective-permute-start.14
  30.0 1.3 %collective-permute-done.14.other = f32[256,128]{1,0:T(8,128)S(1)} collective-permute-done((f32[256,128]{1,0:T(8,128)S(1)}, f32[256,128]{1,0:T(8,128)S(1)}, u32[]{:S(2)}, u32[]{:S(2)}) %collective-permute-start.14) | collective-permute-done | bytes 131104 | tf_op jit(solution)/shard_map/ppermute | solution.py:55
  31.4 0.9 %second_currents.1 = bf16[2,256,128]{2,1,0:T(8,128)(2,1)} custom-call(s32[5,8]{1,0:T(8,128)S(4)} %get-tuple-element.17.meta, bf16[256,128]{1,0:T(8,128)(2,1)S(1)} %first_currents.1.source.first, f32[256,128]{1,0:T(8,128)S(1)} %fresh_part.7.mine, f32[256,128]{1,0:T(8,128)S(1)} %collective-permute-done.14.other, bf16[256,256]{1,0:T(8,128)(2,1)S(1)} %bitcast.6, ...), custom_call_target="tpu_custom_call" | custom-call | tf_op jit(solution)/shard_map/second_currents/pallas_call | solution.py:495
  (17 shorter events, 0.1 us)
Async XLA Ops:
  1.0 10.0 %collective-permute-start = (bf16[1152,128]{1,0:T(8,128)(2,1)S(1)}, bf16[1152,128]{1,0:T(8,128)(2,1)S(1)}, u32[]{:S(2)}, u32[]{:S(2)}) collective-permute-start(bf16[1152,128]{1,0:T(8,128)(2,1)S(1)} %own_planes.1.refs_3_.refs_0_), channel_id=1, source_target_pairs={{0,2},{2,0},{4,6},{6,4},{8,10},{10,8},{12,14},{14,12},{1,3},{3,1},... | collective-permute-start | bytes 884744 | tf_op jit(solution)/shard_map/ppermute | solution.py:418
  4.0 10.4 %collective-permute-start.1 = (bf16[1152,128]{1,0:T(8,128)(2,1)S(1)}, bf16[1152,128]{1,0:T(8,128)(2,1)S(1)}, u32[]{:S(2)}, u32[]{:S(2)}) collective-permute-start(bf16[1152,128]{1,0:T(8,128)(2,1)S(1)} %own_planes.1.refs_3_.refs_0_), channel_id=1, source_target_pairs={{0,4},{2,6},{4,0},{6,2},{8,12},{10,14},{12,8},{14,10},{1,17},{3,19... | collective-permute-start | bytes 884744 | tf_op jit(solution)/shard_map/ppermute | solution.py:418
  5.6 8.9 %collective-permute-start.2 = (bf16[1152,128]{1,0:T(8,128)(2,1)S(1)}, bf16[1152,128]{1,0:T(8,128)(2,1)S(1)}, u32[]{:S(2)}, u32[]{:S(2)}) collective-permute-start(bf16[1152,128]{1,0:T(8,128)(2,1)S(1)} %own_planes.1.refs_3_.refs_0_), channel_id=1, source_target_pairs={{0,16},{2,18},{4,8},{6,10},{8,4},{10,6},{12,28},{14,30},{1,5},{3,7... | collective-permute-start | bytes 884744 | tf_op jit(solution)/shard_map/ppermute | solution.py:418
  9.8 3.1 %collective-permute-start.3 = (bf16[2,256,256]{2,1,0:T(8,128)(2,1)S(1)}, bf16[2,256,256]{2,1,0:T(8,128)(2,1)S(1)}, u32[]{:S(2)}, u32[]{:S(2)}) collective-permute-start(bf16[2,256,256]{2,1,0:T(8,128)(2,1)S(1)} %get-tuple-element.19), channel_id=1, source_target_pairs={{0,1},{1,0},{2,3},{3,2},{4,5},{5,4},{6,7},{7,6},{8,9},{9,8},{10,11... | collective-permute-start | bytes 786440 | tf_op jit(solution)/shard_map/ppermute | solution.py:55
  9.8 5.1 %collective-permute-start.4 = (bf16[2,256,256]{2,1,0:T(8,128)(2,1)S(1)}, bf16[2,256,256]{2,1,0:T(8,128)(2,1)S(1)}, u32[]{:S(2)}, u32[]{:S(2)}) collective-permute-start(bf16[2,256,256]{2,1,0:T(8,128)(2,1)S(1)} %get-tuple-element.20), channel_id=1, source_target_pairs={{0,1},{1,0},{2,3},{3,2},{4,5},{5,4},{6,7},{7,6},{8,9},{9,8},{10,11... | collective-permute-start | bytes 786440 | tf_op jit(solution)/shard_map/ppermute | solution.py:55
  11.0 10.1 %collective-permute-start.8 = (bf16[1056,128]{1,0:T(8,128)(2,1)S(1)}, bf16[1056,128]{1,0:T(8,128)(2,1)S(1)}, u32[]{:S(2)}, u32[]{:S(2)}) collective-permute-start(bf16[1056,128]{1,0:T(8,128)(2,1)S(1)} %cut.3), channel_id=1, source_target_pairs={{0,4},{2,6},{4,0},{6,2},{8,12},{10,14},{12,8},{14,10},{1,17},{3,19... | collective-permute-start | bytes 811016 | tf_op jit(solution)/shard_map/ppermute | solution.py:418
  12.9 8.2 %collective-permute-start.9 = (bf16[1056,128]{1,0:T(8,128)(2,1)S(1)}, bf16[1056,128]{1,0:T(8,128)(2,1)S(1)}, u32[]{:S(2)}, u32[]{:S(2)}) collective-permute-start(bf16[1056,128]{1,0:T(8,128)(2,1)S(1)} %cut.3), channel_id=1, source_target_pairs={{0,16},{2,18},{4,8},{6,10},{8,4},{10,6},{12,28},{14,30},{1,5},{3,7... | collective-permute-start | bytes 811016 | tf_op jit(solution)/shard_map/ppermute | solution.py:418
  14.4 4.6 %collective-permute-start.5 = (bf16[2,256,256]{2,1,0:T(8,128)(2,1)S(1)}, bf16[2,256,256]{2,1,0:T(8,128)(2,1)S(1)}, u32[]{:S(2)}, u32[]{:S(2)}) collective-permute-start(bf16[2,256,256]{2,1,0:T(8,128)(2,1)S(1)} %get-tuple-element.21), channel_id=1, source_target_pairs={{0,1},{1,0},{2,3},{3,2},{4,5},{5,4},{6,7},{7,6},{8,9},{9,8},{10,11... | collective-permute-start | bytes 786440 | tf_op jit(solution)/shard_map/ppermute | solution.py:55
  14.4 4.6 %collective-permute-start.6 = (bf16[2,256,256]{2,1,0:T(8,128)(2,1)S(1)}, bf16[2,256,256]{2,1,0:T(8,128)(2,1)S(1)}, u32[]{:S(2)}, u32[]{:S(2)}) collective-permute-start(bf16[2,256,256]{2,1,0:T(8,128)(2,1)S(1)} %get-tuple-element.22), channel_id=1, source_target_pairs={{0,1},{1,0},{2,3},{3,2},{4,5},{5,4},{6,7},{7,6},{8,9},{9,8},{10,11... | collective-permute-start | bytes 786440 | tf_op jit(solution)/shard_map/ppermute | solution.py:55
  15.0 6.2 %collective-permute-start.7 = (bf16[192,128]{1,0:T(8,128)(2,1)S(1)}, bf16[192,128]{1,0:T(8,128)(2,1)S(1)}, u32[]{:S(2)}, u32[]{:S(2)}) collective-permute-start(bf16[192,128]{1,0:T(8,128)(2,1)S(1)} %cut.2), channel_id=1, source_target_pairs={{0,2},{2,0},{4,6},{6,4},{8,10},{10,8},{12,14},{14,12},{1,3},{3,1},... | collective-permute-start | bytes 147464 | tf_op jit(solution)/shard_map/ppermute | solution.py:418
  21.1 2.5 %copy-start = (bf16[1,256,256]{2,1,0:T(8,128)(2,1)S(1)}, bf16[1,256,256]{2,1,0:T(8,128)(2,1)}, u32[]{:S(2)}) copy-start(bf16[1,256,256]{2,1,0:T(8,128)(2,1)} %param.9) | copy-start | bytes 393220
  21.1 2.5 %copy-start.1 = (f32[2,128]{1,0:T(2,128)S(1)}, f32[2,128]{1,0:T(2,128)}, u32[]{:S(2)}) copy-start(f32[2,128]{1,0:T(2,128)} %wave.3) | copy-start | bytes 3076
  21.1 2.5 %copy-start.2 = (s32[128]{0:T(128)S(1)}, s32[128]{0:T(128)}, u32[]{:S(2)}) copy-start(s32[128]{0:T(128)} %param.12) | copy-start | bytes 1540
  22.2 1.4 %collective-permute-start.10 = (f32[256,128]{1,0:T(8,128)S(1)}, f32[256,128]{1,0:T(8,128)S(1)}, u32[]{:S(2)}, u32[]{:S(2)}) collective-permute-start(f32[256,128]{1,0:T(8,128)S(1)} %get-tuple-element.26.mine), channel_id=1, source_target_pairs={{0,1},{1,0},{2,3},{3,2},{4,5},{5,4},{6,7},{7,6},{8,9},{9,8},{10,11... | collective-permute-start | bytes 393224 | tf_op jit(solution)/shard_map/ppermute | solution.py:55
  23.8 5.0 %collective-permute-start.13 = (bf16[256,128]{1,0:T(8,128)(2,1)S(1)}, bf16[256,128]{1,0:T(8,128)(2,1)S(1)}, u32[]{:S(2)}, u32[]{:S(2)}) collective-permute-start(bf16[256,128]{1,0:T(8,128)(2,1)S(1)} %first_currents.1.source.first), channel_id=1, source_target_pairs={{0,16},{2,18},{4,8},{6,10},{8,4},{10,6},{12,28},{14,30},{1,7},{3,5... | collective-permute-start | bytes 196616 | tf_op jit(solution)/shard_map/ppermute | solution.py:418
  24.4 4.6 %collective-permute-start.12 = (bf16[256,128]{1,0:T(8,128)(2,1)S(1)}, bf16[256,128]{1,0:T(8,128)(2,1)S(1)}, u32[]{:S(2)}, u32[]{:S(2)}) collective-permute-start(bf16[256,128]{1,0:T(8,128)(2,1)S(1)} %first_currents.1.source.first), channel_id=1, source_target_pairs={{0,2},{2,0},{4,6},{6,4},{8,10},{10,8},{12,14},{14,12},{1,17},{3,19... | collective-permute-start | bytes 196616 | tf_op jit(solution)/shard_map/ppermute | solution.py:418
  25.5 4.3 %collective-permute-start.11 = (bf16[256,128]{1,0:T(8,128)(2,1)S(1)}, bf16[256,128]{1,0:T(8,128)(2,1)S(1)}, u32[]{:S(2)}, u32[]{:S(2)}) collective-permute-start(bf16[256,128]{1,0:T(8,128)(2,1)S(1)} %first_currents.1.source.first), channel_id=1, source_target_pairs={{0,4},{2,6},{4,0},{6,2},{8,12},{10,14},{12,8},{14,10},{1,17},{3,19... | collective-permute-start | bytes 196616 | tf_op jit(solution)/shard_map/ppermute | solution.py:418
  29.9 1.4 %collective-permute-start.14 = (f32[256,128]{1,0:T(8,128)S(1)}, f32[256,128]{1,0:T(8,128)S(1)}, u32[]{:S(2)}, u32[]{:S(2)}) collective-permute-start(f32[256,128]{1,0:T(8,128)S(1)} %fresh_part.7.mine), channel_id=1, source_target_pairs={{0,1},{1,0},{2,3},{3,2},{4,5},{5,4},{6,7},{7,6},{8,9},{9,8},{10,11... | collective-permute-start | bytes 393224 | tf_op jit(solution)/shard_map/ppermute | solution.py:55

commit v8 on v7

--- a/solution.py
+++ b/solution.py
@@ -16,7 +16,7 @@
 SMALL = pltpu.CompilerParams(vmem_limit_bytes=4 << 20)
 
 SLOT, LATE, NEWS, ORDER, PLACE = range(5)
-CHUNK = 4
+CHUNK = 2
 PIECES = 4
 HEAD = 96
 
@@ -132,68 +132,55 @@
 
 
 def swapped_kernel(count, meta, tiles, acc, *refs):
-    sources, pieces = refs[:count], refs[count:-4]
-    cross, halves, newest, total = refs[-4:]
+    sources, pieces = refs[:count], refs[count:-2]
+    extra, total = refs[-2:]
     part = pieces[0].shape[0]
     taps, rows = tiles.shape[1:3]
-    half = rows // 2
+    half, width = rows // 2, sources[0].shape[1]
     core = meta[PLACE, 1]
     total[...] = acc[...]
     for n, piece in enumerate(pieces):
-        cross[n * part : (n + 1) * part] = piece[...]
-
-    @pl.when(core == 0)
-    def _():
-        newest[...] = tiles[:, 0]
-        halves[...] = cross[:, :, :half]
-
-    @pl.when(core == 1)
-    def _():
-        newest[...] = cross[...]
-        halves[...] = tiles[:, taps - 1, :, half:]
+        extra[n * part : (n + 1) * part] = piece[...]
+
+    def add(step, left, right):
+        total[:, step * width : (step + 1) * width] += jnp.dot(
+            left, right, preferred_element_type=jnp.float32
+        )
+
+    def one(p, source):
+        late = meta[LATE, p]
+
+        @pl.when((late == 0) & (core == 0))
+        def _():
+            add(1, extra[p], source[(taps - 1) * rows : taps * rows])
+
+        @pl.when((late == 1) & (core == 0))
+        def _():
+            add(0, extra[p, :, :half], source[taps * rows :])
+
+        @pl.when((late == 1) & (core == 1))
+        def _():
+            add(0, extra[p], source[:rows])
+            add(0, tiles[p, taps - 1, :, half:], source[taps * rows :])
 
     @pl.loop(0, tiles.shape[0])
     def _(p):
-        for slot, source in enumerate(sources):
-            used, late = meta[SLOT, p] == slot, meta[LATE, p]
-            width = source.shape[1]
-
-            @pl.when(used & (late == 0) & (core == 0))
-            def _():
-                total[:, width:] += jnp.dot(
-                    cross[p],
-                    source[(taps - 1) * rows : taps * rows],
-                    preferred_element_type=jnp.float32,
-                )
-
-            @pl.when(used & (late == 1))
-            def _():
-                total[:, :width] += jnp.dot(
-                    halves[p],
-                    source[taps * rows :],
-                    preferred_element_type=jnp.float32,
-                )
-
-            @pl.when(used & (late == 1) & (core == 1))
-            def _():
-                total[:, :width] += jnp.dot(
-                    cross[p], source[:rows], preferred_element_type=jnp.float32
-                )
+        @pl.when((meta[LATE, p] == 1) | (core == 0))
+        def _():
+            for slot, source in enumerate(sources):
+                pl.when(meta[SLOT, p] == slot)(functools.partial(one, p, source))
 
 
 def swapped_part(meta, tiles, acc, sources, pieces):
     pairs, _, rows, cols = tiles.shape
-    whole = pltpu.VMEM((pairs, rows, cols), tiles.dtype)
     return pl.pallas_call(
         functools.partial(swapped_kernel, len(sources)),
         out_shape=[
-            whole,
-            pltpu.VMEM((pairs, rows, cols // 2), tiles.dtype),
-            whole,
+            pltpu.VMEM((pairs, rows, cols), tiles.dtype),
             pltpu.VMEM(acc.shape, acc.dtype),
         ],
         in_specs=[SMEM] + [VMEM] * (2 + len(sources) + len(pieces)),
-        out_specs=[VMEM] * 4,
+        out_specs=[VMEM] * 2,
         compiler_params=SMALL,
         name="swapped_part",
     )(table(meta), held(tiles), held(acc), *[held(x) for x in sources + pieces])
@@ -261,27 +248,31 @@
     )(table(meta), held(tiles), *[held(x) for x in sources])
 
 
-def relayed_kernel(first, turns, meta, tiles, cross, halves, acc, *refs):
+def relayed_kernel(first, turns, meta, tiles, extra, acc, *refs):
     sources, (out0, out1, total, store) = refs[: 3 * turns], refs[3 * turns :]
     pairs, taps, rows = tiles.shape[:3]
     half, width = rows // 2, acc.shape[1] // 2
-    block = taps * rows + half
+    held_rows = taps * rows
+    block = held_rows + 3 * half
     none = 2 * turns * block
     core = meta[PLACE, 1]
+    empty = jnp.zeros((half, width), store.dtype)
     for turn in range(turns):
         tops, *rests = sources[3 * turn : 3 * turn + 3]
         for n, rest in enumerate(rests):
             base = (2 * turn + n) * block
             store[base : base + HEAD] = tops[n * HEAD : (n + 1) * HEAD]
-            store[base + HEAD : base + block] = rest[...]
+            store[base + HEAD : base + held_rows] = rest[: held_rows - HEAD]
+            store[base + held_rows : base + held_rows + half] = empty
+            store[base + held_rows + half : base + block - half] = rest[held_rows - HEAD :]
+            store[base + block - half : base + block] = empty
     store[none:] = jnp.zeros((rows, width), store.dtype)
     total[...] = acc[...]
 
-    def plane(at, count):
-        return store[pl.ds(pl.multiple_of(at, half), count)]
-
-    def pair(a, b, count):
-        return jnp.concatenate([plane(a, count), plane(b, count)], axis=1)
+    def pair(a, b):
+        return jnp.concatenate(
+            [store[pl.ds(pl.multiple_of(at, half), rows)] for at in (a, b)], axis=1
+        )
 
     def chunk(start):
         lefts, rights = [], []
@@ -293,21 +284,17 @@
             early = jnp.logical_and(used, late == 0)
             after = jnp.logical_and(used, late == 1)
             ats = [jnp.where(used, base + k * rows, none) for k in range(taps)]
-            before = [none] + ats + [none]
+            last = jnp.where(jnp.logical_and(after, core == 1), base + held_rows, none)
+            before = [none] + ats + [last]
             for k in range(taps):
                 lefts.append(tiles[p, k])
                 a = jnp.where(late == 1, before[k + 2], before[k + 1])
                 b = jnp.where(late == 1, before[k + 1], before[k])
-                rights.append(pair(a, b, rows))
-            lefts.append(cross[p])
-            a = jnp.where(jnp.logical_and(after, core == 1), base, none)
-            b = jnp.where(
-                jnp.logical_and(early, core == 0), base + (taps - 1) * rows, none
-            )
-            rights.append(pair(a, b, rows))
-            lefts.append(halves[p])
-            a = jnp.where(after, base + taps * rows, none)
-            rights.append(pair(a, none, half))
+                rights.append(pair(a, b))
+            lefts.append(extra[p])
+            a = jnp.where(core == 0, base + held_rows + half, base)
+            b = jnp.where(jnp.logical_and(early, core == 0), ats[taps - 1], none)
+            rights.append(pair(jnp.where(after, a, none), b))
         total[...] += jnp.dot(
             jnp.concatenate(lefts, axis=1),
             jnp.concatenate(rights, axis=0),
@@ -320,16 +307,16 @@
     out1[...] = total[:, width:]
 
 
-def relayed_part(meta, tiles, cross, halves, acc, sources, first):
+def relayed_part(meta, tiles, extra, acc, sources, first):
     taps, rows = tiles.shape[1:3]
     width, turns = acc.shape[1] // 2, len(sources) // 3
-    store = (2 * turns * (taps * rows + rows // 2) + rows, width)
+    store = (2 * turns * (taps * rows + 3 * rows // 2) + rows, width)
     half = pltpu.VMEM((rows, width), jnp.float32)
     room = 2 * store[0] * width + 4 * acc.size
     return pl.pallas_call(
         functools.partial(relayed_kernel, first, turns),
         out_shape=[half, half],
-        in_specs=[SMEM] + [VMEM] * (4 + len(sources)),
+        in_specs=[SMEM] + [VMEM] * (3 + len(sources)),
         out_specs=[VMEM, VMEM],
         scratch_shapes=[
             pltpu.VMEM(acc.shape, acc.dtype),
@@ -340,8 +327,7 @@
     )(
         table(meta),
         held(tiles),
-        held(cross),
-        held(halves),
+        held(extra),
         held(acc),
         *[held(x) for x in sources],
     )
@@ -370,27 +356,29 @@
     )
 
 
-def fresh_kernel(number, meta, tiles, source, acc, out):
+def fresh_kernel(number, meta, tiles, extra, source, acc, out):
     out[...] = acc[...]
+
+    def add(tile):
+        out[...] += jnp.dot(tile, source[...], preferred_element_type=jnp.float32)
 
     @pl.loop(0, tiles.shape[0])
     def _(p):
         @pl.when(meta[NEWS, p] == number)
         def _():
-            out[...] += jnp.dot(
-                tiles[p], source[...], preferred_element_type=jnp.float32
-            )
-
-
-def fresh_part(meta, tiles, source, number, acc):
+            pl.when(meta[PLACE, 1] == 0)(lambda: add(tiles[p, 0]))
+            pl.when(meta[PLACE, 1] == 1)(lambda: add(extra[p]))
+
+
+def fresh_part(meta, tiles, extra, source, number, acc):
     return pl.pallas_call(
         functools.partial(fresh_kernel, number),
         out_shape=pltpu.VMEM(acc.shape, acc.dtype),
-        in_specs=[SMEM] + [VMEM] * 3,
+        in_specs=[SMEM] + [VMEM] * 4,
         out_specs=VMEM,
         compiler_params=SMALL,
         name="fresh_part",
-    )(table(meta), held(tiles), held(source), held(acc))
+    )(table(meta), held(tiles), held(extra), held(source), held(acc))
 
 
 def per_device(tiles, history, self_inverse, pair_src, pair_delay, strike_seg, waveform):
@@ -473,10 +461,8 @@
 
     near = own + partners
     acc = near_part(meta, tiles, near)
-    cross, halves, newest, acc = swapped_part(meta, tiles, acc, near, pieces)
-    mine0, mine1 = relayed_part(
-        meta, tiles, cross, halves, acc, relayed, groups + 2
-    )
+    extra, acc = swapped_part(meta, tiles, acc, near, pieces)
+    mine0, mine1 = relayed_part(meta, tiles, extra, acc, relayed, groups + 2)
 
     strike, inverse, wave = held(strike_seg[None, :]), held(inverse), held(waveform)
     current0 = pl.pallas_call(
@@ -490,7 +476,7 @@
 
     fresh = [send(current0, *messages) for messages in rounds]
     for number, block in enumerate([current0] + fresh):
-        mine1 = fresh_part(meta, newest, block, number, mine1)
+        mine1 = fresh_part(meta, tiles, extra, block, number, mine1)
 
     currents = pl.pallas_call(
         second_kernel,

time: 32.4 us -> 32.2 us (level)
  Pallas kernels: 11 us -> 10.3 us
  starting transfers between devices: 15.6 us -> 16 us
    ppermute x9, starting transfers between devices: 14.4 us -> 14.8 us  [send(): return lax.ppermute(x, ALL_AXES, pairs)]
    pallas_call x1, Pallas kernels: 2.09 us -> 1.63 us  [swapped_part(): pl.pallas_call(functools.partial(swapped_kernel, len(sources)), out_shape...]
    pallas_call x1, Pallas kernels: 1.02 us -> 0.64 us  [relayed_part(): pl.pallas_call(functools.partial(relayed_kernel, first, turns), out_shape...]
  transfers between devices with their start and end apart: 15 -> 15, of which waited for: 5 -> 6; matrix products, arithmetic and copies ran while one was open for 0% -> 0% of each run, Pallas kernels for 24% -> 23%
where the time goes in v8:
time: 32.2 us; the launch traced here: 32 us
  starting transfers between devices  16 us (50%)
  Pallas kernels  10.3 us (32%)
  waiting for transfers between devices  5.42 us (17%)
    ppermute x9, starting transfers between devices, send(): return lax.ppermute(x, ALL_AXES, pairs)  14.8 us
    ppermute x9, waiting for transfers between devices, send(): return lax.ppermute(x, ALL_AXES, pairs)  2.74 us
    pallas_call x1, Pallas kernels, per_device(): pl.pallas_call(functools.partial(table_kernel, slots, news, sites, groups...  2.69 us
    ppermute x6, waiting for transfers between devices, swap_cores(): return lax.ppermute(x, 'sub', [(0, 1), (1, 0)])  2.68 us
    pallas_call x1, Pallas kernels, near_part(): pl.pallas_call(functools.partial(near_kernel, len(sources)), out_shape=pl...  2.46 us
    pallas_call x1, Pallas kernels, swapped_part(): pl.pallas_call(functools.partial(swapped_kernel, len(sources)), out_shape...  1.63 us
    ppermute x6, starting transfers between devices, swap_cores(): return lax.ppermute(x, 'sub', [(0, 1), (1, 0)])  1.22 us
    pallas_call x1, Pallas kernels, per_device(): pl.pallas_call(planes_kernel, out_shape=pltpu.VMEM((taps * rows + rows //...  0.98 us
  transfers between devices with their start and end apart: 15, of which 6 were waited for; matrix products, arithmetic and copies ran while one was open for 0% of the time, Pallas kernels for 23%

profile of v8, /device:TPU:0, one launch (start us, length us, event | category | flops | bytes accessed | tf_op | source)
XLA Modules:
  0.0 32.0 jit_solution(10838287093836655384)
XLA Ops:
  0.0 1.0 %own_planes.1.refs_3_.refs_0_ = bf16[1152,128]{1,0:T(8,128)(2,1)S(1)} custom-call(bf16[9,256,128]{2,1,0:T(8,128)(2,1)} %bitcast.10), custom_call_target="tpu_custom_call" | custom-call | tf_op jit(solution)/shard_map/own_planes/pallas_call | solution.py:428
  1.0 3.0 %collective-permute-start = (bf16[1152,128]{1,0:T(8,128)(2,1)S(1)}, bf16[1152,128]{1,0:T(8,128)(2,1)S(1)}, u32[]{:S(2)}, u32[]{:S(2)}) collective-permute-start(bf16[1152,128]{1,0:T(8,128)(2,1)S(1)} %own_planes.1.refs_3_.refs_0_), channel_id=1, source_target_pairs={{0,2},{2,0},{4,6},{6,4},{8,10},{10,8},{12,14},{14,12},{1,3},{3,1},... | collective-permute-start | bytes 884744 | tf_op jit(solution)/shard_map/ppermute | solution.py:406
  4.0 1.6 %collective-permute-start.1 = (bf16[1152,128]{1,0:T(8,128)(2,1)S(1)}, bf16[1152,128]{1,0:T(8,128)(2,1)S(1)}, u32[]{:S(2)}, u32[]{:S(2)}) collective-permute-start(bf16[1152,128]{1,0:T(8,128)(2,1)S(1)} %own_planes.1.refs_3_.refs_0_), channel_id=1, source_target_pairs={{0,4},{2,6},{4,0},{6,2},{8,12},{10,14},{12,8},{14,10},{1,17},{3,19... | collective-permute-start | bytes 884744 | tf_op jit(solution)/shard_map/ppermute | solution.py:406
  5.6 1.5 %collective-permute-start.2 = (bf16[1152,128]{1,0:T(8,128)(2,1)S(1)}, bf16[1152,128]{1,0:T(8,128)(2,1)S(1)}, u32[]{:S(2)}, u32[]{:S(2)}) collective-permute-start(bf16[1152,128]{1,0:T(8,128)(2,1)S(1)} %own_planes.1.refs_3_.refs_0_), channel_id=1, source_target_pairs={{0,16},{2,18},{4,8},{6,10},{8,4},{10,6},{12,28},{14,30},{1,5},{3,7... | collective-permute-start | bytes 884744 | tf_op jit(solution)/shard_map/ppermute | solution.py:406
  7.1 2.7 %table.1 = (bf16[2,256,256]{2,1,0:T(8,128)(2,1)S(1)}, bf16[2,256,256]{2,1,0:T(8,128)(2,1)S(1)}, bf16[2,256,256]{2,1,0:T(8,128)(2,1)S(1)}, bf16[2,256,256]{2,1,0:...) custom-call(s32[1,8]{1,0:T(1,128)} %refs_0_.1, s32[1,8]{1,0:T(1,128)} %refs_1_.1, ...), custom_call_target="tpu_custom_call" | custom-call | tf_op jit(solution)/shard_map/table/pallas_call | solution.py:437
  9.8 0.1 collective-permute-start.3
  9.9 0.5 %collective-permute-start.4 = (bf16[2,256,256]{2,1,0:T(8,128)(2,1)S(1)}, bf16[2,256,256]{2,1,0:T(8,128)(2,1)S(1)}, u32[]{:S(2)}, u32[]{:S(2)}) collective-permute-start(bf16[2,256,256]{2,1,0:T(8,128)(2,1)S(1)} %get-tuple-element.18), channel_id=1, source_target_pairs={{0,1},{1,0},{2,3},{3,2},{4,5},{5,4},{6,7},{7,6},{8,9},{9,8},{10,11... | collective-permute-start | bytes 786440 | tf_op jit(solution)/shard_map/ppermute | solution.py:55
  10.4 0.6 %collective-permute-done.refs_1_.refs_0_ = bf16[1152,128]{1,0:T(8,128)(2,1)S(1)} collective-permute-done((bf16[1152,128]{1,0:T(8,128)(2,1)S(1)}, bf16[1152,128]{1,0:T(8,128)(2,1)S(1)}, u32[]{:S(2)}, u32[]{:S(2)}) %collective-permute-start) | collective-permute-done | bytes 294944 | tf_op jit(solution)/shard_map/ppermute | solution.py:406
  11.0 1.9 %collective-permute-start.8 = (bf16[1056,128]{1,0:T(8,128)(2,1)S(1)}, bf16[1056,128]{1,0:T(8,128)(2,1)S(1)}, u32[]{:S(2)}, u32[]{:S(2)}) collective-permute-start(bf16[1056,128]{1,0:T(8,128)(2,1)S(1)} %cut.3), channel_id=1, source_target_pairs={{0,4},{2,6},{4,0},{6,2},{8,12},{10,14},{12,8},{14,10},{1,17},{3,19... | collective-permute-start | bytes 811016 | tf_op jit(solution)/shard_map/ppermute | solution.py:406
  12.9 1.5 %collective-permute-start.9 = (bf16[1056,128]{1,0:T(8,128)(2,1)S(1)}, bf16[1056,128]{1,0:T(8,128)(2,1)S(1)}, u32[]{:S(2)}, u32[]{:S(2)}) collective-permute-start(bf16[1056,128]{1,0:T(8,128)(2,1)S(1)} %cut.3), channel_id=1, source_target_pairs={{0,16},{2,18},{4,8},{6,10},{8,4},{10,6},{12,28},{14,30},{1,5},{3,7... | collective-permute-start | bytes 811016 | tf_op jit(solution)/shard_map/ppermute | solution.py:406
  14.4 0.5 %collective-permute-start.6 = (bf16[2,256,256]{2,1,0:T(8,128)(2,1)S(1)}, bf16[2,256,256]{2,1,0:T(8,128)(2,1)S(1)}, u32[]{:S(2)}, u32[]{:S(2)}) collective-permute-start(bf16[2,256,256]{2,1,0:T(8,128)(2,1)S(1)} %get-tuple-element.20), channel_id=1, source_target_pairs={{0,1},{1,0},{2,3},{3,2},{4,5},{5,4},{6,7},{7,6},{8,9},{9,8},{10,11... | collective-permute-start | bytes 786440 | tf_op jit(solution)/shard_map/ppermute | solution.py:55
  15.0 1.6 %collective-permute-start.7 = (bf16[192,128]{1,0:T(8,128)(2,1)S(1)}, bf16[192,128]{1,0:T(8,128)(2,1)S(1)}, u32[]{:S(2)}, u32[]{:S(2)}) collective-permute-start(bf16[192,128]{1,0:T(8,128)(2,1)S(1)} %cut.2), channel_id=1, source_target_pairs={{0,2},{2,0},{4,6},{6,4},{8,10},{10,8},{12,14},{14,12},{1,3},{3,1},... | collective-permute-start | bytes 147464 | tf_op jit(solution)/shard_map/ppermute | solution.py:406
  16.5 2.5 %near_part.1.acc = f32[256,256]{1,0:T(8,128)S(1)} custom-call(s32[5,8]{1,0:T(8,128)S(4)} %get-tuple-element.15.meta, bf16[8,4,256,256]{3,2,1,0:T(8,128)(2,1)S(1)} %get-tuple-element.16.tiles, bf16[1152,128]{1,0:T(8,128)(2,1)S(1)} %own_planes.1.refs_3_.refs_0_, bf16[1152,128]{1,0:T(8,128)(2,1)S(1)} %collective-permute-done.refs_1_.refs_0_, ...), custom_call_target="tpu_custom_call" | custom-call | tf_op jit(solution)/shard_map/near_part/pallas_call | solution.py:241
  19.0 1.6 %swapped_part.1 = (bf16[8,256,256]{2,1,0:T(8,128)(2,1)S(1)}, f32[256,256]{1,0:T(8,128)S(1)}) custom-call(s32[5,8]{1,0:T(8,128)S(4)} %get-tuple-element.15.meta, bf16[8,4,256,256]{3,2,1,0:T(8,128)(2,1)S(1)} %get-tuple-element.16.tiles, f32[256,256]{1,0:T(8,128)S(1)} %near_part.1.acc, bf16[1152,128]{1,0:T(8,128)(2,1)S(1)} %own_planes.1.refs_3_.refs_0_, ...), custom_call_target="tpu_custom_call" | custom-call | tf_op jit(solution)/shard_map/swapped_part/pallas_call | solution.py:176
  20.6 0.0 copy-start
  20.7 0.6 %relayed_part.1 = (f32[256,128]{1,0:T(8,128)S(1)}, f32[256,128]{1,0:T(8,128)S(1)}) custom-call(s32[5,8]{1,0:T(8,128)S(4)} %get-tuple-element.15.meta, bf16[8,4,256,256]{3,2,1,0:T(8,128)(2,1)S(1)} %get-tuple-element.16.tiles, bf16[8,256,256]{2,1,0:T(8,128)(2,1)S(1)} %get-tuple-element.21.extra, f32[256,256]{1,0:T(8,128)S(1)} %get-tuple-element.22.acc, ...), custom_call_target="tpu_custom_call" | custom-call | tf_op jit(solution)/shard_map/relayed_part/pallas_call | solution.py:316
  21.4 0.1 collective-permute-start.10
  21.4 1.3 %collective-permute-done.10.other = f32[256,128]{1,0:T(8,128)S(1)} collective-permute-done((f32[256,128]{1,0:T(8,128)S(1)}, f32[256,128]{1,0:T(8,128)S(1)}, u32[]{:S(2)}, u32[]{:S(2)}) %collective-permute-start.10) | collective-permute-done | bytes 131104 | tf_op jit(solution)/shard_map/ppermute | solution.py:55
  22.8 0.2 first_currents.1.source.first
  23.0 0.7 %collective-permute-start.13 = (bf16[256,128]{1,0:T(8,128)(2,1)S(1)}, bf16[256,128]{1,0:T(8,128)(2,1)S(1)}, u32[]{:S(2)}, u32[]{:S(2)}) collective-permute-start(bf16[256,128]{1,0:T(8,128)(2,1)S(1)} %first_currents.1.source.first), channel_id=1, source_target_pairs={{0,16},{2,18},{4,8},{6,10},{8,4},{10,6},{12,28},{14,30},{1,7},{3,5... | collective-permute-start | bytes 196616 | tf_op jit(solution)/shard_map/ppermute | solution.py:406
  23.7 1.5 %collective-permute-start.12 = (bf16[256,128]{1,0:T(8,128)(2,1)S(1)}, bf16[256,128]{1,0:T(8,128)(2,1)S(1)}, u32[]{:S(2)}, u32[]{:S(2)}) collective-permute-start(bf16[256,128]{1,0:T(8,128)(2,1)S(1)} %first_currents.1.source.first), channel_id=1, source_target_pairs={{0,2},{2,0},{4,6},{6,4},{8,10},{10,8},{12,14},{14,12},{1,17},{3,19... | collective-permute-start | bytes 196616 | tf_op jit(solution)/shard_map/ppermute | solution.py:406
  25.2 1.6 %collective-permute-start.11 = (bf16[256,128]{1,0:T(8,128)(2,1)S(1)}, bf16[256,128]{1,0:T(8,128)(2,1)S(1)}, u32[]{:S(2)}, u32[]{:S(2)}) collective-permute-start(bf16[256,128]{1,0:T(8,128)(2,1)S(1)} %first_currents.1.source.first), channel_id=1, source_target_pairs={{0,4},{2,6},{4,0},{6,2},{8,12},{10,14},{12,8},{14,10},{1,17},{3,19... | collective-permute-start | bytes 196616 | tf_op jit(solution)/shard_map/ppermute | solution.py:406
  26.7 0.1 fresh_part.4.acc
  26.9 0.8 %collective-permute-done.13.source = bf16[256,128]{1,0:T(8,128)(2,1)S(1)} collective-permute-done((bf16[256,128]{1,0:T(8,128)(2,1)S(1)}, bf16[256,128]{1,0:T(8,128)(2,1)S(1)}, u32[]{:S(2)}, u32[]{:S(2)}) %collective-permute-start.13) | collective-permute-done | bytes 65568 | tf_op jit(solution)/shard_map/ppermute | solution.py:406
  27.6 0.1 fresh_part.5.acc
  27.8 0.3 %collective-permute-done.12.source = bf16[256,128]{1,0:T(8,128)(2,1)S(1)} collective-permute-done((bf16[256,128]{1,0:T(8,128)(2,1)S(1)}, bf16[256,128]{1,0:T(8,128)(2,1)S(1)}, u32[]{:S(2)}, u32[]{:S(2)}) %collective-permute-start.12) | collective-permute-done | bytes 65568 | tf_op jit(solution)/shard_map/ppermute | solution.py:406
  28.1 0.3 fresh_part.6.acc
  28.4 1.0 %collective-permute-done.11.source = bf16[256,128]{1,0:T(8,128)(2,1)S(1)} collective-permute-done((bf16[256,128]{1,0:T(8,128)(2,1)S(1)}, bf16[256,128]{1,0:T(8,128)(2,1)S(1)}, u32[]{:S(2)}, u32[]{:S(2)}) %collective-permute-start.11) | collective-permute-done | bytes 65568 | tf_op jit(solution)/shard_map/ppermute | solution.py:406
  29.4 0.3 fresh_part.7.mine
  29.7 0.1 collective-permute-start.14
  29.8 1.3 %collective-permute-done.14.other = f32[256,128]{1,0:T(8,128)S(1)} collective-permute-done((f32[256,128]{1,0:T(8,128)S(1)}, f32[256,128]{1,0:T(8,128)S(1)}, u32[]{:S(2)}, u32[]{:S(2)}) %collective-permute-start.14) | collective-permute-done | bytes 131104 | tf_op jit(solution)/shard_map/ppermute | solution.py:55
  31.2 0.8 %second_currents.1 = bf16[2,256,128]{2,1,0:T(8,128)(2,1)} custom-call(s32[5,8]{1,0:T(8,128)S(4)} %get-tuple-element.15.meta, bf16[256,128]{1,0:T(8,128)(2,1)S(1)} %first_currents.1.source.first, f32[256,128]{1,0:T(8,128)S(1)} %fresh_part.7.mine, f32[256,128]{1,0:T(8,128)S(1)} %collective-permute-done.14.other, bf16[256,256]{1,0:T(8,128)(2,1)S(1)} %bitcast.6, ...), custom_call_target="tpu_custom_call" | custom-call | tf_op jit(solution)/shard_map/second_currents/pallas_call | solution.py:481
  (17 shorter events, 0.1 us)
Async XLA Ops:
  1.0 10.0 %collective-permute-start = (bf16[1152,128]{1,0:T(8,128)(2,1)S(1)}, bf16[1152,128]{1,0:T(8,128)(2,1)S(1)}, u32[]{:S(2)}, u32[]{:S(2)}) collective-permute-start(bf16[1152,128]{1,0:T(8,128)(2,1)S(1)} %own_planes.1.refs_3_.refs_0_), channel_id=1, source_target_pairs={{0,2},{2,0},{4,6},{6,4},{8,10},{10,8},{12,14},{14,12},{1,3},{3,1},... | collective-permute-start | bytes 884744 | tf_op jit(solution)/shard_map/ppermute | solution.py:406
  4.0 10.4 %collective-permute-start.1 = (bf16[1152,128]{1,0:T(8,128)(2,1)S(1)}, bf16[1152,128]{1,0:T(8,128)(2,1)S(1)}, u32[]{:S(2)}, u32[]{:S(2)}) collective-permute-start(bf16[1152,128]{1,0:T(8,128)(2,1)S(1)} %own_planes.1.refs_3_.refs_0_), channel_id=1, source_target_pairs={{0,4},{2,6},{4,0},{6,2},{8,12},{10,14},{12,8},{14,10},{1,17},{3,19... | collective-permute-start | bytes 884744 | tf_op jit(solution)/shard_map/ppermute | solution.py:406
  5.6 8.9 %collective-permute-start.2 = (bf16[1152,128]{1,0:T(8,128)(2,1)S(1)}, bf16[1152,128]{1,0:T(8,128)(2,1)S(1)}, u32[]{:S(2)}, u32[]{:S(2)}) collective-permute-start(bf16[1152,128]{1,0:T(8,128)(2,1)S(1)} %own_planes.1.refs_3_.refs_0_), channel_id=1, source_target_pairs={{0,16},{2,18},{4,8},{6,10},{8,4},{10,6},{12,28},{14,30},{1,5},{3,7... | collective-permute-start | bytes 884744 | tf_op jit(solution)/shard_map/ppermute | solution.py:406
  9.8 3.1 %collective-permute-start.3 = (bf16[2,256,256]{2,1,0:T(8,128)(2,1)S(1)}, bf16[2,256,256]{2,1,0:T(8,128)(2,1)S(1)}, u32[]{:S(2)}, u32[]{:S(2)}) collective-permute-start(bf16[2,256,256]{2,1,0:T(8,128)(2,1)S(1)} %get-tuple-element.17), channel_id=1, source_target_pairs={{0,1},{1,0},{2,3},{3,2},{4,5},{5,4},{6,7},{7,6},{8,9},{9,8},{10,11... | collective-permute-start | bytes 786440 | tf_op jit(solution)/shard_map/ppermute | solution.py:55
  9.9 5.1 %collective-permute-start.4 = (bf16[2,256,256]{2,1,0:T(8,128)(2,1)S(1)}, bf16[2,256,256]{2,1,0:T(8,128)(2,1)S(1)}, u32[]{:S(2)}, u32[]{:S(2)}) collective-permute-start(bf16[2,256,256]{2,1,0:T(8,128)(2,1)S(1)} %get-tuple-element.18), channel_id=1, source_target_pairs={{0,1},{1,0},{2,3},{3,2},{4,5},{5,4},{6,7},{7,6},{8,9},{9,8},{10,11... | collective-permute-start | bytes 786440 | tf_op jit(solution)/shard_map/ppermute | solution.py:55
  11.0 9.7 %collective-permute-start.8 = (bf16[1056,128]{1,0:T(8,128)(2,1)S(1)}, bf16[1056,128]{1,0:T(8,128)(2,1)S(1)}, u32[]{:S(2)}, u32[]{:S(2)}) collective-permute-start(bf16[1056,128]{1,0:T(8,128)(2,1)S(1)} %cut.3), channel_id=1, source_target_pairs={{0,4},{2,6},{4,0},{6,2},{8,12},{10,14},{12,8},{14,10},{1,17},{3,19... | collective-permute-start | bytes 811016 | tf_op jit(solution)/shard_map/ppermute | solution.py:406
  12.9 7.8 %collective-permute-start.9 = (bf16[1056,128]{1,0:T(8,128)(2,1)S(1)}, bf16[1056,128]{1,0:T(8,128)(2,1)S(1)}, u32[]{:S(2)}, u32[]{:S(2)}) collective-permute-start(bf16[1056,128]{1,0:T(8,128)(2,1)S(1)} %cut.3), channel_id=1, source_target_pairs={{0,16},{2,18},{4,8},{6,10},{8,4},{10,6},{12,28},{14,30},{1,5},{3,7... | collective-permute-start | bytes 811016 | tf_op jit(solution)/shard_map/ppermute | solution.py:406
  14.4 4.5 %collective-permute-start.5 = (bf16[2,256,256]{2,1,0:T(8,128)(2,1)S(1)}, bf16[2,256,256]{2,1,0:T(8,128)(2,1)S(1)}, u32[]{:S(2)}, u32[]{:S(2)}) collective-permute-start(bf16[2,256,256]{2,1,0:T(8,128)(2,1)S(1)} %get-tuple-element.19), channel_id=1, source_target_pairs={{0,1},{1,0},{2,3},{3,2},{4,5},{5,4},{6,7},{7,6},{8,9},{9,8},{10,11... | collective-permute-start | bytes 786440 | tf_op jit(solution)/shard_map/ppermute | solution.py:55
  14.4 4.6 %collective-permute-start.6 = (bf16[2,256,256]{2,1,0:T(8,128)(2,1)S(1)}, bf16[2,256,256]{2,1,0:T(8,128)(2,1)S(1)}, u32[]{:S(2)}, u32[]{:S(2)}) collective-permute-start(bf16[2,256,256]{2,1,0:T(8,128)(2,1)S(1)} %get-tuple-element.20), channel_id=1, source_target_pairs={{0,1},{1,0},{2,3},{3,2},{4,5},{5,4},{6,7},{7,6},{8,9},{9,8},{10,11... | collective-permute-start | bytes 786440 | tf_op jit(solution)/shard_map/ppermute | solution.py:55
  15.0 5.7 %collective-permute-start.7 = (bf16[192,128]{1,0:T(8,128)(2,1)S(1)}, bf16[192,128]{1,0:T(8,128)(2,1)S(1)}, u32[]{:S(2)}, u32[]{:S(2)}) collective-permute-start(bf16[192,128]{1,0:T(8,128)(2,1)S(1)} %cut.2), channel_id=1, source_target_pairs={{0,2},{2,0},{4,6},{6,4},{8,10},{10,8},{12,14},{14,12},{1,3},{3,1},... | collective-permute-start | bytes 147464 | tf_op jit(solution)/shard_map/ppermute | solution.py:406
  20.6 2.1 %copy-start = (bf16[1,256,256]{2,1,0:T(8,128)(2,1)S(1)}, bf16[1,256,256]{2,1,0:T(8,128)(2,1)}, u32[]{:S(2)}) copy-start(bf16[1,256,256]{2,1,0:T(8,128)(2,1)} %param.9) | copy-start | bytes 393220
  20.7 2.1 %copy-start.1 = (f32[2,128]{1,0:T(2,128)S(1)}, f32[2,128]{1,0:T(2,128)}, u32[]{:S(2)}) copy-start(f32[2,128]{1,0:T(2,128)} %wave.3) | copy-start | bytes 3076
  20.7 2.1 %copy-start.2 = (s32[128]{0:T(128)S(1)}, s32[128]{0:T(128)}, u32[]{:S(2)}) copy-start(s32[128]{0:T(128)} %param.12) | copy-start | bytes 1540
  21.4 1.4 %collective-permute-start.10 = (f32[256,128]{1,0:T(8,128)S(1)}, f32[256,128]{1,0:T(8,128)S(1)}, u32[]{:S(2)}, u32[]{:S(2)}) collective-permute-start(f32[256,128]{1,0:T(8,128)S(1)} %get-tuple-element.23.mine), channel_id=1, source_target_pairs={{0,1},{1,0},{2,3},{3,2},{4,5},{5,4},{6,7},{7,6},{8,9},{9,8},{10,11... | collective-permute-start | bytes 393224 | tf_op jit(solution)/shard_map/ppermute | solution.py:55
  23.0 4.6 %collective-permute-start.13 = (bf16[256,128]{1,0:T(8,128)(2,1)S(1)}, bf16[256,128]{1,0:T(8,128)(2,1)S(1)}, u32[]{:S(2)}, u32[]{:S(2)}) collective-permute-start(bf16[256,128]{1,0:T(8,128)(2,1)S(1)} %first_currents.1.source.first), channel_id=1, source_target_pairs={{0,16},{2,18},{4,8},{6,10},{8,4},{10,6},{12,28},{14,30},{1,7},{3,5... | collective-permute-start | bytes 196616 | tf_op jit(solution)/shard_map/ppermute | solution.py:406
  23.7 4.4 %collective-permute-start.12 = (bf16[256,128]{1,0:T(8,128)(2,1)S(1)}, bf16[256,128]{1,0:T(8,128)(2,1)S(1)}, u32[]{:S(2)}, u32[]{:S(2)}) collective-permute-start(bf16[256,128]{1,0:T(8,128)(2,1)S(1)} %first_currents.1.source.first), channel_id=1, source_target_pairs={{0,2},{2,0},{4,6},{6,4},{8,10},{10,8},{12,14},{14,12},{1,17},{3,19... | collective-permute-start | bytes 196616 | tf_op jit(solution)/shard_map/ppermute | solution.py:406
  25.2 4.3 %collective-permute-start.11 = (bf16[256,128]{1,0:T(8,128)(2,1)S(1)}, bf16[256,128]{1,0:T(8,128)(2,1)S(1)}, u32[]{:S(2)}, u32[]{:S(2)}) collective-permute-start(bf16[256,128]{1,0:T(8,128)(2,1)S(1)} %first_currents.1.source.first), channel_id=1, source_target_pairs={{0,4},{2,6},{4,0},{6,2},{8,12},{10,14},{12,8},{14,10},{1,17},{3,19... | collective-permute-start | bytes 196616 | tf_op jit(solution)/shard_map/ppermute | solution.py:406
  29.7 1.4 %collective-permute-start.14 = (f32[256,128]{1,0:T(8,128)S(1)}, f32[256,128]{1,0:T(8,128)S(1)}, u32[]{:S(2)}, u32[]{:S(2)}) collective-permute-start(f32[256,128]{1,0:T(8,128)S(1)} %fresh_part.7.mine), channel_id=1, source_target_pairs={{0,1},{1,0},{2,3},{3,2},{4,5},{5,4},{6,7},{7,6},{8,9},{9,8},{10,11... | collective-permute-start | bytes 393224 | tf_op jit(solution)/shard_map/ppermute | solution.py:55

commit v9 on v8

--- a/solution.py
+++ b/solution.py
@@ -18,7 +18,7 @@
 SLOT, LATE, NEWS, ORDER, PLACE = range(5)
 CHUNK = 2
 PIECES = 4
-HEAD = 96
+HEAD = 112
 
 
 def held(x):
@@ -357,8 +357,6 @@
 
 
 def fresh_kernel(number, meta, tiles, extra, source, acc, out):
-    out[...] = acc[...]
-
     def add(tile):
         out[...] += jnp.dot(tile, source[...], preferred_element_type=jnp.float32)
 
@@ -376,6 +374,7 @@
         out_shape=pltpu.VMEM(acc.shape, acc.dtype),
         in_specs=[SMEM] + [VMEM] * 4,
         out_specs=VMEM,
+        input_output_aliases={4: 0},
         compiler_params=SMALL,
         name="fresh_part",
     )(table(meta), held(tiles), held(extra), held(source), held(acc))

time: 32.2 us -> 31.9 us (level)
  Pallas kernels: 10.3 us -> 9.64 us
  starting transfers between devices: 16 us -> 16.5 us
    pallas_call x4, Pallas kernels: 0.88 us -> 0.2 us  [fresh_part(): pl.pallas_call(functools.partial(fresh_kernel, number), out_shape=pltpu.V...]
    ppermute x9, starting transfers between devices: 14.8 us -> 15.3 us  [send(): return lax.ppermute(x, ALL_AXES, pairs)]
  transfers between devices with their start and end apart: 15 -> 15, of which waited for: 6 -> 6; matrix products, arithmetic and copies ran while one was open for 0% -> 0% of each run, Pallas kernels for 23% -> 21%
where the time goes in v9:
time: 31.9 us
  starting transfers between devices  16.5 us (52%)
  Pallas kernels  9.64 us (30%)
  waiting for transfers between devices  5.58 us (17%)
    ppermute x9, starting transfers between devices, send(): return lax.ppermute(x, ALL_AXES, pairs)  15.3 us
    ppermute x9, waiting for transfers between devices, send(): return lax.ppermute(x, ALL_AXES, pairs)  2.9 us
    ppermute x6, waiting for transfers between devices, swap_cores(): return lax.ppermute(x, 'sub', [(0, 1), (1, 0)])  2.68 us
    pallas_call x1, Pallas kernels, per_device(): pl.pallas_call(functools.partial(table_kernel, slots, news, sites, groups...  2.67 us
    pallas_call x1, Pallas kernels, near_part(): pl.pallas_call(functools.partial(near_kernel, len(sources)), out_shape=pl...  2.46 us
    pallas_call x1, Pallas kernels, swapped_part(): pl.pallas_call(functools.partial(swapped_kernel, len(sources)), out_shape...  1.63 us
    ppermute x6, starting transfers between devices, swap_cores(): return lax.ppermute(x, 'sub', [(0, 1), (1, 0)])  1.22 us
    pallas_call x1, Pallas kernels, per_device(): pl.pallas_call(planes_kernel, out_shape=pltpu.VMEM((taps * rows + rows //...  0.98 us
  transfers between devices with their start and end apart: 15, of which 6 were waited for; matrix products, arithmetic and copies ran while one was open for 0% of the time, Pallas kernels for 21%

profile of v9, /device:TPU:0, one launch (start us, length us, event | category | flops | bytes accessed | tf_op | source)
XLA Modules:
  0.0 31.9 jit_solution(16533243311985644560)
XLA Ops:
  0.0 1.0 %own_planes.1.refs_3_.refs_0_ = bf16[1152,128]{1,0:T(8,128)(2,1)S(1)} custom-call(bf16[9,256,128]{2,1,0:T(8,128)(2,1)} %bitcast.10), custom_call_target="tpu_custom_call" | custom-call | tf_op jit(solution)/shard_map/own_planes/pallas_call | solution.py:427
  1.0 3.0 %collective-permute-start = (bf16[1152,128]{1,0:T(8,128)(2,1)S(1)}, bf16[1152,128]{1,0:T(8,128)(2,1)S(1)}, u32[]{:S(2)}, u32[]{:S(2)}) collective-permute-start(bf16[1152,128]{1,0:T(8,128)(2,1)S(1)} %own_planes.1.refs_3_.refs_0_), channel_id=1, source_target_pairs={{0,2},{2,0},{4,6},{6,4},{8,10},{10,8},{12,14},{14,12},{1,3},{3,1},... | collective-permute-start | bytes 884744 | tf_op jit(solution)/shard_map/ppermute | solution.py:405
  4.0 1.6 %collective-permute-start.1 = (bf16[1152,128]{1,0:T(8,128)(2,1)S(1)}, bf16[1152,128]{1,0:T(8,128)(2,1)S(1)}, u32[]{:S(2)}, u32[]{:S(2)}) collective-permute-start(bf16[1152,128]{1,0:T(8,128)(2,1)S(1)} %own_planes.1.refs_3_.refs_0_), channel_id=1, source_target_pairs={{0,4},{2,6},{4,0},{6,2},{8,12},{10,14},{12,8},{14,10},{1,17},{3,19... | collective-permute-start | bytes 884744 | tf_op jit(solution)/shard_map/ppermute | solution.py:405
  5.6 1.5 %collective-permute-start.2 = (bf16[1152,128]{1,0:T(8,128)(2,1)S(1)}, bf16[1152,128]{1,0:T(8,128)(2,1)S(1)}, u32[]{:S(2)}, u32[]{:S(2)}) collective-permute-start(bf16[1152,128]{1,0:T(8,128)(2,1)S(1)} %own_planes.1.refs_3_.refs_0_), channel_id=1, source_target_pairs={{0,16},{2,18},{4,8},{6,10},{8,4},{10,6},{12,28},{14,30},{1,5},{3,7... | collective-permute-start | bytes 884744 | tf_op jit(solution)/shard_map/ppermute | solution.py:405
  7.1 2.7 %table.1 = (bf16[2,256,256]{2,1,0:T(8,128)(2,1)S(1)}, bf16[2,256,256]{2,1,0:T(8,128)(2,1)S(1)}, bf16[2,256,256]{2,1,0:T(8,128)(2,1)S(1)}, bf16[2,256,256]{2,1,0:...) custom-call(s32[1,8]{1,0:T(1,128)} %refs_0_.1, s32[1,8]{1,0:T(1,128)} %refs_1_.1, ...), custom_call_target="tpu_custom_call" | custom-call | tf_op jit(solution)/shard_map/table/pallas_call | solution.py:436
  9.8 0.1 collective-permute-start.3
  9.8 0.5 %collective-permute-start.4 = (bf16[2,256,256]{2,1,0:T(8,128)(2,1)S(1)}, bf16[2,256,256]{2,1,0:T(8,128)(2,1)S(1)}, u32[]{:S(2)}, u32[]{:S(2)}) collective-permute-start(bf16[2,256,256]{2,1,0:T(8,128)(2,1)S(1)} %get-tuple-element.18), channel_id=1, source_target_pairs={{0,1},{1,0},{2,3},{3,2},{4,5},{5,4},{6,7},{7,6},{8,9},{9,8},{10,11... | collective-permute-start | bytes 786440 | tf_op jit(solution)/shard_map/ppermute | solution.py:55
  10.3 0.7 %collective-permute-done.refs_1_.refs_0_ = bf16[1152,128]{1,0:T(8,128)(2,1)S(1)} collective-permute-done((bf16[1152,128]{1,0:T(8,128)(2,1)S(1)}, bf16[1152,128]{1,0:T(8,128)(2,1)S(1)}, u32[]{:S(2)}, u32[]{:S(2)}) %collective-permute-start) | collective-permute-done | bytes 294944 | tf_op jit(solution)/shard_map/ppermute | solution.py:405
  11.0 1.9 %collective-permute-start.8 = (bf16[1040,128]{1,0:T(8,128)(2,1)S(1)}, bf16[1040,128]{1,0:T(8,128)(2,1)S(1)}, u32[]{:S(2)}, u32[]{:S(2)}) collective-permute-start(bf16[1040,128]{1,0:T(8,128)(2,1)S(1)} %cut.3), channel_id=1, source_target_pairs={{0,4},{2,6},{4,0},{6,2},{8,12},{10,14},{12,8},{14,10},{1,17},{3,19... | collective-permute-start | bytes 798728 | tf_op jit(solution)/shard_map/ppermute | solution.py:405
  12.9 0.0 collective-permute-done.3.refs_4_
  12.9 1.5 %collective-permute-start.9 = (bf16[1040,128]{1,0:T(8,128)(2,1)S(1)}, bf16[1040,128]{1,0:T(8,128)(2,1)S(1)}, u32[]{:S(2)}, u32[]{:S(2)}) collective-permute-start(bf16[1040,128]{1,0:T(8,128)(2,1)S(1)} %cut.3), channel_id=1, source_target_pairs={{0,16},{2,18},{4,8},{6,10},{8,4},{10,6},{12,28},{14,30},{1,5},{3,7... | collective-permute-start | bytes 798728 | tf_op jit(solution)/shard_map/ppermute | solution.py:405
  14.4 0.5 %collective-permute-start.6 = (bf16[2,256,256]{2,1,0:T(8,128)(2,1)S(1)}, bf16[2,256,256]{2,1,0:T(8,128)(2,1)S(1)}, u32[]{:S(2)}, u32[]{:S(2)}) collective-permute-start(bf16[2,256,256]{2,1,0:T(8,128)(2,1)S(1)} %get-tuple-element.20), channel_id=1, source_target_pairs={{0,1},{1,0},{2,3},{3,2},{4,5},{5,4},{6,7},{7,6},{8,9},{9,8},{10,11... | collective-permute-start | bytes 786440 | tf_op jit(solution)/shard_map/ppermute | solution.py:55
  15.0 1.6 %collective-permute-start.7 = (bf16[224,128]{1,0:T(8,128)(2,1)S(1)}, bf16[224,128]{1,0:T(8,128)(2,1)S(1)}, u32[]{:S(2)}, u32[]{:S(2)}) collective-permute-start(bf16[224,128]{1,0:T(8,128)(2,1)S(1)} %cut.2), channel_id=1, source_target_pairs={{0,2},{2,0},{4,6},{6,4},{8,10},{10,8},{12,14},{14,12},{1,3},{3,1},... | collective-permute-start | bytes 172040 | tf_op jit(solution)/shard_map/ppermute | solution.py:405
  16.5 2.5 %near_part.1.acc = f32[256,256]{1,0:T(8,128)S(1)} custom-call(s32[5,8]{1,0:T(8,128)S(4)} %get-tuple-element.15.meta, bf16[8,4,256,256]{3,2,1,0:T(8,128)(2,1)S(1)} %get-tuple-element.16.tiles, bf16[1152,128]{1,0:T(8,128)(2,1)S(1)} %own_planes.1.refs_3_.refs_0_, bf16[1152,128]{1,0:T(8,128)(2,1)S(1)} %collective-permute-done.refs_1_.refs_0_, ...), custom_call_target="tpu_custom_call" | custom-call | tf_op jit(solution)/shard_map/near_part/pallas_call | solution.py:241
  19.0 1.6 %swapped_part.1 = (bf16[8,256,256]{2,1,0:T(8,128)(2,1)S(1)}, f32[256,256]{1,0:T(8,128)S(1)}) custom-call(s32[5,8]{1,0:T(8,128)S(4)} %get-tuple-element.15.meta, bf16[8,4,256,256]{3,2,1,0:T(8,128)(2,1)S(1)} %get-tuple-element.16.tiles, f32[256,256]{1,0:T(8,128)S(1)} %near_part.1.acc, bf16[1152,128]{1,0:T(8,128)(2,1)S(1)} %own_planes.1.refs_3_.refs_0_, ...), custom_call_target="tpu_custom_call" | custom-call | tf_op jit(solution)/shard_map/swapped_part/pallas_call | solution.py:176
  20.7 0.0 copy-start
  20.7 0.0 copy-start.1
  20.7 0.0 copy-start.2
  20.7 0.6 %relayed_part.1 = (f32[256,128]{1,0:T(8,128)S(1)}, f32[256,128]{1,0:T(8,128)S(1)}) custom-call(s32[5,8]{1,0:T(8,128)S(4)} %get-tuple-element.15.meta, bf16[8,4,256,256]{3,2,1,0:T(8,128)(2,1)S(1)} %get-tuple-element.16.tiles, bf16[8,256,256]{2,1,0:T(8,128)(2,1)S(1)} %get-tuple-element.21.extra, f32[256,256]{1,0:T(8,128)S(1)} %get-tuple-element.22.acc, ...), custom_call_target="tpu_custom_call" | custom-call | tf_op jit(solution)/shard_map/relayed_part/pallas_call | solution.py:316
  21.4 0.1 collective-permute-start.10
  21.4 1.3 %collective-permute-done.10.other = f32[256,128]{1,0:T(8,128)S(1)} collective-permute-done((f32[256,128]{1,0:T(8,128)S(1)}, f32[256,128]{1,0:T(8,128)S(1)}, u32[]{:S(2)}, u32[]{:S(2)}) %collective-permute-start.10) | collective-permute-done | bytes 131104 | tf_op jit(solution)/shard_map/ppermute | solution.py:55
  22.8 0.2 first_currents.1.source.first
  23.0 0.6 %collective-permute-start.13 = (bf16[256,128]{1,0:T(8,128)(2,1)S(1)}, bf16[256,128]{1,0:T(8,128)(2,1)S(1)}, u32[]{:S(2)}, u32[]{:S(2)}) collective-permute-start(bf16[256,128]{1,0:T(8,128)(2,1)S(1)} %first_currents.1.source.first), channel_id=1, source_target_pairs={{0,16},{2,18},{4,8},{6,10},{8,4},{10,6},{12,28},{14,30},{1,7},{3,5... | collective-permute-start | bytes 196616 | tf_op jit(solution)/shard_map/ppermute | solution.py:405
  23.6 1.0 %collective-permute-start.12 = (bf16[256,128]{1,0:T(8,128)(2,1)S(1)}, bf16[256,128]{1,0:T(8,128)(2,1)S(1)}, u32[]{:S(2)}, u32[]{:S(2)}) collective-permute-start(bf16[256,128]{1,0:T(8,128)(2,1)S(1)} %first_currents.1.source.first), channel_id=1, source_target_pairs={{0,2},{2,0},{4,6},{6,4},{8,10},{10,8},{12,14},{14,12},{1,17},{3,19... | collective-permute-start | bytes 196616 | tf_op jit(solution)/shard_map/ppermute | solution.py:405
  24.6 2.6 %collective-permute-start.11 = (bf16[256,128]{1,0:T(8,128)(2,1)S(1)}, bf16[256,128]{1,0:T(8,128)(2,1)S(1)}, u32[]{:S(2)}, u32[]{:S(2)}) collective-permute-start(bf16[256,128]{1,0:T(8,128)(2,1)S(1)} %first_currents.1.source.first), channel_id=1, source_target_pairs={{0,4},{2,6},{4,0},{6,2},{8,12},{10,14},{12,8},{14,10},{1,17},{3,19... | collective-permute-start | bytes 196616 | tf_op jit(solution)/shard_map/ppermute | solution.py:405
  27.2 0.3 %collective-permute-done.13.source = bf16[256,128]{1,0:T(8,128)(2,1)S(1)} collective-permute-done((bf16[256,128]{1,0:T(8,128)(2,1)S(1)}, bf16[256,128]{1,0:T(8,128)(2,1)S(1)}, u32[]{:S(2)}, u32[]{:S(2)}) %collective-permute-start.13) | collective-permute-done | bytes 65568 | tf_op jit(solution)/shard_map/ppermute | solution.py:405
  27.5 0.6 %collective-permute-done.12.source = bf16[256,128]{1,0:T(8,128)(2,1)S(1)} collective-permute-done((bf16[256,128]{1,0:T(8,128)(2,1)S(1)}, bf16[256,128]{1,0:T(8,128)(2,1)S(1)}, u32[]{:S(2)}, u32[]{:S(2)}) %collective-permute-start.12) | collective-permute-done | bytes 65568 | tf_op jit(solution)/shard_map/ppermute | solution.py:405
  28.1 1.3 %collective-permute-done.11.source = bf16[256,128]{1,0:T(8,128)(2,1)S(1)} collective-permute-done((bf16[256,128]{1,0:T(8,128)(2,1)S(1)}, bf16[256,128]{1,0:T(8,128)(2,1)S(1)}, u32[]{:S(2)}, u32[]{:S(2)}) %collective-permute-start.11) | collective-permute-done | bytes 65568 | tf_op jit(solution)/shard_map/ppermute | solution.py:405
  29.4 0.2 fresh_part.7.mine
  29.6 0.1 collective-permute-start.14
  29.7 1.3 %collective-permute-done.14.other = f32[256,128]{1,0:T(8,128)S(1)} collective-permute-done((f32[256,128]{1,0:T(8,128)S(1)}, f32[256,128]{1,0:T(8,128)S(1)}, u32[]{:S(2)}, u32[]{:S(2)}) %collective-permute-start.14) | collective-permute-done | bytes 131104 | tf_op jit(solution)/shard_map/ppermute | solution.py:55
  31.0 0.8 %second_currents.1 = bf16[2,256,128]{2,1,0:T(8,128)(2,1)} custom-call(s32[5,8]{1,0:T(8,128)S(4)} %get-tuple-element.15.meta, bf16[256,128]{1,0:T(8,128)(2,1)S(1)} %first_currents.1.source.first, f32[256,128]{1,0:T(8,128)S(1)} %fresh_part.7.mine, f32[256,128]{1,0:T(8,128)S(1)} %collective-permute-done.14.other, bf16[256,256]{1,0:T(8,128)(2,1)S(1)} %bitcast.6, ...), custom_call_target="tpu_custom_call" | custom-call | tf_op jit(solution)/shard_map/second_currents/pallas_call | solution.py:480
  (17 shorter events, 0.1 us)
Async XLA Ops:
  1.0 10.0 %collective-permute-start = (bf16[1152,128]{1,0:T(8,128)(2,1)S(1)}, bf16[1152,128]{1,0:T(8,128)(2,1)S(1)}, u32[]{:S(2)}, u32[]{:S(2)}) collective-permute-start(bf16[1152,128]{1,0:T(8,128)(2,1)S(1)} %own_planes.1.refs_3_.refs_0_), channel_id=1, source_target_pairs={{0,2},{2,0},{4,6},{6,4},{8,10},{10,8},{12,14},{14,12},{1,3},{3,1},... | collective-permute-start | bytes 884744 | tf_op jit(solution)/shard_map/ppermute | solution.py:405
  4.0 10.4 %collective-permute-start.1 = (bf16[1152,128]{1,0:T(8,128)(2,1)S(1)}, bf16[1152,128]{1,0:T(8,128)(2,1)S(1)}, u32[]{:S(2)}, u32[]{:S(2)}) collective-permute-start(bf16[1152,128]{1,0:T(8,128)(2,1)S(1)} %own_planes.1.refs_3_.refs_0_), channel_id=1, source_target_pairs={{0,4},{2,6},{4,0},{6,2},{8,12},{10,14},{12,8},{14,10},{1,17},{3,19... | collective-permute-start | bytes 884744 | tf_op jit(solution)/shard_map/ppermute | solution.py:405
  5.6 8.9 %collective-permute-start.2 = (bf16[1152,128]{1,0:T(8,128)(2,1)S(1)}, bf16[1152,128]{1,0:T(8,128)(2,1)S(1)}, u32[]{:S(2)}, u32[]{:S(2)}) collective-permute-start(bf16[1152,128]{1,0:T(8,128)(2,1)S(1)} %own_planes.1.refs_3_.refs_0_), channel_id=1, source_target_pairs={{0,16},{2,18},{4,8},{6,10},{8,4},{10,6},{12,28},{14,30},{1,5},{3,7... | collective-permute-start | bytes 884744 | tf_op jit(solution)/shard_map/ppermute | solution.py:405
  9.8 3.1 %collective-permute-start.3 = (bf16[2,256,256]{2,1,0:T(8,128)(2,1)S(1)}, bf16[2,256,256]{2,1,0:T(8,128)(2,1)S(1)}, u32[]{:S(2)}, u32[]{:S(2)}) collective-permute-start(bf16[2,256,256]{2,1,0:T(8,128)(2,1)S(1)} %get-tuple-element.17), channel_id=1, source_target_pairs={{0,1},{1,0},{2,3},{3,2},{4,5},{5,4},{6,7},{7,6},{8,9},{9,8},{10,11... | collective-permute-start | bytes 786440 | tf_op jit(solution)/shard_map/ppermute | solution.py:55
  9.8 5.1 %collective-permute-start.4 = (bf16[2,256,256]{2,1,0:T(8,128)(2,1)S(1)}, bf16[2,256,256]{2,1,0:T(8,128)(2,1)S(1)}, u32[]{:S(2)}, u32[]{:S(2)}) collective-permute-start(bf16[2,256,256]{2,1,0:T(8,128)(2,1)S(1)} %get-tuple-element.18), channel_id=1, source_target_pairs={{0,1},{1,0},{2,3},{3,2},{4,5},{5,4},{6,7},{7,6},{8,9},{9,8},{10,11... | collective-permute-start | bytes 786440 | tf_op jit(solution)/shard_map/ppermute | solution.py:55
  11.0 9.7 %collective-permute-start.8 = (bf16[1040,128]{1,0:T(8,128)(2,1)S(1)}, bf16[1040,128]{1,0:T(8,128)(2,1)S(1)}, u32[]{:S(2)}, u32[]{:S(2)}) collective-permute-start(bf16[1040,128]{1,0:T(8,128)(2,1)S(1)} %cut.3), channel_id=1, source_target_pairs={{0,4},{2,6},{4,0},{6,2},{8,12},{10,14},{12,8},{14,10},{1,17},{3,19... | collective-permute-start | bytes 798728 | tf_op jit(solution)/shard_map/ppermute | solution.py:405
  12.9 7.8 %collective-permute-start.9 = (bf16[1040,128]{1,0:T(8,128)(2,1)S(1)}, bf16[1040,128]{1,0:T(8,128)(2,1)S(1)}, u32[]{:S(2)}, u32[]{:S(2)}) collective-permute-start(bf16[1040,128]{1,0:T(8,128)(2,1)S(1)} %cut.3), channel_id=1, source_target_pairs={{0,16},{2,18},{4,8},{6,10},{8,4},{10,6},{12,28},{14,30},{1,5},{3,7... | collective-permute-start | bytes 798728 | tf_op jit(solution)/shard_map/ppermute | solution.py:405
  14.4 4.6 %collective-permute-start.5 = (bf16[2,256,256]{2,1,0:T(8,128)(2,1)S(1)}, bf16[2,256,256]{2,1,0:T(8,128)(2,1)S(1)}, u32[]{:S(2)}, u32[]{:S(2)}) collective-permute-start(bf16[2,256,256]{2,1,0:T(8,128)(2,1)S(1)} %get-tuple-element.19), channel_id=1, source_target_pairs={{0,1},{1,0},{2,3},{3,2},{4,5},{5,4},{6,7},{7,6},{8,9},{9,8},{10,11... | collective-permute-start | bytes 786440 | tf_op jit(solution)/shard_map/ppermute | solution.py:55
  14.4 4.6 %collective-permute-start.6 = (bf16[2,256,256]{2,1,0:T(8,128)(2,1)S(1)}, bf16[2,256,256]{2,1,0:T(8,128)(2,1)S(1)}, u32[]{:S(2)}, u32[]{:S(2)}) collective-permute-start(bf16[2,256,256]{2,1,0:T(8,128)(2,1)S(1)} %get-tuple-element.20), channel_id=1, source_target_pairs={{0,1},{1,0},{2,3},{3,2},{4,5},{5,4},{6,7},{7,6},{8,9},{9,8},{10,11... | collective-permute-start | bytes 786440 | tf_op jit(solution)/shard_map/ppermute | solution.py:55
  15.0 5.7 %collective-permute-start.7 = (bf16[224,128]{1,0:T(8,128)(2,1)S(1)}, bf16[224,128]{1,0:T(8,128)(2,1)S(1)}, u32[]{:S(2)}, u32[]{:S(2)}) collective-permute-start(bf16[224,128]{1,0:T(8,128)(2,1)S(1)} %cut.2), channel_id=1, source_target_pairs={{0,2},{2,0},{4,6},{6,4},{8,10},{10,8},{12,14},{14,12},{1,3},{3,1},... | collective-permute-start | bytes 172040 | tf_op jit(solution)/shard_map/ppermute | solution.py:405
  20.7 2.1 %copy-start = (bf16[1,256,256]{2,1,0:T(8,128)(2,1)S(1)}, bf16[1,256,256]{2,1,0:T(8,128)(2,1)}, u32[]{:S(2)}) copy-start(bf16[1,256,256]{2,1,0:T(8,128)(2,1)} %param.9) | copy-start | bytes 393220
  20.7 2.1 %copy-start.1 = (f32[2,128]{1,0:T(2,128)S(1)}, f32[2,128]{1,0:T(2,128)}, u32[]{:S(2)}) copy-start(f32[2,128]{1,0:T(2,128)} %wave.3) | copy-start | bytes 3076
  20.7 2.1 %copy-start.2 = (s32[128]{0:T(128)S(1)}, s32[128]{0:T(128)}, u32[]{:S(2)}) copy-start(s32[128]{0:T(128)} %param.12) | copy-start | bytes 1540
  21.4 1.4 %collective-permute-start.10 = (f32[256,128]{1,0:T(8,128)S(1)}, f32[256,128]{1,0:T(8,128)S(1)}, u32[]{:S(2)}, u32[]{:S(2)}) collective-permute-start(f32[256,128]{1,0:T(8,128)S(1)} %get-tuple-element.23.mine), channel_id=1, source_target_pairs={{0,1},{1,0},{2,3},{3,2},{4,5},{5,4},{6,7},{7,6},{8,9},{9,8},{10,11... | collective-permute-start | bytes 393224 | tf_op jit(solution)/shard_map/ppermute | solution.py:55
  23.0 4.5 %collective-permute-start.13 = (bf16[256,128]{1,0:T(8,128)(2,1)S(1)}, bf16[256,128]{1,0:T(8,128)(2,1)S(1)}, u32[]{:S(2)}, u32[]{:S(2)}) collective-permute-start(bf16[256,128]{1,0:T(8,128)(2,1)S(1)} %first_currents.1.source.first), channel_id=1, source_target_pairs={{0,16},{2,18},{4,8},{6,10},{8,4},{10,6},{12,28},{14,30},{1,7},{3,5... | collective-permute-start | bytes 196616 | tf_op jit(solution)/shard_map/ppermute | solution.py:405
  23.6 4.5 %collective-permute-start.12 = (bf16[256,128]{1,0:T(8,128)(2,1)S(1)}, bf16[256,128]{1,0:T(8,128)(2,1)S(1)}, u32[]{:S(2)}, u32[]{:S(2)}) collective-permute-start(bf16[256,128]{1,0:T(8,128)(2,1)S(1)} %first_currents.1.source.first), channel_id=1, source_target_pairs={{0,2},{2,0},{4,6},{6,4},{8,10},{10,8},{12,14},{14,12},{1,17},{3,19... | collective-permute-start | bytes 196616 | tf_op jit(solution)/shard_map/ppermute | solution.py:405
  24.6 4.9 %collective-permute-start.11 = (bf16[256,128]{1,0:T(8,128)(2,1)S(1)}, bf16[256,128]{1,0:T(8,128)(2,1)S(1)}, u32[]{:S(2)}, u32[]{:S(2)}) collective-permute-start(bf16[256,128]{1,0:T(8,128)(2,1)S(1)} %first_currents.1.source.first), channel_id=1, source_target_pairs={{0,4},{2,6},{4,0},{6,2},{8,12},{10,14},{12,8},{14,10},{1,17},{3,19... | collective-permute-start | bytes 196616 | tf_op jit(solution)/shard_map/ppermute | solution.py:405
  29.6 1.4 %collective-permute-start.14 = (f32[256,128]{1,0:T(8,128)S(1)}, f32[256,128]{1,0:T(8,128)S(1)}, u32[]{:S(2)}, u32[]{:S(2)}) collective-permute-start(f32[256,128]{1,0:T(8,128)S(1)} %fresh_part.7.mine), channel_id=1, source_target_pairs={{0,1},{1,0},{2,3},{3,2},{4,5},{5,4},{6,7},{7,6},{8,9},{9,8},{10,11... | collective-permute-start | bytes 393224 | tf_op jit(solution)/shard_map/ppermute | solution.py:55

commit v10 on v9

--- a/solution.py
+++ b/solution.py
@@ -18,7 +18,7 @@
 SLOT, LATE, NEWS, ORDER, PLACE = range(5)
 CHUNK = 2
 PIECES = 4
-HEAD = 112
+HEAD = 96
 
 
 def held(x):

time: 31.9 us -> 32 us (level)
    pallas_call x4, Pallas kernels: 0.2 us -> 0.7 us  [fresh_part(): pl.pallas_call(functools.partial(fresh_kernel, number), out_shape=pltpu.V...]
where the time goes in v10:
time: 32 us; the launch traced here: 31.9 us
  starting transfers between devices  16.5 us (52%)
  Pallas kernels  9.7 us (30%)
  waiting for transfers between devices  5.56 us (17%)
    ppermute x9, starting transfers between devices, send(): return lax.ppermute(x, ALL_AXES, pairs)  15.3 us
    ppermute x9, waiting for transfers between devices, send(): return lax.ppermute(x, ALL_AXES, pairs)  2.88 us
    ppermute x6, waiting for transfers between devices, swap_cores(): return lax.ppermute(x, 'sub', [(0, 1), (1, 0)])  2.68 us
    pallas_call x1, Pallas kernels, per_device(): pl.pallas_call(functools.partial(table_kernel, slots, news, sites, groups...  2.67 us
    pallas_call x1, Pallas kernels, near_part(): pl.pallas_call(functools.partial(near_kernel, len(sources)), out_shape=pl...  2.16 us
    pallas_call x1, Pallas kernels, swapped_part(): pl.pallas_call(functools.partial(swapped_kernel, len(sources)), out_shape...  1.5 us
    ppermute x6, starting transfers between devices, swap_cores(): return lax.ppermute(x, 'sub', [(0, 1), (1, 0)])  1.22 us
    pallas_call x1, Pallas kernels, per_device(): pl.pallas_call(planes_kernel, out_shape=pltpu.VMEM((taps * rows + rows //...  0.98 us
  transfers between devices with their start and end apart: 15, of which 6 were waited for; matrix products, arithmetic and copies ran while one was open for 0% of the time, Pallas kernels for 21%

profile of v10, /device:TPU:0, one launch (start us, length us, event | category | flops | bytes accessed | tf_op | source)
XLA Modules:
  0.0 31.9 jit_solution(2365292473639865757)
XLA Ops:
  0.0 1.0 %own_planes.1.refs_3_.refs_0_ = bf16[1152,128]{1,0:T(8,128)(2,1)S(1)} custom-call(bf16[9,256,128]{2,1,0:T(8,128)(2,1)} %bitcast.10), custom_call_target="tpu_custom_call" | custom-call | tf_op jit(solution)/shard_map/own_planes/pallas_call | solution.py:427
  1.0 3.0 %collective-permute-start = (bf16[1152,128]{1,0:T(8,128)(2,1)S(1)}, bf16[1152,128]{1,0:T(8,128)(2,1)S(1)}, u32[]{:S(2)}, u32[]{:S(2)}) collective-permute-start(bf16[1152,128]{1,0:T(8,128)(2,1)S(1)} %own_planes.1.refs_3_.refs_0_), channel_id=1, source_target_pairs={{0,2},{2,0},{4,6},{6,4},{8,10},{10,8},{12,14},{14,12},{1,3},{3,1},... | collective-permute-start | bytes 884744 | tf_op jit(solution)/shard_map/ppermute | solution.py:405
  4.0 1.6 %collective-permute-start.1 = (bf16[1152,128]{1,0:T(8,128)(2,1)S(1)}, bf16[1152,128]{1,0:T(8,128)(2,1)S(1)}, u32[]{:S(2)}, u32[]{:S(2)}) collective-permute-start(bf16[1152,128]{1,0:T(8,128)(2,1)S(1)} %own_planes.1.refs_3_.refs_0_), channel_id=1, source_target_pairs={{0,4},{2,6},{4,0},{6,2},{8,12},{10,14},{12,8},{14,10},{1,17},{3,19... | collective-permute-start | bytes 884744 | tf_op jit(solution)/shard_map/ppermute | solution.py:405
  5.6 1.5 %collective-permute-start.2 = (bf16[1152,128]{1,0:T(8,128)(2,1)S(1)}, bf16[1152,128]{1,0:T(8,128)(2,1)S(1)}, u32[]{:S(2)}, u32[]{:S(2)}) collective-permute-start(bf16[1152,128]{1,0:T(8,128)(2,1)S(1)} %own_planes.1.refs_3_.refs_0_), channel_id=1, source_target_pairs={{0,16},{2,18},{4,8},{6,10},{8,4},{10,6},{12,28},{14,30},{1,5},{3,7... | collective-permute-start | bytes 884744 | tf_op jit(solution)/shard_map/ppermute | solution.py:405
  7.1 2.7 %table.1 = (bf16[2,256,256]{2,1,0:T(8,128)(2,1)S(1)}, bf16[2,256,256]{2,1,0:T(8,128)(2,1)S(1)}, bf16[2,256,256]{2,1,0:T(8,128)(2,1)S(1)}, bf16[2,256,256]{2,1,0:...) custom-call(s32[1,8]{1,0:T(1,128)} %refs_0_.1, s32[1,8]{1,0:T(1,128)} %refs_1_.1, ...), custom_call_target="tpu_custom_call" | custom-call | tf_op jit(solution)/shard_map/table/pallas_call | solution.py:436
  9.8 0.1 collective-permute-start.3
  9.8 0.5 %collective-permute-start.4 = (bf16[2,256,256]{2,1,0:T(8,128)(2,1)S(1)}, bf16[2,256,256]{2,1,0:T(8,128)(2,1)S(1)}, u32[]{:S(2)}, u32[]{:S(2)}) collective-permute-start(bf16[2,256,256]{2,1,0:T(8,128)(2,1)S(1)} %get-tuple-element.18), channel_id=1, source_target_pairs={{0,1},{1,0},{2,3},{3,2},{4,5},{5,4},{6,7},{7,6},{8,9},{9,8},{10,11... | collective-permute-start | bytes 786440 | tf_op jit(solution)/shard_map/ppermute | solution.py:55
  10.3 0.7 %collective-permute-done.refs_1_.refs_0_ = bf16[1152,128]{1,0:T(8,128)(2,1)S(1)} collective-permute-done((bf16[1152,128]{1,0:T(8,128)(2,1)S(1)}, bf16[1152,128]{1,0:T(8,128)(2,1)S(1)}, u32[]{:S(2)}, u32[]{:S(2)}) %collective-permute-start) | collective-permute-done | bytes 294944 | tf_op jit(solution)/shard_map/ppermute | solution.py:405
  11.0 1.9 %collective-permute-start.8 = (bf16[1056,128]{1,0:T(8,128)(2,1)S(1)}, bf16[1056,128]{1,0:T(8,128)(2,1)S(1)}, u32[]{:S(2)}, u32[]{:S(2)}) collective-permute-start(bf16[1056,128]{1,0:T(8,128)(2,1)S(1)} %cut.3), channel_id=1, source_target_pairs={{0,4},{2,6},{4,0},{6,2},{8,12},{10,14},{12,8},{14,10},{1,17},{3,19... | collective-permute-start | bytes 811016 | tf_op jit(solution)/shard_map/ppermute | solution.py:405
  12.9 1.5 %collective-permute-start.9 = (bf16[1056,128]{1,0:T(8,128)(2,1)S(1)}, bf16[1056,128]{1,0:T(8,128)(2,1)S(1)}, u32[]{:S(2)}, u32[]{:S(2)}) collective-permute-start(bf16[1056,128]{1,0:T(8,128)(2,1)S(1)} %cut.3), channel_id=1, source_target_pairs={{0,16},{2,18},{4,8},{6,10},{8,4},{10,6},{12,28},{14,30},{1,5},{3,7... | collective-permute-start | bytes 811016 | tf_op jit(solution)/shard_map/ppermute | solution.py:405
  14.4 0.5 %collective-permute-start.6 = (bf16[2,256,256]{2,1,0:T(8,128)(2,1)S(1)}, bf16[2,256,256]{2,1,0:T(8,128)(2,1)S(1)}, u32[]{:S(2)}, u32[]{:S(2)}) collective-permute-start(bf16[2,256,256]{2,1,0:T(8,128)(2,1)S(1)} %get-tuple-element.20), channel_id=1, source_target_pairs={{0,1},{1,0},{2,3},{3,2},{4,5},{5,4},{6,7},{7,6},{8,9},{9,8},{10,11... | collective-permute-start | bytes 786440 | tf_op jit(solution)/shard_map/ppermute | solution.py:55
  15.0 1.6 %collective-permute-start.7 = (bf16[192,128]{1,0:T(8,128)(2,1)S(1)}, bf16[192,128]{1,0:T(8,128)(2,1)S(1)}, u32[]{:S(2)}, u32[]{:S(2)}) collective-permute-start(bf16[192,128]{1,0:T(8,128)(2,1)S(1)} %cut.2), channel_id=1, source_target_pairs={{0,2},{2,0},{4,6},{6,4},{8,10},{10,8},{12,14},{14,12},{1,3},{3,1},... | collective-permute-start | bytes 147464 | tf_op jit(solution)/shard_map/ppermute | solution.py:405
  16.5 2.2 %near_part.1.acc = f32[256,256]{1,0:T(8,128)S(1)} custom-call(s32[5,8]{1,0:T(8,128)S(4)} %get-tuple-element.15.meta, bf16[8,4,256,256]{3,2,1,0:T(8,128)(2,1)S(1)} %get-tuple-element.16.tiles, bf16[1152,128]{1,0:T(8,128)(2,1)S(1)} %own_planes.1.refs_3_.refs_0_, bf16[1152,128]{1,0:T(8,128)(2,1)S(1)} %collective-permute-done.refs_1_.refs_0_, ...), custom_call_target="tpu_custom_call" | custom-call | tf_op jit(solution)/shard_map/near_part/pallas_call | solution.py:241
  18.7 1.5 %swapped_part.1 = (bf16[8,256,256]{2,1,0:T(8,128)(2,1)S(1)}, f32[256,256]{1,0:T(8,128)S(1)}) custom-call(s32[5,8]{1,0:T(8,128)S(4)} %get-tuple-element.15.meta, bf16[8,4,256,256]{3,2,1,0:T(8,128)(2,1)S(1)} %get-tuple-element.16.tiles, f32[256,256]{1,0:T(8,128)S(1)} %near_part.1.acc, bf16[1152,128]{1,0:T(8,128)(2,1)S(1)} %own_planes.1.refs_3_.refs_0_, ...), custom_call_target="tpu_custom_call" | custom-call | tf_op jit(solution)/shard_map/swapped_part/pallas_call | solution.py:176
  20.2 0.0 copy-start
  20.2 0.0 copy-start.1
  20.2 0.0 copy-start.2
  20.3 0.6 %relayed_part.1 = (f32[256,128]{1,0:T(8,128)S(1)}, f32[256,128]{1,0:T(8,128)S(1)}) custom-call(s32[5,8]{1,0:T(8,128)S(4)} %get-tuple-element.15.meta, bf16[8,4,256,256]{3,2,1,0:T(8,128)(2,1)S(1)} %get-tuple-element.16.tiles, bf16[8,256,256]{2,1,0:T(8,128)(2,1)S(1)} %get-tuple-element.21.extra, f32[256,256]{1,0:T(8,128)S(1)} %get-tuple-element.22.acc, ...), custom_call_target="tpu_custom_call" | custom-call | tf_op jit(solution)/shard_map/relayed_part/pallas_call | solution.py:316
  20.9 0.1 collective-permute-start.10
  21.0 1.3 %collective-permute-done.10.other = f32[256,128]{1,0:T(8,128)S(1)} collective-permute-done((f32[256,128]{1,0:T(8,128)S(1)}, f32[256,128]{1,0:T(8,128)S(1)}, u32[]{:S(2)}, u32[]{:S(2)}) %collective-permute-start.10) | collective-permute-done | bytes 131104 | tf_op jit(solution)/shard_map/ppermute | solution.py:55
  22.3 0.2 first_currents.1.source.first
  22.5 1.1 %collective-permute-start.13 = (bf16[256,128]{1,0:T(8,128)(2,1)S(1)}, bf16[256,128]{1,0:T(8,128)(2,1)S(1)}, u32[]{:S(2)}, u32[]{:S(2)}) collective-permute-start(bf16[256,128]{1,0:T(8,128)(2,1)S(1)} %first_currents.1.source.first), channel_id=1, source_target_pairs={{0,16},{2,18},{4,8},{6,10},{8,4},{10,6},{12,28},{14,30},{1,7},{3,5... | collective-permute-start | bytes 196616 | tf_op jit(solution)/shard_map/ppermute | solution.py:405
  23.7 1.5 %collective-permute-start.12 = (bf16[256,128]{1,0:T(8,128)(2,1)S(1)}, bf16[256,128]{1,0:T(8,128)(2,1)S(1)}, u32[]{:S(2)}, u32[]{:S(2)}) collective-permute-start(bf16[256,128]{1,0:T(8,128)(2,1)S(1)} %first_currents.1.source.first), channel_id=1, source_target_pairs={{0,2},{2,0},{4,6},{6,4},{8,10},{10,8},{12,14},{14,12},{1,17},{3,19... | collective-permute-start | bytes 196616 | tf_op jit(solution)/shard_map/ppermute | solution.py:405
  25.2 1.6 %collective-permute-start.11 = (bf16[256,128]{1,0:T(8,128)(2,1)S(1)}, bf16[256,128]{1,0:T(8,128)(2,1)S(1)}, u32[]{:S(2)}, u32[]{:S(2)}) collective-permute-start(bf16[256,128]{1,0:T(8,128)(2,1)S(1)} %first_currents.1.source.first), channel_id=1, source_target_pairs={{0,4},{2,6},{4,0},{6,2},{8,12},{10,14},{12,8},{14,10},{1,17},{3,19... | collective-permute-start | bytes 196616 | tf_op jit(solution)/shard_map/ppermute | solution.py:405
  26.7 0.1 collective-permute-done.13.source
  26.9 1.1 %collective-permute-done.12.source = bf16[256,128]{1,0:T(8,128)(2,1)S(1)} collective-permute-done((bf16[256,128]{1,0:T(8,128)(2,1)S(1)}, bf16[256,128]{1,0:T(8,128)(2,1)S(1)}, u32[]{:S(2)}, u32[]{:S(2)}) %collective-permute-start.12) | collective-permute-done | bytes 65568 | tf_op jit(solution)/shard_map/ppermute | solution.py:405
  27.9 0.5 %fresh_part.6.acc = f32[256,128]{1,0:T(8,128)S(1)} custom-call(s32[5,8]{1,0:T(8,128)S(4)} %get-tuple-element.15.meta, bf16[8,4,256,256]{3,2,1,0:T(8,128)(2,1)S(1)} %get-tuple-element.16.tiles, bf16[8,256,256]{2,1,0:T(8,128)(2,1)S(1)} %get-tuple-element.21.extra, bf16[256,128]{1,0:T(8,128)(2,1)S(1)} %collective-permute-done.12.source, ...), custom_call_target="tpu_custom_call", output_to_operand_aliasing={{}: (4, {})} | custom-call | tf_op jit(solution)/shard_map/fresh_part/pallas_call | solution.py:372
  28.4 1.0 %collective-permute-done.11.source = bf16[256,128]{1,0:T(8,128)(2,1)S(1)} collective-permute-done((bf16[256,128]{1,0:T(8,128)(2,1)S(1)}, bf16[256,128]{1,0:T(8,128)(2,1)S(1)}, u32[]{:S(2)}, u32[]{:S(2)}) %collective-permute-start.11) | collective-permute-done | bytes 65568 | tf_op jit(solution)/shard_map/ppermute | solution.py:405
  29.4 0.2 fresh_part.7.mine
  29.7 0.1 collective-permute-start.14
  29.7 1.3 %collective-permute-done.14.other = f32[256,128]{1,0:T(8,128)S(1)} collective-permute-done((f32[256,128]{1,0:T(8,128)S(1)}, f32[256,128]{1,0:T(8,128)S(1)}, u32[]{:S(2)}, u32[]{:S(2)}) %collective-permute-start.14) | collective-permute-done | bytes 131104 | tf_op jit(solution)/shard_map/ppermute | solution.py:55
  31.1 0.8 %second_currents.1 = bf16[2,256,128]{2,1,0:T(8,128)(2,1)} custom-call(s32[5,8]{1,0:T(8,128)S(4)} %get-tuple-element.15.meta, bf16[256,128]{1,0:T(8,128)(2,1)S(1)} %first_currents.1.source.first, f32[256,128]{1,0:T(8,128)S(1)} %fresh_part.7.mine, f32[256,128]{1,0:T(8,128)S(1)} %collective-permute-done.14.other, bf16[256,256]{1,0:T(8,128)(2,1)S(1)} %bitcast.6, ...), custom_call_target="tpu_custom_call" | custom-call | tf_op jit(solution)/shard_map/second_currents/pallas_call | solution.py:480
  (17 shorter events, 0.1 us)
Async XLA Ops:
  1.0 10.0 %collective-permute-start = (bf16[1152,128]{1,0:T(8,128)(2,1)S(1)}, bf16[1152,128]{1,0:T(8,128)(2,1)S(1)}, u32[]{:S(2)}, u32[]{:S(2)}) collective-permute-start(bf16[1152,128]{1,0:T(8,128)(2,1)S(1)} %own_planes.1.refs_3_.refs_0_), channel_id=1, source_target_pairs={{0,2},{2,0},{4,6},{6,4},{8,10},{10,8},{12,14},{14,12},{1,3},{3,1},... | collective-permute-start | bytes 884744 | tf_op jit(solution)/shard_map/ppermute | solution.py:405
  4.0 10.4 %collective-permute-start.1 = (bf16[1152,128]{1,0:T(8,128)(2,1)S(1)}, bf16[1152,128]{1,0:T(8,128)(2,1)S(1)}, u32[]{:S(2)}, u32[]{:S(2)}) collective-permute-start(bf16[1152,128]{1,0:T(8,128)(2,1)S(1)} %own_planes.1.refs_3_.refs_0_), channel_id=1, source_target_pairs={{0,4},{2,6},{4,0},{6,2},{8,12},{10,14},{12,8},{14,10},{1,17},{3,19... | collective-permute-start | bytes 884744 | tf_op jit(solution)/shard_map/ppermute | solution.py:405
  5.6 8.9 %collective-permute-start.2 = (bf16[1152,128]{1,0:T(8,128)(2,1)S(1)}, bf16[1152,128]{1,0:T(8,128)(2,1)S(1)}, u32[]{:S(2)}, u32[]{:S(2)}) collective-permute-start(bf16[1152,128]{1,0:T(8,128)(2,1)S(1)} %own_planes.1.refs_3_.refs_0_), channel_id=1, source_target_pairs={{0,16},{2,18},{4,8},{6,10},{8,4},{10,6},{12,28},{14,30},{1,5},{3,7... | collective-permute-start | bytes 884744 | tf_op jit(solution)/shard_map/ppermute | solution.py:405
  9.8 3.1 %collective-permute-start.3 = (bf16[2,256,256]{2,1,0:T(8,128)(2,1)S(1)}, bf16[2,256,256]{2,1,0:T(8,128)(2,1)S(1)}, u32[]{:S(2)}, u32[]{:S(2)}) collective-permute-start(bf16[2,256,256]{2,1,0:T(8,128)(2,1)S(1)} %get-tuple-element.17), channel_id=1, source_target_pairs={{0,1},{1,0},{2,3},{3,2},{4,5},{5,4},{6,7},{7,6},{8,9},{9,8},{10,11... | collective-permute-start | bytes 786440 | tf_op jit(solution)/shard_map/ppermute | solution.py:55
  9.8 5.1 %collective-permute-start.4 = (bf16[2,256,256]{2,1,0:T(8,128)(2,1)S(1)}, bf16[2,256,256]{2,1,0:T(8,128)(2,1)S(1)}, u32[]{:S(2)}, u32[]{:S(2)}) collective-permute-start(bf16[2,256,256]{2,1,0:T(8,128)(2,1)S(1)} %get-tuple-element.18), channel_id=1, source_target_pairs={{0,1},{1,0},{2,3},{3,2},{4,5},{5,4},{6,7},{7,6},{8,9},{9,8},{10,11... | collective-permute-start | bytes 786440 | tf_op jit(solution)/shard_map/ppermute | solution.py:55
  11.0 9.2 %collective-permute-start.8 = (bf16[1056,128]{1,0:T(8,128)(2,1)S(1)}, bf16[1056,128]{1,0:T(8,128)(2,1)S(1)}, u32[]{:S(2)}, u32[]{:S(2)}) collective-permute-start(bf16[1056,128]{1,0:T(8,128)(2,1)S(1)} %cut.3), channel_id=1, source_target_pairs={{0,4},{2,6},{4,0},{6,2},{8,12},{10,14},{12,8},{14,10},{1,17},{3,19... | collective-permute-start | bytes 811016 | tf_op jit(solution)/shard_map/ppermute | solution.py:405
  12.9 7.4 %collective-permute-start.9 = (bf16[1056,128]{1,0:T(8,128)(2,1)S(1)}, bf16[1056,128]{1,0:T(8,128)(2,1)S(1)}, u32[]{:S(2)}, u32[]{:S(2)}) collective-permute-start(bf16[1056,128]{1,0:T(8,128)(2,1)S(1)} %cut.3), channel_id=1, source_target_pairs={{0,16},{2,18},{4,8},{6,10},{8,4},{10,6},{12,28},{14,30},{1,5},{3,7... | collective-permute-start | bytes 811016 | tf_op jit(solution)/shard_map/ppermute | solution.py:405
  14.4 4.2 %collective-permute-start.5 = (bf16[2,256,256]{2,1,0:T(8,128)(2,1)S(1)}, bf16[2,256,256]{2,1,0:T(8,128)(2,1)S(1)}, u32[]{:S(2)}, u32[]{:S(2)}) collective-permute-start(bf16[2,256,256]{2,1,0:T(8,128)(2,1)S(1)} %get-tuple-element.19), channel_id=1, source_target_pairs={{0,1},{1,0},{2,3},{3,2},{4,5},{5,4},{6,7},{7,6},{8,9},{9,8},{10,11... | collective-permute-start | bytes 786440 | tf_op jit(solution)/shard_map/ppermute | solution.py:55
  14.4 4.2 %collective-permute-start.6 = (bf16[2,256,256]{2,1,0:T(8,128)(2,1)S(1)}, bf16[2,256,256]{2,1,0:T(8,128)(2,1)S(1)}, u32[]{:S(2)}, u32[]{:S(2)}) collective-permute-start(bf16[2,256,256]{2,1,0:T(8,128)(2,1)S(1)} %get-tuple-element.20), channel_id=1, source_target_pairs={{0,1},{1,0},{2,3},{3,2},{4,5},{5,4},{6,7},{7,6},{8,9},{9,8},{10,11... | collective-permute-start | bytes 786440 | tf_op jit(solution)/shard_map/ppermute | solution.py:55
  15.0 5.3 %collective-permute-start.7 = (bf16[192,128]{1,0:T(8,128)(2,1)S(1)}, bf16[192,128]{1,0:T(8,128)(2,1)S(1)}, u32[]{:S(2)}, u32[]{:S(2)}) collective-permute-start(bf16[192,128]{1,0:T(8,128)(2,1)S(1)} %cut.2), channel_id=1, source_target_pairs={{0,2},{2,0},{4,6},{6,4},{8,10},{10,8},{12,14},{14,12},{1,3},{3,1},... | collective-permute-start | bytes 147464 | tf_op jit(solution)/shard_map/ppermute | solution.py:405
  20.2 2.1 %copy-start = (bf16[1,256,256]{2,1,0:T(8,128)(2,1)S(1)}, bf16[1,256,256]{2,1,0:T(8,128)(2,1)}, u32[]{:S(2)}) copy-start(bf16[1,256,256]{2,1,0:T(8,128)(2,1)} %param.9) | copy-start | bytes 393220
  20.2 2.1 %copy-start.1 = (f32[2,128]{1,0:T(2,128)S(1)}, f32[2,128]{1,0:T(2,128)}, u32[]{:S(2)}) copy-start(f32[2,128]{1,0:T(2,128)} %wave.3) | copy-start | bytes 3076
  20.2 2.1 %copy-start.2 = (s32[128]{0:T(128)S(1)}, s32[128]{0:T(128)}, u32[]{:S(2)}) copy-start(s32[128]{0:T(128)} %param.12) | copy-start | bytes 1540
  20.9 1.4 %collective-permute-start.10 = (f32[256,128]{1,0:T(8,128)S(1)}, f32[256,128]{1,0:T(8,128)S(1)}, u32[]{:S(2)}, u32[]{:S(2)}) collective-permute-start(f32[256,128]{1,0:T(8,128)S(1)} %get-tuple-element.23.mine), channel_id=1, source_target_pairs={{0,1},{1,0},{2,3},{3,2},{4,5},{5,4},{6,7},{7,6},{8,9},{9,8},{10,11... | collective-permute-start | bytes 393224 | tf_op jit(solution)/shard_map/ppermute | solution.py:55
  22.5 4.3 %collective-permute-start.13 = (bf16[256,128]{1,0:T(8,128)(2,1)S(1)}, bf16[256,128]{1,0:T(8,128)(2,1)S(1)}, u32[]{:S(2)}, u32[]{:S(2)}) collective-permute-start(bf16[256,128]{1,0:T(8,128)(2,1)S(1)} %first_currents.1.source.first), channel_id=1, source_target_pairs={{0,16},{2,18},{4,8},{6,10},{8,4},{10,6},{12,28},{14,30},{1,7},{3,5... | collective-permute-start | bytes 196616 | tf_op jit(solution)/shard_map/ppermute | solution.py:405
  23.7 4.3 %collective-permute-start.12 = (bf16[256,128]{1,0:T(8,128)(2,1)S(1)}, bf16[256,128]{1,0:T(8,128)(2,1)S(1)}, u32[]{:S(2)}, u32[]{:S(2)}) collective-permute-start(bf16[256,128]{1,0:T(8,128)(2,1)S(1)} %first_currents.1.source.first), channel_id=1, source_target_pairs={{0,2},{2,0},{4,6},{6,4},{8,10},{10,8},{12,14},{14,12},{1,17},{3,19... | collective-permute-start | bytes 196616 | tf_op jit(solution)/shard_map/ppermute | solution.py:405
  25.2 4.3 %collective-permute-start.11 = (bf16[256,128]{1,0:T(8,128)(2,1)S(1)}, bf16[256,128]{1,0:T(8,128)(2,1)S(1)}, u32[]{:S(2)}, u32[]{:S(2)}) collective-permute-start(bf16[256,128]{1,0:T(8,128)(2,1)S(1)} %first_currents.1.source.first), channel_id=1, source_target_pairs={{0,4},{2,6},{4,0},{6,2},{8,12},{10,14},{12,8},{14,10},{1,17},{3,19... | collective-permute-start | bytes 196616 | tf_op jit(solution)/shard_map/ppermute | solution.py:405
  29.7 1.4 %collective-permute-start.14 = (f32[256,128]{1,0:T(8,128)S(1)}, f32[256,128]{1,0:T(8,128)S(1)}, u32[]{:S(2)}, u32[]{:S(2)}) collective-permute-start(f32[256,128]{1,0:T(8,128)S(1)} %fresh_part.7.mine), channel_id=1, source_target_pairs={{0,1},{1,0},{2,3},{3,2},{4,5},{5,4},{6,7},{7,6},{8,9},{9,8},{10,11... | collective-permute-start | bytes 393224 | tf_op jit(solution)/shard_map/ppermute | solution.py:55

commit v11 on v10

--- a/solution.py
+++ b/solution.py
@@ -249,7 +249,7 @@
 
 
 def relayed_kernel(first, turns, meta, tiles, extra, acc, *refs):
-    sources, (out0, out1, total, store) = refs[: 3 * turns], refs[3 * turns :]
+    sources, (out0, out1, store) = refs[: 3 * turns], refs[3 * turns :]
     pairs, taps, rows = tiles.shape[:3]
     half, width = rows // 2, acc.shape[1] // 2
     held_rows = taps * rows
@@ -267,7 +267,8 @@
             store[base + held_rows + half : base + block - half] = rest[held_rows - HEAD :]
             store[base + block - half : base + block] = empty
     store[none:] = jnp.zeros((rows, width), store.dtype)
-    total[...] = acc[...]
+    out0[...] = acc[:, :width]
+    out1[...] = acc[:, width:]
 
     def pair(a, b):
         return jnp.concatenate(
@@ -295,16 +296,16 @@
             a = jnp.where(core == 0, base + held_rows + half, base)
             b = jnp.where(jnp.logical_and(early, core == 0), ats[taps - 1], none)
             rights.append(pair(jnp.where(after, a, none), b))
-        total[...] += jnp.dot(
+        sums = jnp.dot(
             jnp.concatenate(lefts, axis=1),
             jnp.concatenate(rights, axis=0),
             preferred_element_type=jnp.float32,
         )
+        out0[...] += sums[:, :width]
+        out1[...] += sums[:, width:]
 
     for start in range(0, pairs, CHUNK):
         pl.when(meta[PLACE, 2] > start)(functools.partial(chunk, start))
-    out0[...] = total[:, :width]
-    out1[...] = total[:, width:]
 
 
 def relayed_part(meta, tiles, extra, acc, sources, first):
@@ -318,10 +319,7 @@
         out_shape=[half, half],
         in_specs=[SMEM] + [VMEM] * (3 + len(sources)),
         out_specs=[VMEM, VMEM],
-        scratch_shapes=[
-            pltpu.VMEM(acc.shape, acc.dtype),
-            pltpu.VMEM(store, sources[0].dtype),
-        ],
+        scratch_shapes=[pltpu.VMEM(store, sources[0].dtype)],
         compiler_params=pltpu.CompilerParams(vmem_limit_bytes=room + (4 << 20)),
         name="relayed_part",
     )(

time: 32 us -> 31.9 us (level)
  waiting for transfers between devices: 5.56 us -> 6.8 us
  Pallas kernels: 9.7 us -> 8.94 us
    ppermute x9, waiting for transfers between devices: 2.88 us -> 4.1 us  [send(): return lax.ppermute(x, ALL_AXES, pairs)]
    pallas_call x4, Pallas kernels: 0.7 us -> 0.01 us  [fresh_part(): pl.pallas_call(functools.partial(fresh_kernel, number), out_shape=pltpu.V...]
    pallas_call x1, Pallas kernels: 0.64 us -> 1.14 us  [relayed_part(): pl.pallas_call(functools.partial(relayed_kernel, first, turns), out_shape...]
  transfers between devices with their start and end apart: 15 -> 15, of which waited for: 6 -> 7; matrix products, arithmetic and copies ran while one was open for 0% -> 0% of each run, Pallas kernels for 21% -> 18%
where the time goes in v11:
time: 31.9 us; the launch traced here: 32.1 us
  starting transfers between devices  16.2 us (51%)
  Pallas kernels  8.94 us (28%)
  waiting for transfers between devices  6.8 us (21%)
    ppermute x9, starting transfers between devices, send(): return lax.ppermute(x, ALL_AXES, pairs)  15.1 us
    ppermute x9, waiting for transfers between devices, send(): return lax.ppermute(x, ALL_AXES, pairs)  4.1 us
    pallas_call x1, Pallas kernels, per_device(): pl.pallas_call(functools.partial(table_kernel, slots, news, sites, groups...  2.69 us
    ppermute x6, waiting for transfers between devices, swap_cores(): return lax.ppermute(x, 'sub', [(0, 1), (1, 0)])  2.69 us
    pallas_call x1, Pallas kernels, near_part(): pl.pallas_call(functools.partial(near_kernel, len(sources)), out_shape=pl...  1.85 us
    pallas_call x1, Pallas kernels, swapped_part(): pl.pallas_call(functools.partial(swapped_kernel, len(sources)), out_shape...  1.22 us
    ppermute x6, starting transfers between devices, swap_cores(): return lax.ppermute(x, 'sub', [(0, 1), (1, 0)])  1.15 us
    pallas_call x1, Pallas kernels, relayed_part(): pl.pallas_call(functools.partial(relayed_kernel, first, turns), out_shape...  1.14 us
  transfers between devices with their start and end apart: 15, of which 7 were waited for; matrix products, arithmetic and copies ran while one was open for 0% of the time, Pallas kernels for 18%

profile of v11, /device:TPU:0, one launch (start us, length us, event | category | flops | bytes accessed | tf_op | source)
XLA Modules:
  0.0 32.1 jit_solution(196519179972847198)
XLA Ops:
  0.0 1.0 %own_planes.1.refs_3_.refs_0_ = bf16[1152,128]{1,0:T(8,128)(2,1)S(1)} custom-call(bf16[9,256,128]{2,1,0:T(8,128)(2,1)} %bitcast.10), custom_call_target="tpu_custom_call" | custom-call | tf_op jit(solution)/shard_map/own_planes/pallas_call | solution.py:425
  1.0 3.0 %collective-permute-start = (bf16[1152,128]{1,0:T(8,128)(2,1)S(1)}, bf16[1152,128]{1,0:T(8,128)(2,1)S(1)}, u32[]{:S(2)}, u32[]{:S(2)}) collective-permute-start(bf16[1152,128]{1,0:T(8,128)(2,1)S(1)} %own_planes.1.refs_3_.refs_0_), channel_id=1, source_target_pairs={{0,2},{2,0},{4,6},{6,4},{8,10},{10,8},{12,14},{14,12},{1,3},{3,1},... | collective-permute-start | bytes 884744 | tf_op jit(solution)/shard_map/ppermute | solution.py:403
  4.0 1.6 %collective-permute-start.1 = (bf16[1152,128]{1,0:T(8,128)(2,1)S(1)}, bf16[1152,128]{1,0:T(8,128)(2,1)S(1)}, u32[]{:S(2)}, u32[]{:S(2)}) collective-permute-start(bf16[1152,128]{1,0:T(8,128)(2,1)S(1)} %own_planes.1.refs_3_.refs_0_), channel_id=1, source_target_pairs={{0,4},{2,6},{4,0},{6,2},{8,12},{10,14},{12,8},{14,10},{1,17},{3,19... | collective-permute-start | bytes 884744 | tf_op jit(solution)/shard_map/ppermute | solution.py:403
  5.6 1.5 %collective-permute-start.2 = (bf16[1152,128]{1,0:T(8,128)(2,1)S(1)}, bf16[1152,128]{1,0:T(8,128)(2,1)S(1)}, u32[]{:S(2)}, u32[]{:S(2)}) collective-permute-start(bf16[1152,128]{1,0:T(8,128)(2,1)S(1)} %own_planes.1.refs_3_.refs_0_), channel_id=1, source_target_pairs={{0,16},{2,18},{4,8},{6,10},{8,4},{10,6},{12,28},{14,30},{1,5},{3,7... | collective-permute-start | bytes 884744 | tf_op jit(solution)/shard_map/ppermute | solution.py:403
  7.1 2.7 %table.1 = (bf16[2,256,256]{2,1,0:T(8,128)(2,1)S(1)}, bf16[2,256,256]{2,1,0:T(8,128)(2,1)S(1)}, bf16[2,256,256]{2,1,0:T(8,128)(2,1)S(1)}, bf16[2,256,256]{2,1,0:...) custom-call(s32[1,8]{1,0:T(1,128)} %refs_0_.1, s32[1,8]{1,0:T(1,128)} %refs_1_.1, ...), custom_call_target="tpu_custom_call" | custom-call | tf_op jit(solution)/shard_map/table/pallas_call | solution.py:434
  9.8 0.1 collective-permute-start.3
  9.9 0.5 %collective-permute-start.4 = (bf16[2,256,256]{2,1,0:T(8,128)(2,1)S(1)}, bf16[2,256,256]{2,1,0:T(8,128)(2,1)S(1)}, u32[]{:S(2)}, u32[]{:S(2)}) collective-permute-start(bf16[2,256,256]{2,1,0:T(8,128)(2,1)S(1)} %get-tuple-element.18), channel_id=1, source_target_pairs={{0,1},{1,0},{2,3},{3,2},{4,5},{5,4},{6,7},{7,6},{8,9},{9,8},{10,11... | collective-permute-start | bytes 786440 | tf_op jit(solution)/shard_map/ppermute | solution.py:55
  10.4 0.6 %collective-permute-done.refs_1_.refs_0_ = bf16[1152,128]{1,0:T(8,128)(2,1)S(1)} collective-permute-done((bf16[1152,128]{1,0:T(8,128)(2,1)S(1)}, bf16[1152,128]{1,0:T(8,128)(2,1)S(1)}, u32[]{:S(2)}, u32[]{:S(2)}) %collective-permute-start) | collective-permute-done | bytes 294944 | tf_op jit(solution)/shard_map/ppermute | solution.py:403
  11.0 1.9 %collective-permute-start.8 = (bf16[1056,128]{1,0:T(8,128)(2,1)S(1)}, bf16[1056,128]{1,0:T(8,128)(2,1)S(1)}, u32[]{:S(2)}, u32[]{:S(2)}) collective-permute-start(bf16[1056,128]{1,0:T(8,128)(2,1)S(1)} %cut.3), channel_id=1, source_target_pairs={{0,4},{2,6},{4,0},{6,2},{8,12},{10,14},{12,8},{14,10},{1,17},{3,19... | collective-permute-start | bytes 811016 | tf_op jit(solution)/shard_map/ppermute | solution.py:403
  12.9 0.0 collective-permute-done.3.refs_4_
  12.9 1.5 %collective-permute-start.9 = (bf16[1056,128]{1,0:T(8,128)(2,1)S(1)}, bf16[1056,128]{1,0:T(8,128)(2,1)S(1)}, u32[]{:S(2)}, u32[]{:S(2)}) collective-permute-start(bf16[1056,128]{1,0:T(8,128)(2,1)S(1)} %cut.3), channel_id=1, source_target_pairs={{0,16},{2,18},{4,8},{6,10},{8,4},{10,6},{12,28},{14,30},{1,5},{3,7... | collective-permute-start | bytes 811016 | tf_op jit(solution)/shard_map/ppermute | solution.py:403
  14.4 0.0 collective-permute-done.1.refs_2_.refs_0_
  14.4 0.5 %collective-permute-start.6 = (bf16[2,256,256]{2,1,0:T(8,128)(2,1)S(1)}, bf16[2,256,256]{2,1,0:T(8,128)(2,1)S(1)}, u32[]{:S(2)}, u32[]{:S(2)}) collective-permute-start(bf16[2,256,256]{2,1,0:T(8,128)(2,1)S(1)} %get-tuple-element.20), channel_id=1, source_target_pairs={{0,1},{1,0},{2,3},{3,2},{4,5},{5,4},{6,7},{7,6},{8,9},{9,8},{10,11... | collective-permute-start | bytes 786440 | tf_op jit(solution)/shard_map/ppermute | solution.py:55
  15.0 1.6 %collective-permute-start.7 = (bf16[192,128]{1,0:T(8,128)(2,1)S(1)}, bf16[192,128]{1,0:T(8,128)(2,1)S(1)}, u32[]{:S(2)}, u32[]{:S(2)}) collective-permute-start(bf16[192,128]{1,0:T(8,128)(2,1)S(1)} %cut.2), channel_id=1, source_target_pairs={{0,2},{2,0},{4,6},{6,4},{8,10},{10,8},{12,14},{14,12},{1,3},{3,1},... | collective-permute-start | bytes 147464 | tf_op jit(solution)/shard_map/ppermute | solution.py:403
  16.5 1.8 %near_part.1.acc = f32[256,256]{1,0:T(8,128)S(1)} custom-call(s32[5,8]{1,0:T(8,128)S(4)} %get-tuple-element.15.meta, bf16[8,4,256,256]{3,2,1,0:T(8,128)(2,1)S(1)} %get-tuple-element.16.tiles, bf16[1152,128]{1,0:T(8,128)(2,1)S(1)} %own_planes.1.refs_3_.refs_0_, bf16[1152,128]{1,0:T(8,128)(2,1)S(1)} %collective-permute-done.refs_1_.refs_0_, ...), custom_call_target="tpu_custom_call" | custom-call | tf_op jit(solution)/shard_map/near_part/pallas_call | solution.py:241
  18.4 1.2 %swapped_part.1 = (bf16[8,256,256]{2,1,0:T(8,128)(2,1)S(1)}, f32[256,256]{1,0:T(8,128)S(1)}) custom-call(s32[5,8]{1,0:T(8,128)S(4)} %get-tuple-element.15.meta, bf16[8,4,256,256]{3,2,1,0:T(8,128)(2,1)S(1)} %get-tuple-element.16.tiles, f32[256,256]{1,0:T(8,128)S(1)} %near_part.1.acc, bf16[1152,128]{1,0:T(8,128)(2,1)S(1)} %own_planes.1.refs_3_.refs_0_, ...), custom_call_target="tpu_custom_call" | custom-call | tf_op jit(solution)/shard_map/swapped_part/pallas_call | solution.py:176
  19.6 0.0 copy-start
  19.6 0.0 copy-start.1
  19.6 0.0 copy-start.2
  19.7 0.3 collective-permute-done.8.refs_1_
  19.9 1.1 %relayed_part.1 = (f32[256,128]{1,0:T(8,128)S(1)}, f32[256,128]{1,0:T(8,128)S(1)}) custom-call(s32[5,8]{1,0:T(8,128)S(4)} %get-tuple-element.15.meta, bf16[8,4,256,256]{3,2,1,0:T(8,128)(2,1)S(1)} %get-tuple-element.16.tiles, bf16[8,256,256]{2,1,0:T(8,128)(2,1)S(1)} %get-tuple-element.21.extra, f32[256,256]{1,0:T(8,128)S(1)} %get-tuple-element.22.acc, ...), custom_call_target="tpu_custom_call" | custom-call | tf_op jit(solution)/shard_map/relayed_part/pallas_call | solution.py:317
  21.1 0.1 collective-permute-start.10
  21.2 1.3 %collective-permute-done.10.other = f32[256,128]{1,0:T(8,128)S(1)} collective-permute-done((f32[256,128]{1,0:T(8,128)S(1)}, f32[256,128]{1,0:T(8,128)S(1)}, u32[]{:S(2)}, u32[]{:S(2)}) %collective-permute-start.10) | collective-permute-done | bytes 131104 | tf_op jit(solution)/shard_map/ppermute | solution.py:55
  22.5 0.2 first_currents.1.source.first
  22.7 1.5 %collective-permute-start.13 = (bf16[256,128]{1,0:T(8,128)(2,1)S(1)}, bf16[256,128]{1,0:T(8,128)(2,1)S(1)}, u32[]{:S(2)}, u32[]{:S(2)}) collective-permute-start(bf16[256,128]{1,0:T(8,128)(2,1)S(1)} %first_currents.1.source.first), channel_id=1, source_target_pairs={{0,16},{2,18},{4,8},{6,10},{8,4},{10,6},{12,28},{14,30},{1,7},{3,5... | collective-permute-start | bytes 196616 | tf_op jit(solution)/shard_map/ppermute | solution.py:403
  24.2 1.5 %collective-permute-start.12 = (bf16[256,128]{1,0:T(8,128)(2,1)S(1)}, bf16[256,128]{1,0:T(8,128)(2,1)S(1)}, u32[]{:S(2)}, u32[]{:S(2)}) collective-permute-start(bf16[256,128]{1,0:T(8,128)(2,1)S(1)} %first_currents.1.source.first), channel_id=1, source_target_pairs={{0,2},{2,0},{4,6},{6,4},{8,10},{10,8},{12,14},{14,12},{1,17},{3,19... | collective-permute-start | bytes 196616 | tf_op jit(solution)/shard_map/ppermute | solution.py:403
  25.7 1.1 %collective-permute-start.11 = (bf16[256,128]{1,0:T(8,128)(2,1)S(1)}, bf16[256,128]{1,0:T(8,128)(2,1)S(1)}, u32[]{:S(2)}, u32[]{:S(2)}) collective-permute-start(bf16[256,128]{1,0:T(8,128)(2,1)S(1)} %first_currents.1.source.first), channel_id=1, source_target_pairs={{0,4},{2,6},{4,0},{6,2},{8,12},{10,14},{12,8},{14,10},{1,17},{3,19... | collective-permute-start | bytes 196616 | tf_op jit(solution)/shard_map/ppermute | solution.py:403
  26.7 0.3 collective-permute-done.13.source
  27.0 1.4 %collective-permute-done.12.source = bf16[256,128]{1,0:T(8,128)(2,1)S(1)} collective-permute-done((bf16[256,128]{1,0:T(8,128)(2,1)S(1)}, bf16[256,128]{1,0:T(8,128)(2,1)S(1)}, u32[]{:S(2)}, u32[]{:S(2)}) %collective-permute-start.12) | collective-permute-done | bytes 65568 | tf_op jit(solution)/shard_map/ppermute | solution.py:403
  28.4 1.5 %collective-permute-done.11.source = bf16[256,128]{1,0:T(8,128)(2,1)S(1)} collective-permute-done((bf16[256,128]{1,0:T(8,128)(2,1)S(1)}, bf16[256,128]{1,0:T(8,128)(2,1)S(1)}, u32[]{:S(2)}, u32[]{:S(2)}) %collective-permute-start.11) | collective-permute-done | bytes 65568 | tf_op jit(solution)/shard_map/ppermute | solution.py:403
  29.9 1.3 %collective-permute-done.14.other = f32[256,128]{1,0:T(8,128)S(1)} collective-permute-done((f32[256,128]{1,0:T(8,128)S(1)}, f32[256,128]{1,0:T(8,128)S(1)}, u32[]{:S(2)}, u32[]{:S(2)}) %collective-permute-start.14) | collective-permute-done | bytes 131104 | tf_op jit(solution)/shard_map/ppermute | solution.py:55
  31.3 0.8 %second_currents.1 = bf16[2,256,128]{2,1,0:T(8,128)(2,1)} custom-call(s32[5,8]{1,0:T(8,128)S(4)} %get-tuple-element.15.meta, bf16[256,128]{1,0:T(8,128)(2,1)S(1)} %first_currents.1.source.first, f32[256,128]{1,0:T(8,128)S(1)} %fresh_part.7.mine, f32[256,128]{1,0:T(8,128)S(1)} %collective-permute-done.14.other, bf16[256,256]{1,0:T(8,128)(2,1)S(1)} %bitcast.6, ...), custom_call_target="tpu_custom_call" | custom-call | tf_op jit(solution)/shard_map/second_currents/pallas_call | solution.py:478
  (17 shorter events, 0.1 us)
Async XLA Ops:
  1.0 10.0 %collective-permute-start = (bf16[1152,128]{1,0:T(8,128)(2,1)S(1)}, bf16[1152,128]{1,0:T(8,128)(2,1)S(1)}, u32[]{:S(2)}, u32[]{:S(2)}) collective-permute-start(bf16[1152,128]{1,0:T(8,128)(2,1)S(1)} %own_planes.1.refs_3_.refs_0_), channel_id=1, source_target_pairs={{0,2},{2,0},{4,6},{6,4},{8,10},{10,8},{12,14},{14,12},{1,3},{3,1},... | collective-permute-start | bytes 884744 | tf_op jit(solution)/shard_map/ppermute | solution.py:403
  4.0 10.4 %collective-permute-start.1 = (bf16[1152,128]{1,0:T(8,128)(2,1)S(1)}, bf16[1152,128]{1,0:T(8,128)(2,1)S(1)}, u32[]{:S(2)}, u32[]{:S(2)}) collective-permute-start(bf16[1152,128]{1,0:T(8,128)(2,1)S(1)} %own_planes.1.refs_3_.refs_0_), channel_id=1, source_target_pairs={{0,4},{2,6},{4,0},{6,2},{8,12},{10,14},{12,8},{14,10},{1,17},{3,19... | collective-permute-start | bytes 884744 | tf_op jit(solution)/shard_map/ppermute | solution.py:403
  5.6 8.9 %collective-permute-start.2 = (bf16[1152,128]{1,0:T(8,128)(2,1)S(1)}, bf16[1152,128]{1,0:T(8,128)(2,1)S(1)}, u32[]{:S(2)}, u32[]{:S(2)}) collective-permute-start(bf16[1152,128]{1,0:T(8,128)(2,1)S(1)} %own_planes.1.refs_3_.refs_0_), channel_id=1, source_target_pairs={{0,16},{2,18},{4,8},{6,10},{8,4},{10,6},{12,28},{14,30},{1,5},{3,7... | collective-permute-start | bytes 884744 | tf_op jit(solution)/shard_map/ppermute | solution.py:403
  9.8 3.1 %collective-permute-start.3 = (bf16[2,256,256]{2,1,0:T(8,128)(2,1)S(1)}, bf16[2,256,256]{2,1,0:T(8,128)(2,1)S(1)}, u32[]{:S(2)}, u32[]{:S(2)}) collective-permute-start(bf16[2,256,256]{2,1,0:T(8,128)(2,1)S(1)} %get-tuple-element.17), channel_id=1, source_target_pairs={{0,1},{1,0},{2,3},{3,2},{4,5},{5,4},{6,7},{7,6},{8,9},{9,8},{10,11... | collective-permute-start | bytes 786440 | tf_op jit(solution)/shard_map/ppermute | solution.py:55
  9.9 5.1 %collective-permute-start.4 = (bf16[2,256,256]{2,1,0:T(8,128)(2,1)S(1)}, bf16[2,256,256]{2,1,0:T(8,128)(2,1)S(1)}, u32[]{:S(2)}, u32[]{:S(2)}) collective-permute-start(bf16[2,256,256]{2,1,0:T(8,128)(2,1)S(1)} %get-tuple-element.18), channel_id=1, source_target_pairs={{0,1},{1,0},{2,3},{3,2},{4,5},{5,4},{6,7},{7,6},{8,9},{9,8},{10,11... | collective-permute-start | bytes 786440 | tf_op jit(solution)/shard_map/ppermute | solution.py:55
  11.0 8.9 %collective-permute-start.8 = (bf16[1056,128]{1,0:T(8,128)(2,1)S(1)}, bf16[1056,128]{1,0:T(8,128)(2,1)S(1)}, u32[]{:S(2)}, u32[]{:S(2)}) collective-permute-start(bf16[1056,128]{1,0:T(8,128)(2,1)S(1)} %cut.3), channel_id=1, source_target_pairs={{0,4},{2,6},{4,0},{6,2},{8,12},{10,14},{12,8},{14,10},{1,17},{3,19... | collective-permute-start | bytes 811016 | tf_op jit(solution)/shard_map/ppermute | solution.py:403
  12.9 7.0 %collective-permute-start.9 = (bf16[1056,128]{1,0:T(8,128)(2,1)S(1)}, bf16[1056,128]{1,0:T(8,128)(2,1)S(1)}, u32[]{:S(2)}, u32[]{:S(2)}) collective-permute-start(bf16[1056,128]{1,0:T(8,128)(2,1)S(1)} %cut.3), channel_id=1, source_target_pairs={{0,16},{2,18},{4,8},{6,10},{8,4},{10,6},{12,28},{14,30},{1,5},{3,7... | collective-permute-start | bytes 811016 | tf_op jit(solution)/shard_map/ppermute | solution.py:403
  14.4 3.9 %collective-permute-start.5 = (bf16[2,256,256]{2,1,0:T(8,128)(2,1)S(1)}, bf16[2,256,256]{2,1,0:T(8,128)(2,1)S(1)}, u32[]{:S(2)}, u32[]{:S(2)}) collective-permute-start(bf16[2,256,256]{2,1,0:T(8,128)(2,1)S(1)} %get-tuple-element.19), channel_id=1, source_target_pairs={{0,1},{1,0},{2,3},{3,2},{4,5},{5,4},{6,7},{7,6},{8,9},{9,8},{10,11... | collective-permute-start | bytes 786440 | tf_op jit(solution)/shard_map/ppermute | solution.py:55
  14.4 3.9 %collective-permute-start.6 = (bf16[2,256,256]{2,1,0:T(8,128)(2,1)S(1)}, bf16[2,256,256]{2,1,0:T(8,128)(2,1)S(1)}, u32[]{:S(2)}, u32[]{:S(2)}) collective-permute-start(bf16[2,256,256]{2,1,0:T(8,128)(2,1)S(1)} %get-tuple-element.20), channel_id=1, source_target_pairs={{0,1},{1,0},{2,3},{3,2},{4,5},{5,4},{6,7},{7,6},{8,9},{9,8},{10,11... | collective-permute-start | bytes 786440 | tf_op jit(solution)/shard_map/ppermute | solution.py:55
  15.0 4.7 %collective-permute-start.7 = (bf16[192,128]{1,0:T(8,128)(2,1)S(1)}, bf16[192,128]{1,0:T(8,128)(2,1)S(1)}, u32[]{:S(2)}, u32[]{:S(2)}) collective-permute-start(bf16[192,128]{1,0:T(8,128)(2,1)S(1)} %cut.2), channel_id=1, source_target_pairs={{0,2},{2,0},{4,6},{6,4},{8,10},{10,8},{12,14},{14,12},{1,3},{3,1},... | collective-permute-start | bytes 147464 | tf_op jit(solution)/shard_map/ppermute | solution.py:403
  19.6 2.9 %copy-start = (bf16[1,256,256]{2,1,0:T(8,128)(2,1)S(1)}, bf16[1,256,256]{2,1,0:T(8,128)(2,1)}, u32[]{:S(2)}) copy-start(bf16[1,256,256]{2,1,0:T(8,128)(2,1)} %param.9) | copy-start | bytes 393220
  19.6 2.9 %copy-start.1 = (f32[2,128]{1,0:T(2,128)S(1)}, f32[2,128]{1,0:T(2,128)}, u32[]{:S(2)}) copy-start(f32[2,128]{1,0:T(2,128)} %wave.3) | copy-start | bytes 3076
  19.6 2.9 %copy-start.2 = (s32[128]{0:T(128)S(1)}, s32[128]{0:T(128)}, u32[]{:S(2)}) copy-start(s32[128]{0:T(128)} %param.12) | copy-start | bytes 1540
  21.1 1.4 %collective-permute-start.10 = (f32[256,128]{1,0:T(8,128)S(1)}, f32[256,128]{1,0:T(8,128)S(1)}, u32[]{:S(2)}, u32[]{:S(2)}) collective-permute-start(f32[256,128]{1,0:T(8,128)S(1)} %get-tuple-element.23.mine), channel_id=1, source_target_pairs={{0,1},{1,0},{2,3},{3,2},{4,5},{5,4},{6,7},{7,6},{8,9},{9,8},{10,11... | collective-permute-start | bytes 393224 | tf_op jit(solution)/shard_map/ppermute | solution.py:55
  22.7 4.3 %collective-permute-start.13 = (bf16[256,128]{1,0:T(8,128)(2,1)S(1)}, bf16[256,128]{1,0:T(8,128)(2,1)S(1)}, u32[]{:S(2)}, u32[]{:S(2)}) collective-permute-start(bf16[256,128]{1,0:T(8,128)(2,1)S(1)} %first_currents.1.source.first), channel_id=1, source_target_pairs={{0,16},{2,18},{4,8},{6,10},{8,4},{10,6},{12,28},{14,30},{1,7},{3,5... | collective-permute-start | bytes 196616 | tf_op jit(solution)/shard_map/ppermute | solution.py:403
  24.2 4.3 %collective-permute-start.12 = (bf16[256,128]{1,0:T(8,128)(2,1)S(1)}, bf16[256,128]{1,0:T(8,128)(2,1)S(1)}, u32[]{:S(2)}, u32[]{:S(2)}) collective-permute-start(bf16[256,128]{1,0:T(8,128)(2,1)S(1)} %first_currents.1.source.first), channel_id=1, source_target_pairs={{0,2},{2,0},{4,6},{6,4},{8,10},{10,8},{12,14},{14,12},{1,17},{3,19... | collective-permute-start | bytes 196616 | tf_op jit(solution)/shard_map/ppermute | solution.py:403
  25.7 4.3 %collective-permute-start.11 = (bf16[256,128]{1,0:T(8,128)(2,1)S(1)}, bf16[256,128]{1,0:T(8,128)(2,1)S(1)}, u32[]{:S(2)}, u32[]{:S(2)}) collective-permute-start(bf16[256,128]{1,0:T(8,128)(2,1)S(1)} %first_currents.1.source.first), channel_id=1, source_target_pairs={{0,4},{2,6},{4,0},{6,2},{8,12},{10,14},{12,8},{14,10},{1,17},{3,19... | collective-permute-start | bytes 196616 | tf_op jit(solution)/shard_map/ppermute | solution.py:403
  29.9 1.3 %collective-permute-start.14 = (f32[256,128]{1,0:T(8,128)S(1)}, f32[256,128]{1,0:T(8,128)S(1)}, u32[]{:S(2)}, u32[]{:S(2)}) collective-permute-start(f32[256,128]{1,0:T(8,128)S(1)} %fresh_part.7.mine), channel_id=1, source_target_pairs={{0,1},{1,0},{2,3},{3,2},{4,5},{5,4},{6,7},{7,6},{8,9},{9,8},{10,11... | collective-permute-start | bytes 393224 | tf_op jit(solution)/shard_map/ppermute | solution.py:55
